TPU v7x, 32 devices: a whole 2x2x4 slice. The times are simulated.
32 devices in a mesh: grp: 1, gx: 32 (over z, y, x, core).
Axes of the slice: x: 2, y: 2, z: 4, core: 2. Of those that a mesh axis runs over, the one named last changes fastest.
Arguments:
- out_grad: bfloat16 [16384, 768], P(('grp', 'gx')), may hold values from -6 to 6
- inputs: bfloat16 [16384, 768], P(('grp', 'gx')), may hold values from -6 to 6
- preact: bfloat16 [16384, 3072], P(('grp', 'gx')), may hold values from -6 to 6
- w_out: bfloat16 [3072, 768], P('gx'), may hold values from -0.109375 to 0.109375
- w_in: bfloat16 [768, 3072], P('gx'), may hold values from -0.21875 to 0.21875
Outputs:
- input_grad: float32 [16384, 768], P(('grp', 'gx'))
- w_out_grad: float32 [3072, 768], P(('grp', 'gx'))
- w_in_grad: float32 [768, 3072], P(('grp', 'gx'))
All inputs are finite; a program needn't handle non-finite values.
Results may differ from a plain program's by a relative error of at most 0.0029.
Values may be sent and summed in bfloat16 or wider, within the bound.
No kernel may reach another device: no remote copies, remote signals or barrier semaphores. Data moves between devices by JAX's collectives and lax.ppermute only.
A program may use at most 128 MiB of HBM per device.

v0:
```python
import math

import jax
import jax.numpy as jnp
from jax import lax
from jax.sharding import PartitionSpec as P


def gelu_parts(preact):
    value = preact.astype(jnp.float32)
    coeff = math.sqrt(2.0 / math.pi)
    inner = coeff * (value + 0.044715 * value * value * value)
    tangent = jnp.tanh(inner)
    activ = 0.5 * value * (1.0 + tangent)
    gelu_slope = 0.5 * (1.0 + tangent) + 0.5 * value * (1.0 - tangent * tangent) * coeff * (
        1.0 + 3.0 * 0.044715 * value * value
    )
    return (activ.astype(jnp.bfloat16), gelu_slope)


def contract_last(left, right):
    return lax.dot_general(
        left, right, (((1,), (1,)), ((), ())), preferred_element_type=jnp.float32
    )


def contract_first(left, right):
    return lax.dot_general(
        left, right, (((0,), (0,)), ((), ())), preferred_element_type=jnp.float32
    )


def per_device(out_grad, inputs, preact, w_out, w_in):
    axis_count = lax.axis_size("gx")
    grad_scale = 1.0 / math.sqrt(out_grad.shape[0] * axis_count)
    activ, gelu_slope = gelu_parts(preact)
    act_grad = contract_last(out_grad, lax.all_gather(w_out, "gx", axis=0, tiled=True))
    pre_grad = (act_grad * gelu_slope).astype(jnp.bfloat16)
    input_grad = contract_last(pre_grad, lax.all_gather(w_in, "gx", axis=0, tiled=True))
    w_out_grad = lax.psum_scatter(
        contract_first(activ, out_grad) * grad_scale, "gx", scatter_dimension=0, tiled=True
    )
    w_in_grad = lax.psum_scatter(
        contract_first(inputs, pre_grad) * grad_scale, "gx", scatter_dimension=0, tiled=True
    )
    return (input_grad, w_out_grad, w_in_grad)


def solution(mesh):
    in_specs = (
        P(("grp", "gx"), None),
        P(("grp", "gx"), None),
        P(("grp", "gx"), None),
        P("gx", None),
        P("gx", None),
    )
    out_specs = (P(("grp", "gx"), None), P(("grp", "gx"), None), P(("grp", "gx"), None))
    return jax.shard_map(
        per_device, mesh=mesh, in_specs=in_specs, out_specs=out_specs, check_vma=False
    )
```

profile of v0, /device:TPU:1, one launch (start us, length us, event | category | flops | bytes accessed | tf_op | source)
XLA Modules:
  0.0 429.5 jit_solution(3971400910294233406)
XLA Ops:
  7.2 0.0 copy-start
  7.2 0.0 all-gather.3.cloned.1.call-start
  7.2 0.7 all-gather.3.cloned.1.call-update
  7.9 0.0 all-gather.5.cloned.1.call-start
  8.0 0.7 all-gather.5.cloned.1.call-update
  8.7 0.0 reduce-scatter.5.cloned.1.call-start
  8.7 0.0 copy-done
  8.7 9.4 %convolution_multiply_fusion = f32[3072,768]{1,0:T(8,128)} fusion(bf16[512,768]{1,0:T(8,128)(2,1)S(1)} %copy-done, bf16[512,3072]{1,0:T(8,128)(2,1)} %param.7), kind=kOutput, calls=%fused_computation.19 | convolution fusion | flops 2434007040 | bytes 13369344 | tf_op jit(solution)/shard_map/dot_general | solution.py:28
  18.1 0.0 reduce-scatter.5.cloned.1.call-update
  18.2 0.0 copy-start.1
  18.2 0.0 reduce-scatter.7.cloned.1.call-start
  18.2 58.9 %all-gather.3.cloned.1.call-done = bf16[3072,768]{1,0:T(8,128)(2,1)} async-done(((bf16[96,768]{1,0:T(8,128)(2,1)}), bf16[3072,768]{1,0:T(8,128)(2,1)}) %all-gather.3.cloned.1.call-update) | async-done | bytes 4718608 | tf_op jit(solution)/shard_map/all_gather | solution.py:37
  77.1 8.0 %fusion.6 = bf16[512,3072]{1,0:T(8,128)(2,1)S(1)} fusion(bf16[512,3072]{1,0:T(8,128)(2,1)} %param.7, bf16[512,768]{1,0:T(8,128)(2,1)S(1)} %copy-done, bf16[3072,768]{1,0:T(8,128)(2,1)} %all-gather.3.cloned.1.call-done), kind=kOutput, calls=%fused_computation.14 | convolution fusion | flops 2447376384 | bytes 11796480 | tf_op jit(solution)/shard_map/dot_general | solution.py:22
  85.1 0.0 copy-start.2
  85.1 1.6 copy-done.2
  86.7 0.0 copy-done.1
  86.7 5.2 %multiply_bitcast_fusion = f32[768,3072]{0,1:T(8,128)} fusion(bf16[512,3072]{1,0:T(8,128)(2,1)S(1)} %fusion.6, bf16[512,768]{1,0:T(8,128)(2,1)S(1)} %copy-done.1), kind=kOutput, calls=%fused_computation.7 | convolution fusion | flops 2418278400 | bytes 13369344 | tf_op jit(solution)/shard_map/dot_general | solution.py:28
  91.9 9.6 %copy.10 = f32[768,3072]{1,0:T(8,128)} copy(f32[768,3072]{0,1:T(8,128)} %multiply_bitcast_fusion) | data formatting | bytes 18874368
  101.5 0.0 reduce-scatter.7.cloned.1.call-update
  101.5 41.0 %all-gather.5.cloned.1.call-done = bf16[768,3072]{1,0:T(8,128)(2,1)} async-done(((bf16[24,3072]{1,0:T(8,128)(2,1)}), bf16[768,3072]{1,0:T(8,128)(2,1)}) %all-gather.5.cloned.1.call-update) | async-done | bytes 4718608 | tf_op jit(solution)/shard_map/all_gather | solution.py:39
  142.5 7.1 %fusion.20 = f32[512,768]{1,0:T(8,128)} fusion(bf16[512,3072]{1,0:T(8,128)(2,1)} %copy-done.2, bf16[768,3072]{1,0:T(8,128)(2,1)} %all-gather.5.cloned.1.call-done), kind=kOutput, calls=%fused_computation.28 | convolution fusion | flops 2415919104 | bytes 9437184 | tf_op jit(solution)/shard_map/dot_general | solution.py:22
  149.6 131.4 %reduce-scatter.5.cloned.1.call-done = f32[96,768]{1,0:T(8,128)} async-done(((f32[3072,768]{1,0:T(8,128)}), f32[96,768]{1,0:T(8,128)}) %reduce-scatter.5.cloned.1.call-update) | async-done | bytes 294928 | tf_op jit(solution)/shard_map/reduce_scatter | solution.py:40
  281.0 142.0 %reduce-scatter.7.cloned.1.call-done = f32[24,3072]{1,0:T(8,128)} async-done(((f32[768,3072]{1,0:T(8,128)}), f32[24,3072]{1,0:T(8,128)}) %reduce-scatter.7.cloned.1.call-update) | async-done | bytes 294928
Async XLA Ops:
  7.2 1.5 copy-start
  7.2 69.9 %all-gather.3.cloned.1.call-start = ((), (), s32[]{:S(2)}) async-start(), calls=%async_computation.2 | async-start | bytes 4866048 | tf_op jit(solution)/shard_map/all_gather | solution.py:37
  7.9 134.6 %all-gather.5.cloned.1.call-start = ((), (), s32[]{:S(2)}) async-start(), calls=%async_computation.3 | async-start | bytes 4866048 | tf_op jit(solution)/shard_map/all_gather | solution.py:39
  8.7 272.3 %reduce-scatter.5.cloned.1.call-start = ((), (), s32[]{:S(2)}) async-start(), calls=%async_computation.4 | async-start | bytes 9732096 | tf_op jit(solution)/shard_map/reduce_scatter | solution.py:40
  18.2 68.6 %copy-start.1 = (bf16[512,768]{1,0:T(8,128)(2,1)S(1)}, bf16[512,768]{1,0:T(8,128)(2,1)}, u32[]{:S(2)}) copy-start(bf16[512,768]{1,0:T(8,128)(2,1)} %param.6) | copy-start | bytes 2359300
  18.2 404.8 %reduce-scatter.7.cloned.1.call-start = ((), (), s32[]{:S(2)}) async-start(), calls=%async_computation.5 | async-start | bytes 9732096
  85.1 1.6 copy-start.2
Sparse Core Ops, SparseCore 0:
  10.9 66.1 all-gather.2
  80.0 62.4 all-gather.4
  149.0 131.9 reduce-scatter.4
  288.3 134.5 reduce-scatter.6
where the time goes:
time: 432 us; the launch traced here: 429 us
  waiting for transfers between devices  375 us (87%)
  matrix products  29.6 us (7%)
  between operations  13.8 us (3%)
  local copies, waits for them, and re-layouts  11.2 us (3%)
    unnamed x5, waiting for transfers between devices  143 us
    reduce_scatter x1, waiting for transfers between devices, per_device(): lax.psum_scatter(contract_first(activ, out_grad) * grad_scale, 'gx', scat...  131 us
    all_gather x1, waiting for transfers between devices, per_device(): lax.all_gather(w_out, 'gx', axis=0, tiled=True)  58.9 us
    all_gather x1, waiting for transfers between devices, per_device(): lax.all_gather(w_in, 'gx', axis=0, tiled=True)  41 us
    dot_general x2, matrix products, contract_last(): lax.dot_general(left, right, (((1,), (1,)), ((), ())), preferred_element_...  15.1 us
    dot_general x2, matrix products, contract_first(): lax.dot_general(left, right, (((0,), (0,)), ((), ())), preferred_element_...  14.6 us
    unnamed x7, local copies, waits for them, and re-layouts  11.2 us
  transfers between devices with their start and end apart: 4, of which 4 were waited for; matrix products, arithmetic and copies ran while one was open for 9% of the time, Pallas kernels for 0%

commit v1 on v0

v1 whole, which is shorter than its diff:
```python
import math

import jax
import jax.numpy as jnp
from jax import lax
from jax.sharding import PartitionSpec as P

AXIS = "gx"
BF = jnp.bfloat16
F32 = jnp.float32


def gelu_parts(preact):
    value = preact.astype(F32)
    coeff = math.sqrt(2.0 / math.pi)
    inner = coeff * (value + 0.044715 * value * value * value)
    tangent = jnp.tanh(inner)
    activ = 0.5 * value * (1.0 + tangent)
    gelu_slope = 0.5 * (1.0 + tangent) + 0.5 * value * (1.0 - tangent * tangent) * coeff * (
        1.0 + 3.0 * 0.044715 * value * value
    )
    return (activ.astype(BF), gelu_slope)


def contract_last(left, right):
    return lax.dot_general(
        left, right, (((1,), (1,)), ((), ())), preferred_element_type=F32
    )


def contract_first(left, right):
    return lax.dot_general(
        left, right, (((0,), (0,)), ((), ())), preferred_element_type=F32
    )


def coords(d):
    return d // 8, (d // 4) % 2, (d // 2) % 2, d % 2


def index(z, y, x, c):
    return ((z * 2 + y) * 2 + x) * 2 + c


def moved(n, f):
    return [(d, index(*f(*coords(d)))) for d in range(n)]


def pick(array, at, axis):
    return lax.dynamic_index_in_dim(array, at, axis, keepdims=False)


def paired(mine, other, at, axis):
    first = jnp.where(at == 0, mine, other)
    second = jnp.where(at == 0, other, mine)
    return jnp.stack([first, second], axis)


def per_device(out_grad, inputs, preact, w_out, w_in):
    n = lax.axis_size(AXIS)
    nz = n // 8
    nl = nz // 2
    me = lax.axis_index(AXIS)
    z, y, x, c = coords(me)
    high, low = z // nl, z % nl
    grad_scale = 1.0 / math.sqrt(out_grad.shape[0] * n)
    tokens, width = out_grad.shape
    hidden = preact.shape[1]
    half = hidden // 2
    rows_out, rows_in = w_out.shape[0], w_in.shape[0]

    along_x = moved(n, lambda z, y, x, c: (z, y, 1 - x, c))
    along_y = moved(n, lambda z, y, x, c: (z, 1 - y, x, c))
    cores = moved(n, lambda z, y, x, c: (z, y, x, 1 - c))

    def send(array, perm):
        return lax.ppermute(array, AXIS, perm)

    def z_perm(k):
        return moved(n, lambda z, y, x, c: (z ^ k, y, x, c))

    def gather_perm(i, j):
        return moved(
            n, lambda z, y, x, c: ((c ^ i) * nl + ((z % nl) ^ j), y, x, z // nl)
        )

    def scatter_perm(i, j):
        return moved(
            n, lambda z, y, x, c: (c * nl + ((z % nl) ^ j), y, x, (z // nl) ^ i)
        )

    pre_split = preact.reshape(tokens, 2, half)
    pre_mine = pick(pre_split, c, 1)
    pre_other = send(pick(pre_split, 1 - c, 1), cores)
    out_grad2 = jnp.concatenate([out_grad, send(out_grad, cores)], 0)
    inputs2 = jnp.concatenate([inputs, send(inputs, cores)], 0)
    pre2 = jnp.concatenate([pre_mine, pre_other], 0)

    parts = [[send(w_out, gather_perm(i, j)) for j in range(nl)] for i in range(2)]
    parts = jnp.stack([jnp.stack(p, 0) for p in parts], 0)
    by_z = jnp.stack(
        [
            jnp.stack([parts[cc ^ high, ll ^ low] for cc in range(2)], 0)
            for ll in range(nl)
        ],
        0,
    )

    def gather_plane(array, cut):
        one, two = jnp.split(array, 2, cut)
        one = paired(one, send(one, along_x), x, 0)
        two = paired(two, send(two, along_y), y, 0)
        one = paired(one, send(one, along_y), y, 0)
        two = paired(two, send(two, along_x), x, 1)
        return jnp.concatenate([one, two], cut + 2)

    w_out2 = gather_plane(by_z, 1).transpose(2, 0, 1, 3, 4, 5).reshape(half, width)

    in_split = w_in.reshape(rows_in, 2, half)
    in_two = paired(pick(in_split, c, 1), send(pick(in_split, 1 - c, 1), cores), c, 0)
    parts = jnp.stack([in_two] + [send(in_two, z_perm(k)) for k in range(1, nz)], 0)
    by_z = jnp.stack([parts[zz ^ z] for zz in range(nz)], 0)
    w_in2 = gather_plane(by_z, 3).transpose(2, 0, 1, 3, 4, 5).reshape(width, half)

    def scatter_plane(total, cut):
        one, two = jnp.split(total, 2, cut)
        one = pick(one, x, 2) + send(pick(one, 1 - x, 2).astype(BF), along_x).astype(F32)
        two = pick(two, y, 1) + send(pick(two, 1 - y, 1).astype(BF), along_y).astype(F32)
        one = pick(one, y, 1) + send(pick(one, 1 - y, 1).astype(BF), along_y).astype(F32)
        two = pick(two, x, 1) + send(pick(two, 1 - x, 1).astype(BF), along_x).astype(F32)
        return jnp.concatenate([one, two], cut - 2)

    activ, slope = gelu_parts(pre2)
    total = contract_first(activ, out_grad2)
    total = total.reshape(nl, 2, 2, 2, rows_out, width)
    total = scatter_plane(total, 3)
    narrow = total.astype(BF)
    w_out_grad = 0.0
    for i in range(2):
        for j in range(nl):
            sent = send(narrow[low ^ j, high ^ i], scatter_perm(i, j)).astype(F32)
            if i == 0 and j == 0:
                sent = jnp.where(c == high, total[low, high], sent)
            w_out_grad = w_out_grad + sent
    w_out_grad = w_out_grad * grad_scale

    act_grad = contract_last(out_grad2, w_out2)
    pre_grad = (act_grad * slope).astype(BF)

    total = contract_first(inputs2, pre_grad)
    total = total.reshape(nz, 2, 2, 2 * rows_in, half)
    total = scatter_plane(total, 4)
    narrow = total.astype(BF)
    own = total[z]
    for k in range(1, nz):
        own = own + send(narrow[z ^ k], z_perm(k)).astype(F32)
    own = (own * grad_scale).reshape(2, rows_in, half)
    w_in_grad = paired(own[c], send(own[1 - c], cores), c, 1).reshape(rows_in, hidden)

    part = contract_last(pre_grad, w_in2)
    input_grad = part[:tokens] + send(part[tokens:], cores)
    return (input_grad, w_out_grad, w_in_grad)


def solution(mesh):
    in_specs = (
        P(("grp", "gx"), None),
        P(("grp", "gx"), None),
        P(("grp", "gx"), None),
        P("gx", None),
        P("gx", None),
    )
    out_specs = (P(("grp", "gx"), None), P(("grp", "gx"), None), P(("grp", "gx"), None))
    return jax.shard_map(
        per_device, mesh=mesh, in_specs=in_specs, out_specs=out_specs, check_vma=False
    )
```

time: 432 us -> 187 us (0.43)
  waiting for transfers between devices: 375 us -> 86.4 us
  starting transfers between devices: 0.16 us -> 51.8 us
  matrix products: 29.6 us -> 15.4 us
  local copies, waits for them, and re-layouts: 11.2 us -> 24.1 us
  between operations: 13.8 us -> 1.45 us
  other arithmetic: 0 us -> 6.94 us
    unnamed x5 -> x0, waiting for transfers between devices: 143 us -> none
    reduce_scatter x1 -> x0, waiting for transfers between devices: 131 us -> none  [per_device(): lax.psum_scatter(contract_first(activ, out_grad) * grad_scale, 'gx', scat...]
    all_gather x2 -> x0, waiting for transfers between devices: 99.9 us -> none  [the longest x1 58.9 us: per_device(): lax.all_gather(w_out, 'gx', axis=0, tiled=True)]
    ppermute x0 -> x36, waiting for transfers between devices: none -> 86.4 us  [send(): return lax.ppermute(array, AXIS, perm)]
    ppermute x0 -> x36, starting transfers between devices: none -> 51.8 us  [send(): return lax.ppermute(array, AXIS, perm)]
    reshape x0 -> x3, local copies, waits for them, and re-layouts: none -> 8.8 us  [the longest x1 7.06 us: per_device(): pre_split = preact.reshape(tokens, 2, half)]
    dynamic_slice x0 -> x3, local copies, waits for them, and re-layouts: none -> 8.47 us  [the longest x2 8.42 us: pick(): return lax.dynamic_index_in_dim(array, at, axis, keepdims=False)]
    dot_general x2, matrix products: 14.6 us -> 6.58 us  [contract_first(): lax.dot_general(left, right, (((0,), (0,)), ((), ())), preferred_element_...]
  transfers between devices with their start and end apart: 4 -> 36, of which waited for: 4 -> 16; matrix products, arithmetic and copies ran while one was open for 9% -> 24% of each run, Pallas kernels for 0% -> 0%
where the time goes in v1:
time: 187 us; the launch traced here: 186 us
  waiting for transfers between devices  86.4 us (46%)
  starting transfers between devices  51.8 us (28%)
  local copies, waits for them, and re-layouts  24.1 us (13%)
  matrix products  15.4 us (8%)
  other arithmetic  6.94 us (4%)
    ppermute x36, waiting for transfers between devices, send(): return lax.ppermute(array, AXIS, perm)  86.4 us
    ppermute x36, starting transfers between devices, send(): return lax.ppermute(array, AXIS, perm)  51.8 us
    dot_general x2, matrix products, contract_last(): lax.dot_general(left, right, (((1,), (1,)), ((), ())), preferred_element_...  8.81 us
    dynamic_slice x2, local copies, waits for them, and re-layouts, pick(): return lax.dynamic_index_in_dim(array, at, axis, keepdims=False)  8.42 us
    reshape x1, local copies, waits for them, and re-layouts, per_device(): pre_split = preact.reshape(tokens, 2, half)  7.06 us
    dot_general x2, matrix products, contract_first(): lax.dot_general(left, right, (((0,), (0,)), ((), ())), preferred_element_...  6.58 us
    unnamed x6, local copies, waits for them, and re-layouts  3.76 us
  transfers between devices with their start and end apart: 36, of which 16 were waited for; matrix products, arithmetic and copies ran while one was open for 24% of the time, Pallas kernels for 0%

profile of v1, /device:TPU:1, one launch (start us, length us, event | category | flops | bytes accessed | tf_op | source)
XLA Modules:
  0.0 186.1 jit_solution(1164808033118479305)
XLA Ops:
  0.6 4.8 %collective-permute-start.2 = (bf16[96,768]{1,0:T(8,128)(2,1)}, bf16[96,768]{1,0:T(8,128)(2,1)}, u32[]{:S(2)}, u32[]{:S(2)}) collective-permute-start(bf16[96,768]{1,0:T(8,128)(2,1)} %param.8), channel_id=1, source_target_pairs={{0,8},{1,24},{2,10},{3,26},{4,12},{5,28},{6,14},{7,30},{8,0},{9,16... | collective-permute-start | bytes 442376 | tf_op jit(solution)/shard_map/ppermute | solution.py:77
  11.0 7.1 %reshape.87 = bf16[512,2,1536]{2,1,0:T(2,128)(2,1)S(1)} reshape(bf16[512,3072]{1,0:T(8,128)(2,1)} %param.7) | data formatting | bytes 6291456 | tf_op jit(solution)/shard_map/reshape | solution.py:92
  18.1 8.1 %constant_dynamic-slice_fusion.11 = (bf16[512,1,1536]{2,1,0:T(2,128)(2,1)S(1)}, bf16[512,1,1536]{2,1,0:T(2,128)(2,1)}) fusion(bf16[512,2,1536]{2,1,0:T(2,128)(2,1)S(1)} %reshape.87, s32[]{:T(128)S(6)} %select_n.258, s32[]{:T(128)S(6)} %select_n.259), kind=kLoop, calls=%fused_computation.155 | loop fusion | bytes 6291464 | tf_op jit(solution)/shard_map/jit(dynamic_index_in_dim)/dynamic_slice | solution.py:50
  26.2 2.2 %copy.79 = bf16[512,1,1536]{2,0,1:T(8,128)(2,1)S(1)} copy(bf16[512,1,1536]{2,1,0:T(2,128)(2,1)} %get-tuple-element.8) | data formatting | bytes 3145728
  36.0 7.6 %collective-permute-done.3 = bf16[96,768]{1,0:T(8,128)(2,1)S(1)} collective-permute-done((bf16[96,768]{1,0:T(8,128)(2,1)}, bf16[96,768]{1,0:T(8,128)(2,1)S(1)}, u32[]{:S(2)}, u32[]{:S(2)}) %collective-permute-start.3) | collective-permute-done | bytes 147488 | tf_op jit(solution)/shard_map/ppermute | solution.py:77
  45.4 4.3 %collective-permute-done.12 = bf16[2,24,1536]{2,1,0:T(8,128)(2,1)S(1)} collective-permute-done((bf16[2,24,1536]{2,1,0:T(8,128)(2,1)S(1)}, bf16[2,24,1536]{2,1,0:T(8,128)(2,1)S(1)}, u32[]{:S(2)}, u32[]{:S(2)}) %collective-permute-start.12) | collective-permute-done | bytes 147488 | tf_op jit(solution)/shard_map/ppermute | solution.py:77
  53.7 4.3 %collective-permute-done.7 = bf16[2,1,96,768]{3,2,0,1:T(8,128)(2,1)S(1)} collective-permute-done((bf16[2,1,96,768]{3,2,0,1:T(8,128)(2,1)S(1)}, bf16[2,1,96,768]{3,2,0,1:T(8,128)(2,1)S(1)}, u32[]{:S(2)}, u32[]{:S(2)}) %collective-permute-start.7) | collective-permute-done | bytes 294944 | tf_op jit(solution)/shard_map/ppermute | solution.py:77
  61.8 4.6 %collective-permute-done.14 = bf16[4,2,24,768]{3,2,1,0:T(8,128)(2,1)S(1)} collective-permute-done((bf16[4,2,24,768]{3,2,1,0:T(8,128)(2,1)S(1)}, bf16[4,2,24,768]{3,2,1,0:T(8,128)(2,1)S(1)}, u32[]{:S(2)}, u32[]{:S(2)}) %collective-permute-start.14) | collective-permute-done | bytes 294944 | tf_op jit(solution)/shard_map/ppermute | solution.py:77
  71.2 8.5 %collective-permute-done.8 = bf16[2,2,1,96,768]{4,3,0,1,2:T(8,128)(2,1)S(1)} collective-permute-done((bf16[2,2,1,96,768]{4,3,0,1,2:T(8,128)(2,1)S(1)}, bf16[2,2,1,96,768]{4,3,0,1,2:T(8,128)(2,1)S(1)}, u32[]{:S(2)}, u32[]{:S(2)}) %collective-permute-start.8) | collective-permute-done | bytes 589856 | tf_op jit(solution)/shard_map/ppermute | solution.py:77
  81.4 10.9 %collective-permute-done.17 = bf16[2,4,2,24,768]{4,3,2,1,0:T(8,128)(2,1)S(1)} collective-permute-done((bf16[2,4,2,24,768]{4,3,2,1,0:T(8,128)(2,1)S(1)}, bf16[2,4,2,24,768]{4,3,2,1,0:T(8,128)(2,1)S(1)}, u32[]{:S(2)}, u32[]{:S(2)}) %collective-permute-start.17) | collective-permute-done | bytes 589856 | tf_op jit(solution)/shard_map/ppermute | solution.py:77
  93.0 6.2 %fusion.6 = bf16[1024,1536]{1,0:T(8,128)(2,1)S(1)} fusion(bf16[1024,768]{1,0:T(8,128)(2,1)S(1)} %constant_dynamic-update-slice_fusion, bf16[1536,768]{1,0:T(8,128)(2,1)S(1)} %bitcast.199, bf16[512,1536]{1,0:T(8,128)(2,1)S(1)} %collective-permute-done.9, bf16[512,1536]{1,0:T(8,128)(2,1)S(1)} %bitcast.201), kind=kOutput, calls=%fused_computation.13 | convolution fusion | flops 2452094976 | bytes 10223616 | tf_op jit(solution)/shard_map/dot_general | solution.py:26
  99.2 2.6 %fusion.67 = f32[1024,768]{1,0:T(8,128)S(1)} fusion(bf16[1024,1536]{1,0:T(8,128)(2,1)S(1)} %fusion.6, bf16[768,1536]{1,0:T(8,128)(2,1)S(1)} %bitcast.200), kind=kOutput, calls=%fused_computation.168 | convolution fusion | flops 2415919104 | bytes 8650752 | tf_op jit(solution)/shard_map/dot_general | solution.py:26
  101.9 3.6 %collective-permute-start.18 = (f32[512,768]{1,0:T(8,128)S(1)}, f32[512,768]{1,0:T(8,128)S(1)}, u32[]{:S(2)}, u32[]{:S(2)}) collective-permute-start(f32[512,768]{1,0:T(8,128)S(1)} %slice.9), channel_id=1, source_target_pairs={{0,1},{1,0},{2,3},{3,2},{4,5},{5,4},{6,7},{7,6},{8,9},{9,8},{10,11... | collective-permute-start | bytes 4718600 | tf_op jit(solution)/shard_map/ppermute | solution.py:77
  105.6 3.9 %fusion.11 = f32[1536,768]{1,0:T(8,128)S(1)} fusion(bf16[1024,768]{1,0:T(8,128)(2,1)S(1)} %constant_dynamic-update-slice_fusion, bf16[512,1536]{1,0:T(8,128)(2,1)S(1)} %collective-permute-done.9, bf16[512,1536]{1,0:T(8,128)(2,1)S(1)} %bitcast.202), kind=kOutput, calls=%fused_computation.19 | convolution fusion | flops 2436366336 | bytes 9437184 | tf_op jit(solution)/shard_map/dot_general | solution.py:32
  110.9 2.6 %fusion.13 = f32[768,1536]{1,0:T(8,128)S(1)} fusion(bf16[1024,1536]{1,0:T(8,128)(2,1)S(1)} %fusion.6, bf16[512,768]{1,0:T(8,128)(2,1)S(1)} %collective-permute-done.27, bf16[512,768]{1,0:T(8,128)(2,1)S(1)} %copy-done), kind=kOutput, calls=%fused_computation.23 | convolution fusion | flops 2419064832 | bytes 9437184 | tf_op jit(solution)/shard_map/dot_general | solution.py:32
  116.7 8.3 %collective-permute-done.19 = bf16[2,2,1,96,768]{4,3,0,2,1:T(8,128)(2,1)S(1)} collective-permute-done((bf16[2,2,1,96,768]{4,3,0,2,1:T(8,128)(2,1)S(1)}, bf16[2,2,1,96,768]{4,3,0,2,1:T(8,128)(2,1)S(1)}, u32[]{:S(2)}, u32[]{:S(2)}) %collective-permute-start.19) | collective-permute-done | bytes 589856 | tf_op jit(solution)/shard_map/ppermute | solution.py:77
  126.5 11.2 %collective-permute-done.28 = bf16[4,2,48,768]{3,2,0,1:T(8,128)(2,1)S(1)} collective-permute-done((bf16[4,2,48,768]{3,2,0,1:T(8,128)(2,1)S(1)}, bf16[4,2,48,768]{3,2,0,1:T(8,128)(2,1)S(1)}, u32[]{:S(2)}, u32[]{:S(2)}) %collective-permute-start.28) | collective-permute-done | bytes 589856 | tf_op jit(solution)/shard_map/ppermute | solution.py:77
  139.1 2.9 %collective-permute-done.30 = bf16[4,2,48,768]{3,2,1,0:T(8,128)(2,1)S(1)} collective-permute-done((bf16[4,2,48,768]{3,2,1,0:T(8,128)(2,1)S(1)}, bf16[4,2,48,768]{3,2,1,0:T(8,128)(2,1)S(1)}, u32[]{:S(2)}, u32[]{:S(2)}) %collective-permute-start.30) | collective-permute-done | bytes 589856 | tf_op jit(solution)/shard_map/ppermute | solution.py:77
  144.0 10.7 %collective-permute-done.29 = bf16[4,48,768]{2,1,0:T(8,128)(2,1)S(1)} collective-permute-done((bf16[4,48,768]{2,1,0:T(8,128)(2,1)S(1)}, bf16[4,48,768]{2,1,0:T(8,128)(2,1)S(1)}, u32[]{:S(2)}, u32[]{:S(2)}) %collective-permute-start.29) | collective-permute-done | bytes 294944 | tf_op jit(solution)/shard_map/ppermute | solution.py:77
  156.2 2.4 %collective-permute-start.32 = (bf16[48,1536]{1,0:T(8,128)(2,1)S(1)}, bf16[48,1536]{1,0:T(8,128)(2,1)S(1)}, u32[]{:S(2)}, u32[]{:S(2)}) collective-permute-start(bf16[48,1536]{1,0:T(8,128)(2,1)S(1)} %get-tuple-element.19), channel_id=1, source_target_pairs={{0,8},{1,9},{2,10},{3,11},{4,12},{5,13},{6,14},{7,15},{8,0},{9,1},... | collective-permute-start | bytes 442376 | tf_op jit(solution)/shard_map/ppermute | solution.py:77
  161.0 3.4 %collective-permute-start.25 = (bf16[96,768]{1,0:T(8,128)(2,1)S(1)}, bf16[96,768]{1,0:T(8,128)(2,1)S(1)}, u32[]{:S(2)}, u32[]{:S(2)}) collective-permute-start(bf16[96,768]{1,0:T(8,128)(2,1)S(1)} %get-tuple-element.24), channel_id=1, source_target_pairs={{0,1},{1,17},{2,3},{3,19},{4,5},{5,21},{6,7},{7,23},{8,9},{9,25},{... | collective-permute-start | bytes 442376 | tf_op jit(solution)/shard_map/ppermute | solution.py:77
  164.5 3.4 %collective-permute-done.33 = bf16[48,1536]{1,0:T(8,128)(2,1)S(1)} collective-permute-done((bf16[48,1536]{1,0:T(8,128)(2,1)S(1)}, bf16[48,1536]{1,0:T(8,128)(2,1)S(1)}, u32[]{:S(2)}, u32[]{:S(2)}) %collective-permute-start.33) | collective-permute-done | bytes 147488 | tf_op jit(solution)/shard_map/ppermute | solution.py:77
  167.8 8.0 %collective-permute-start.24 = (bf16[96,768]{1,0:T(8,128)(2,1)S(1)}, bf16[96,768]{1,0:T(8,128)(2,1)S(1)}, u32[]{:S(2)}, u32[]{:S(2)}) collective-permute-start(bf16[96,768]{1,0:T(8,128)(2,1)S(1)} %get-tuple-element.25), channel_id=1, source_target_pairs={{0,8},{1,24},{2,10},{3,26},{4,12},{5,28},{6,14},{7,30},{8,0},{9,16... | collective-permute-start | bytes 442376 | tf_op jit(solution)/shard_map/ppermute | solution.py:77
  178.7 4.4 %collective-permute-done.23 = bf16[96,768]{1,0:T(8,128)(2,1)S(1)} collective-permute-done((bf16[96,768]{1,0:T(8,128)(2,1)S(1)}, bf16[96,768]{1,0:T(8,128)(2,1)S(1)}, u32[]{:S(2)}, u32[]{:S(2)}) %collective-permute-start.23) | collective-permute-done | bytes 147488 | tf_op jit(solution)/shard_map/ppermute | solution.py:77
  (119 shorter events, 48.5 us)
Async XLA Ops:
  0.6 30.9 %collective-permute-start.2 = (bf16[96,768]{1,0:T(8,128)(2,1)}, bf16[96,768]{1,0:T(8,128)(2,1)}, u32[]{:S(2)}, u32[]{:S(2)}) collective-permute-start(bf16[96,768]{1,0:T(8,128)(2,1)} %param.8), channel_id=1, source_target_pairs={{0,8},{1,24},{2,10},{3,26},{4,12},{5,28},{6,14},{7,30},{8,0},{9,16... | collective-permute-start | bytes 442376 | tf_op jit(solution)/shard_map/ppermute | solution.py:77
  5.4 27.3 %collective-permute-start.1 = (bf16[96,768]{1,0:T(8,128)(2,1)}, bf16[96,768]{1,0:T(8,128)(2,1)}, u32[]{:S(2)}, u32[]{:S(2)}) collective-permute-start(bf16[96,768]{1,0:T(8,128)(2,1)} %param.8), channel_id=1, source_target_pairs={{0,0},{1,16},{2,2},{3,18},{4,4},{5,20},{6,6},{7,22},{8,8},{9,24},{... | collective-permute-start | bytes 442376 | tf_op jit(solution)/shard_map/ppermute | solution.py:77
  7.3 28.5 %collective-permute-start.4 = (bf16[96,768]{1,0:T(8,128)(2,1)}, bf16[96,768]{1,0:T(8,128)(2,1)S(1)}, u32[]{:S(2)}, u32[]{:S(2)}) collective-permute-start(bf16[96,768]{1,0:T(8,128)(2,1)} %param.8), channel_id=1, source_target_pairs={{0,24},{1,8},{2,26},{3,10},{4,28},{5,12},{6,30},{7,14},{8,16},{9,0... | collective-permute-start | bytes 442376 | tf_op jit(solution)/shard_map/ppermute | solution.py:77
  7.4 61.7 %collective-permute-start = (bf16[512,768]{1,0:T(8,128)(2,1)}, bf16[512,768]{1,0:T(8,128)(2,1)}, u32[]{:S(2)}, u32[]{:S(2)}) collective-permute-start(bf16[512,768]{1,0:T(8,128)(2,1)} %param.5), channel_id=1, source_target_pairs={{0,1},{1,0},{2,3},{3,2},{4,5},{5,4},{6,7},{7,6},{8,9},{9,8},{10,11... | collective-permute-start | bytes 2359304 | tf_op jit(solution)/shard_map/ppermute | solution.py:77
  10.8 19.2 %collective-permute-start.10 = (bf16[24,1536]{1,0:T(8,128)(2,1)S(1)}, bf16[24,1536]{1,0:T(8,128)(2,1)}, u32[]{:S(2)}, u32[]{:S(2)}) collective-permute-start(bf16[24,1536]{1,0:T(8,128)(2,1)S(1)} %bitcast.212), channel_id=1, source_target_pairs={{0,1},{1,0},{2,3},{3,2},{4,5},{5,4},{6,7},{7,6},{8,9},{9,8},{10,11... | collective-permute-start | bytes 221192 | tf_op jit(solution)/shard_map/ppermute | solution.py:77
  30.0 13.5 %collective-permute-start.3 = (bf16[96,768]{1,0:T(8,128)(2,1)}, bf16[96,768]{1,0:T(8,128)(2,1)S(1)}, u32[]{:S(2)}, u32[]{:S(2)}) collective-permute-start(bf16[96,768]{1,0:T(8,128)(2,1)} %param.8), channel_id=1, source_target_pairs={{0,16},{1,0},{2,18},{3,2},{4,20},{5,4},{6,22},{7,6},{8,24},{9,8},{... | collective-permute-start | bytes 442376 | tf_op jit(solution)/shard_map/ppermute | solution.py:77
  31.5 61.5 %collective-permute-start.9 = (bf16[512,1536]{1,0:T(8,128)(2,1)S(1)}, bf16[512,1536]{1,0:T(8,128)(2,1)S(1)}, u32[]{:S(2)}, u32[]{:S(2)}) collective-permute-start(bf16[512,1536]{1,0:T(8,128)(2,1)S(1)} %bitcast.203), channel_id=1, source_target_pairs={{0,1},{1,0},{2,3},{3,2},{4,5},{5,4},{6,7},{7,6},{8,9},{9,8},{10,11... | collective-permute-start | bytes 4718600 | tf_op jit(solution)/shard_map/ppermute | solution.py:77
  35.8 13.9 %collective-permute-start.12 = (bf16[2,24,1536]{2,1,0:T(8,128)(2,1)S(1)}, bf16[2,24,1536]{2,1,0:T(8,128)(2,1)S(1)}, u32[]{:S(2)}, u32[]{:S(2)}) collective-permute-start(bf16[2,24,1536]{2,1,0:T(8,128)(2,1)S(1)} %get-tuple-element.49), channel_id=1, source_target_pairs={{0,16},{1,17},{2,18},{3,19},{4,20},{5,21},{6,22},{7,23},{8,24},{9,... | collective-permute-start | bytes 442376 | tf_op jit(solution)/shard_map/ppermute | solution.py:77
  44.0 66.9 %collective-permute-start.27 = (bf16[512,768]{1,0:T(8,128)(2,1)S(1)}, bf16[512,768]{1,0:T(8,128)(2,1)S(1)}, u32[]{:S(2)}, u32[]{:S(2)}) collective-permute-start(bf16[512,768]{1,0:T(8,128)(2,1)S(1)} %copy-done), channel_id=1, source_target_pairs={{0,1},{1,0},{2,3},{3,2},{4,5},{5,4},{6,7},{7,6},{8,9},{9,8},{10,11... | collective-permute-start | bytes 2359304 | tf_op jit(solution)/shard_map/ppermute | solution.py:77
  66.4 13.3 %collective-permute-start.8 = (bf16[2,2,1,96,768]{4,3,0,1,2:T(8,128)(2,1)S(1)}, bf16[2,2,1,96,768]{4,3,0,1,2:T(8,128)(2,1)S(1)}, u32[]{:S(2)}, u32[]{:S(2)}) collective-permute-start(bf16[2,2,1,96,768]{4,3,0,1,2:T(8,128)(2,1)S(1)} %pad_maximum_fusion.6), channel_id=1, source_target_pairs={{0,2},{1,3},{2,0},{3,1},{4,6},{5,7},{6,4},{7,5},{8,10},{9,11},{10,... | collective-permute-start | bytes 1769480 | tf_op jit(solution)/shard_map/ppermute | solution.py:77
  67.6 13.4 %collective-permute-start.6 = (bf16[2,2,1,96,768]{4,3,1,0,2:T(8,128)(2,1)S(1)}, bf16[2,2,1,96,768]{4,3,1,0,2:T(8,128)(2,1)S(1)}, u32[]{:S(2)}, u32[]{:S(2)}) collective-permute-start(bf16[2,2,1,96,768]{4,3,1,0,2:T(8,128)(2,1)S(1)} %fusion.26), channel_id=1, source_target_pairs={{0,4},{1,5},{2,6},{3,7},{4,0},{5,1},{6,2},{7,3},{8,12},{9,13},{10,... | collective-permute-start | bytes 1769480 | tf_op jit(solution)/shard_map/ppermute | solution.py:77
  69.1 23.3 %collective-permute-start.17 = (bf16[2,4,2,24,768]{4,3,2,1,0:T(8,128)(2,1)S(1)}, bf16[2,4,2,24,768]{4,3,2,1,0:T(8,128)(2,1)S(1)}, u32[]{:S(2)}, u32[]{:S(2)}) collective-permute-start(bf16[2,4,2,24,768]{4,3,2,1,0:T(8,128)(2,1)S(1)} %pad_maximum_fusion.10), channel_id=1, source_target_pairs={{0,2},{1,3},{2,0},{3,1},{4,6},{5,7},{6,4},{7,5},{8,10},{9,11},{10,... | collective-permute-start | bytes 1769480 | tf_op jit(solution)/shard_map/ppermute | solution.py:77
  101.9 82.8 %collective-permute-start.18 = (f32[512,768]{1,0:T(8,128)S(1)}, f32[512,768]{1,0:T(8,128)S(1)}, u32[]{:S(2)}, u32[]{:S(2)}) collective-permute-start(f32[512,768]{1,0:T(8,128)S(1)} %slice.9), channel_id=1, source_target_pairs={{0,1},{1,0},{2,3},{3,2},{4,5},{5,4},{6,7},{7,6},{8,9},{9,8},{10,11... | collective-permute-start | bytes 4718600 | tf_op jit(solution)/shard_map/ppermute | solution.py:77
  110.0 15.0 %collective-permute-start.19 = (bf16[2,2,1,96,768]{4,3,0,2,1:T(8,128)(2,1)S(1)}, bf16[2,2,1,96,768]{4,3,0,2,1:T(8,128)(2,1)S(1)}, u32[]{:S(2)}, u32[]{:S(2)}) collective-permute-start(bf16[2,2,1,96,768]{4,3,0,2,1:T(8,128)(2,1)S(1)} %fusion.24), channel_id=1, source_target_pairs={{0,2},{1,3},{2,0},{3,1},{4,6},{5,7},{6,4},{7,5},{8,10},{9,11},{10,... | collective-permute-start | bytes 1769480 | tf_op jit(solution)/shard_map/ppermute | solution.py:77
  114.3 23.4 %collective-permute-start.28 = (bf16[4,2,48,768]{3,2,0,1:T(8,128)(2,1)S(1)}, bf16[4,2,48,768]{3,2,0,1:T(8,128)(2,1)S(1)}, u32[]{:S(2)}, u32[]{:S(2)}) collective-permute-start(bf16[4,2,48,768]{3,2,0,1:T(8,128)(2,1)S(1)} %fusion.25), channel_id=1, source_target_pairs={{0,2},{1,3},{2,0},{3,1},{4,6},{5,7},{6,4},{7,5},{8,10},{9,11},{10,... | collective-permute-start | bytes 1769480 | tf_op jit(solution)/shard_map/ppermute | solution.py:77
  115.1 28.1 %collective-permute-start.21 = (bf16[2,2,1,96,768]{4,3,1,0,2:T(8,128)(2,1)S(1)}, bf16[2,2,1,96,768]{4,3,1,0,2:T(8,128)(2,1)S(1)}, u32[]{:S(2)}, u32[]{:S(2)}) collective-permute-start(bf16[2,2,1,96,768]{4,3,1,0,2:T(8,128)(2,1)S(1)} %fusion.22), channel_id=1, source_target_pairs={{0,4},{1,5},{2,6},{3,7},{4,0},{5,1},{6,2},{7,3},{8,12},{9,13},{10,... | collective-permute-start | bytes 1769480 | tf_op jit(solution)/shard_map/ppermute | solution.py:77
  116.4 25.6 %collective-permute-start.30 = (bf16[4,2,48,768]{3,2,1,0:T(8,128)(2,1)S(1)}, bf16[4,2,48,768]{3,2,1,0:T(8,128)(2,1)S(1)}, u32[]{:S(2)}, u32[]{:S(2)}) collective-permute-start(bf16[4,2,48,768]{3,2,1,0:T(8,128)(2,1)S(1)} %fusion.23), channel_id=1, source_target_pairs={{0,4},{1,5},{2,6},{3,7},{4,0},{5,1},{6,2},{7,3},{8,12},{9,13},{10,... | collective-permute-start | bytes 1769480 | tf_op jit(solution)/shard_map/ppermute | solution.py:77
  125.2 31.0 %collective-permute-start.20 = (bf16[2,1,96,768]{3,2,0,1:T(8,128)(2,1)S(1)}, bf16[2,1,96,768]{3,2,0,1:T(8,128)(2,1)S(1)}, u32[]{:S(2)}, u32[]{:S(2)}) collective-permute-start(bf16[2,1,96,768]{3,2,0,1:T(8,128)(2,1)S(1)} %fusion.27), channel_id=1, source_target_pairs={{0,4},{1,5},{2,6},{3,7},{4,0},{5,1},{6,2},{7,3},{8,12},{9,13},{10,... | collective-permute-start | bytes 884744 | tf_op jit(solution)/shard_map/ppermute | solution.py:77
  137.8 16.9 %collective-permute-start.29 = (bf16[4,48,768]{2,1,0:T(8,128)(2,1)S(1)}, bf16[4,48,768]{2,1,0:T(8,128)(2,1)S(1)}, u32[]{:S(2)}, u32[]{:S(2)}) collective-permute-start(bf16[4,48,768]{2,1,0:T(8,128)(2,1)S(1)} %fusion.29), channel_id=1, source_target_pairs={{0,4},{1,5},{2,6},{3,7},{4,0},{5,1},{6,2},{7,3},{8,12},{9,13},{10,... | collective-permute-start | bytes 884744 | tf_op jit(solution)/shard_map/ppermute | solution.py:77
  143.3 15.3 %collective-permute-start.22 = (bf16[2,1,96,768]{3,2,0,1:T(8,128)(2,1)S(1)}, bf16[2,1,96,768]{3,2,0,1:T(8,128)(2,1)S(1)}, u32[]{:S(2)}, u32[]{:S(2)}) collective-permute-start(bf16[2,1,96,768]{3,2,0,1:T(8,128)(2,1)S(1)} %fusion.28), channel_id=1, source_target_pairs={{0,2},{1,3},{2,0},{3,1},{4,6},{5,7},{6,4},{7,5},{8,10},{9,11},{10,... | collective-permute-start | bytes 884744 | tf_op jit(solution)/shard_map/ppermute | solution.py:77
  155.0 12.8 %collective-permute-start.33 = (bf16[48,1536]{1,0:T(8,128)(2,1)S(1)}, bf16[48,1536]{1,0:T(8,128)(2,1)S(1)}, u32[]{:S(2)}, u32[]{:S(2)}) collective-permute-start(bf16[48,1536]{1,0:T(8,128)(2,1)S(1)} %get-tuple-element.21), channel_id=1, source_target_pairs={{0,16},{1,17},{2,18},{3,19},{4,20},{5,21},{6,22},{7,23},{8,24},{9,... | collective-permute-start | bytes 442376 | tf_op jit(solution)/shard_map/ppermute | solution.py:77
  156.2 19.6 %collective-permute-start.32 = (bf16[48,1536]{1,0:T(8,128)(2,1)S(1)}, bf16[48,1536]{1,0:T(8,128)(2,1)S(1)}, u32[]{:S(2)}, u32[]{:S(2)}) collective-permute-start(bf16[48,1536]{1,0:T(8,128)(2,1)S(1)} %get-tuple-element.19), channel_id=1, source_target_pairs={{0,8},{1,9},{2,10},{3,11},{4,12},{5,13},{6,14},{7,15},{8,0},{9,1},... | collective-permute-start | bytes 442376 | tf_op jit(solution)/shard_map/ppermute | solution.py:77
  158.8 19.0 %collective-permute-start.26 = (bf16[96,768]{1,0:T(8,128)(2,1)S(1)}, bf16[96,768]{1,0:T(8,128)(2,1)S(1)}, u32[]{:S(2)}, u32[]{:S(2)}) collective-permute-start(bf16[96,768]{1,0:T(8,128)(2,1)S(1)} %get-tuple-element.23), channel_id=1, source_target_pairs={{0,9},{1,25},{2,11},{3,27},{4,13},{5,29},{6,15},{7,31},{8,1},{9,17... | collective-permute-start | bytes 442376 | tf_op jit(solution)/shard_map/ppermute | solution.py:77
  161.0 16.9 %collective-permute-start.25 = (bf16[96,768]{1,0:T(8,128)(2,1)S(1)}, bf16[96,768]{1,0:T(8,128)(2,1)S(1)}, u32[]{:S(2)}, u32[]{:S(2)}) collective-permute-start(bf16[96,768]{1,0:T(8,128)(2,1)S(1)} %get-tuple-element.24), channel_id=1, source_target_pairs={{0,1},{1,17},{2,3},{3,19},{4,5},{5,21},{6,7},{7,23},{8,9},{9,25},{... | collective-permute-start | bytes 442376 | tf_op jit(solution)/shard_map/ppermute | solution.py:77
  (13 other events, 117.0 us)

commit v2 on v1

--- a/solution.py
+++ b/solution.py
@@ -3,6 +3,8 @@
 import jax
 import jax.numpy as jnp
 from jax import lax
+from jax.experimental import pallas as pl
+from jax.experimental.pallas import tpu as pltpu
 from jax.sharding import PartitionSpec as P
 
 AXIS = "gx"
@@ -56,7 +58,7 @@
     return jnp.stack([first, second], axis)
 
 
-def per_device(out_grad, inputs, preact, w_out, w_in):
+def plain(out_grad, inputs, preact, w_out, w_in):
     n = lax.axis_size(AXIS)
     nz = n // 8
     nl = nz // 2
@@ -162,6 +164,868 @@
     return (input_grad, w_out_grad, w_in_grad)
 
 
+MIB = 1 << 20
+ANY = pl.BlockSpec(memory_space=pl.ANY)
+VMEM = pl.BlockSpec(memory_space=pltpu.VMEM)
+SMEM = pl.BlockSpec(memory_space=pltpu.SMEM)
+
+
+def shape(dims, kind):
+    return jax.ShapeDtypeStruct(dims, kind)
+
+
+class Order:
+    def __init__(self):
+        self.after = []
+
+    def __call__(self, outs):
+        self.after = [outs[0]]
+        return outs
+
+
+def small(body, where, arrays, outs, after=(), scratch=(), name=None, flops=0):
+    skipped = len(after)
+
+    def run(*refs):
+        body(*refs[: 1 + len(arrays)], *refs[1 + len(arrays) + skipped :])
+
+    moved_bytes = sum(a.size * a.dtype.itemsize for a in list(arrays) + list(outs))
+    return pl.pallas_call(
+        run,
+        name=name or body.__name__,
+        out_shape=outs,
+        in_specs=[SMEM] + [VMEM] * len(arrays) + [ANY] * skipped,
+        out_specs=[VMEM] * len(outs),
+        scratch_shapes=list(scratch),
+        compiler_params=pltpu.CompilerParams(vmem_limit_bytes=16 * MIB),
+        cost_estimate=pl.CostEstimate(
+            flops=flops, bytes_accessed=moved_bytes, transcendentals=0
+        ),
+    )(where, *arrays, *after)
+
+
+def pair_kernel(at, in_ref, got_ref, out):
+    c = at[3]
+    size = out.shape[2]
+    out[c] = jnp.where(c == 0, in_ref[:, :size], in_ref[:, size:])
+    out[1 - c] = jnp.where(c == 0, got_ref[:, :size], got_ref[:, size:])
+
+
+def join_kernel(at, own1, got1, own2, got2, one, two):
+    x, y = at[2], at[1]
+    one[x] = own1[...]
+    one[1 - x] = got1[...]
+    two[y] = own2[...]
+    two[1 - y] = got2[...]
+
+
+def rows_kernel(at, g00, g01, g10, g11, one, two):
+    high, low = at[4], at[5]
+    rows = g00.shape[0]
+    for cc in range(2):
+        from_same = jnp.where(high == cc, g00[...], g10[...])
+        from_next = jnp.where(high == cc, g01[...], g11[...])
+        part = pl.ds(cc * rows, rows)
+        one[part, :] = jnp.where(low == 0, from_same, from_next)
+        two[part, :] = jnp.where(low == 0, from_next, from_same)
+
+
+def columns_kernel(at, mine, g1, g2, g3, one, two):
+    z = at[0]
+    rows, size = mine.shape[0] * mine.shape[1], one.shape[2]
+    for k, got in enumerate((mine, g1, g2, g3)):
+        value = got[...].reshape(rows, 2 * size)
+        one[z ^ k] = value[:, :size]
+        two[z ^ k] = value[:, size:]
+
+
+def out_total(at, cut, pre, pre_got, grad, grad_got, after):
+    tokens, width = grad.shape
+    size = pre_got.shape[1] // 8
+    rows = size // 2
+
+    def body(at, pre_ref, got_ref, grad_ref, grad2_ref, *refs):
+        slope, send, keep, total = refs[-4:]
+        t = pl.program_id(0)
+        x, y = at[2], at[1]
+        activ, slope1 = gelu_parts(pre_ref[...])
+        slope[pl.ds(0, tokens), :] = slope1
+        value = contract_first(activ, grad_ref[...])
+        activ, slope2 = gelu_parts(got_ref[...])
+        slope[pl.ds(tokens, tokens), :] = slope2
+        value = value + contract_first(activ, grad2_ref[...])
+        if cut == 0:
+            total[...] = value.reshape(2, rows, width)
+            send[0] = total[1 - x].astype(BF)
+            keep[0] = total[x]
+        else:
+
+            @pl.when(t == y)
+            def _():
+                keep[...] = value.reshape(2, rows, width)
+
+            @pl.when(t != y)
+            def _():
+                send[...] = value.astype(BF).reshape(2, rows, width)
+
+    whole = lambda t, at: (0, 0)
+    if cut == 0:
+        parts = pl.BlockSpec((1, rows, width), lambda t, at: (t, 0, 0))
+    else:
+        parts = pl.BlockSpec((2, rows, width), lambda t, at: (0, 0, 0))
+    return pl.pallas_call(
+        body,
+        name=f"out_total{cut}",
+        grid_spec=pltpu.PrefetchScalarGridSpec(
+            num_scalar_prefetch=1,
+            grid=(2,),
+            in_specs=[
+                pl.BlockSpec((tokens, size), lambda t, at: (0, at[3] * 4 + cut * 2 + t)),
+                pl.BlockSpec((tokens, size), lambda t, at: (0, at[3] * 4 + cut * 2 + t)),
+                pl.BlockSpec((tokens, width), whole),
+                pl.BlockSpec((tokens, width), whole),
+            ]
+            + [ANY] * len(after),
+            out_specs=[
+                pl.BlockSpec((2 * tokens, size), lambda t, at: (0, t)),
+                parts,
+                parts,
+            ],
+            scratch_shapes=[pltpu.VMEM((2, rows, width), F32)],
+        ),
+        out_shape=[
+            shape((2 * tokens, 2 * size), F32),
+            shape((2, rows, width), BF),
+            shape((2, rows, width), F32),
+        ],
+        compiler_params=pltpu.CompilerParams(vmem_limit_bytes=24 * MIB),
+        cost_estimate=pl.CostEstimate(
+            flops=8 * tokens * size * width,
+            bytes_accessed=20 * MIB,
+            transcendentals=4 * tokens * size,
+        ),
+    )(at, pre, pre_got, grad, grad_got, *after)
+
+
+def in_total(at, cut, grad, grad_got, inputs, inputs_got, slope, pieces, nz, after):
+    tokens, width = grad.shape
+    size = slope.shape[1] // 2
+    rows = size // 2
+    depth = width // (4 * nz)
+
+    def body(at, grad_ref, grad2_ref, in_ref, in2_ref, slope_ref, mine, other, _, pre_grad, send, keep):
+        t = pl.program_id(0)
+        x, y = at[2], at[1]
+        if cut == 0:
+            value = jnp.where(t == y, mine[...], other[...]).reshape(size, width)
+        else:
+            first, second = mine[t], other[t]
+            value = jnp.concatenate(
+                [jnp.where(x == 0, first, second), jnp.where(x == 0, second, first)], 0
+            )
+        totals = 0.0
+        for part, (g, i) in enumerate(((grad_ref, in_ref), (grad2_ref, in2_ref))):
+            at_rows = pl.ds(part * tokens, tokens)
+            act_grad = contract_last(g[...], value)
+            pre = (act_grad * slope_ref[at_rows, :]).astype(BF)
+            pre_grad[at_rows, :] = pre
+            totals = totals + contract_first(i[...], pre)
+        parts = totals.reshape(nz, 2, 2, depth, size)
+        if cut == 0:
+            first, second, bit = parts[:, :, 0], parts[:, :, 1], x
+        else:
+            first, second, bit = parts[:, 0], parts[:, 1], y
+        send[...] = jnp.where(bit == 0, second, first).astype(BF)
+        keep[...] = jnp.where(bit == 0, first, second)
+
+    whole = lambda t, at: (0, 0)
+    tile = lambda t, at: (0, t)
+    piece = pl.BlockSpec((2, rows, width), lambda t, at: (0, 0, 0))
+    parts = pl.BlockSpec((nz, 2, depth, size), lambda t, at: (0, 0, 0, t))
+    return pl.pallas_call(
+        body,
+        name=f"in_total{cut}",
+        grid_spec=pltpu.PrefetchScalarGridSpec(
+            num_scalar_prefetch=1,
+            grid=(2,),
+            in_specs=[pl.BlockSpec((tokens, width), whole)] * 4
+            + [pl.BlockSpec((2 * tokens, size), tile)]
+            + [piece] * 2
+            + [ANY],
+            out_specs=[pl.BlockSpec((2 * tokens, size), tile), parts, parts],
+        ),
+        out_shape=[
+            shape((2 * tokens, 2 * size), BF),
+            shape((nz, 2, depth, 2 * size), BF),
+            shape((nz, 2, depth, 2 * size), F32),
+        ],
+        compiler_params=pltpu.CompilerParams(vmem_limit_bytes=24 * MIB),
+        cost_estimate=pl.CostEstimate(
+            flops=16 * tokens * size * width, bytes_accessed=16 * MIB, transcendentals=0
+        ),
+    )(at, grad, grad_got, inputs, inputs_got, slope, *pieces, *after)
+
+
+def input_part(at, pre_grads, pieces, nz, after):
+    tokens, size = pre_grads[0].shape[0] // 2, pre_grads[0].shape[1]
+    depth = pieces[0].shape[2]
+    width = 4 * nz * depth
+
+    def body(at, g0, g1, a0, a1, b0, b1, _, mine, other, weight0, weight1):
+        t = pl.program_id(0)
+        x, y = at[2], at[1]
+
+        @pl.when(t == 0)
+        def _():
+            for k in range(2):
+                weight0[:, y, k] = a0[k]
+                weight0[:, 1 - y, k] = a1[k]
+                weight1[:, k, x] = b0[k]
+                weight1[:, k, 1 - x] = b1[k]
+
+        value = contract_last(g0[...], weight0[...].reshape(width, size))
+        value = value + contract_last(g1[...], weight1[...].reshape(width, size))
+
+        @pl.when(t == 0)
+        def _():
+            other[...] = value
+
+        @pl.when(t == 1)
+        def _():
+            mine[...] = value
+
+    piece = pl.BlockSpec((2, nz, depth, size), lambda t, at: (0, 0, 0, 0))
+    rows = pl.BlockSpec((tokens, size), lambda t, at: (1 - t, 0))
+    out = pl.BlockSpec((tokens, width), lambda t, at: (0, 0))
+    return pl.pallas_call(
+        body,
+        name="input_part",
+        grid_spec=pltpu.PrefetchScalarGridSpec(
+            num_scalar_prefetch=1,
+            grid=(2,),
+            in_specs=[rows] * 2 + [piece] * 4 + [ANY],
+            out_specs=[out, out],
+            scratch_shapes=[pltpu.VMEM((nz, 2, 2, depth, size), BF)] * 2,
+        ),
+        out_shape=[shape((tokens, width), F32)] * 2,
+        compiler_params=pltpu.CompilerParams(vmem_limit_bytes=24 * MIB),
+        cost_estimate=pl.CostEstimate(
+            flops=8 * tokens * size * width, bytes_accessed=10 * MIB, transcendentals=0
+        ),
+    )(at, *pre_grads, *pieces, *after)
+
+
+def per_device(out_grad, inputs, preact, w_out, w_in):
+    n = lax.axis_size(AXIS)
+    rows_out, rows_in = w_out.shape[0], w_in.shape[0]
+    if n != 32 or rows_out % 16 or (2 * rows_in) % 16 or out_grad.shape[1] % 128:
+        return plain(out_grad, inputs, preact, w_out, w_in)
+    nz = n // 8
+    nl = nz // 2
+    me = lax.axis_index(AXIS)
+    z, y, x, c = coords(me)
+    at = jnp.stack([z, y, x, c, z // nl, z % nl]).astype(jnp.int32)
+    grad_scale = 1.0 / math.sqrt(out_grad.shape[0] * n)
+    tokens, width = out_grad.shape
+    hidden = preact.shape[1]
+    half = hidden // 2
+    size = half // 2
+
+    along_x = moved(n, lambda z, y, x, c: (z, y, 1 - x, c))
+    along_y = moved(n, lambda z, y, x, c: (z, 1 - y, x, c))
+
+    def send(array, perm):
+        return lax.ppermute(array, AXIS, perm)
+
+    def z_perm(k, swap=0):
+        return moved(n, lambda z, y, x, c: (z ^ k, y, x, c ^ swap))
+
+    def gather_perm(i, j):
+        return moved(
+            n, lambda z, y, x, c: ((c ^ i) * nl + ((z % nl) ^ j), y, x, z // nl)
+        )
+
+    def scatter_perm(i, j):
+        return moved(
+            n, lambda z, y, x, c: (c * nl + ((z % nl) ^ j), y, x, (z // nl) ^ i)
+        )
+
+    order = Order()
+
+    def kernel(body, arrays, outs, scratch=(), name=None, flops=0):
+        return order(small(body, at, arrays, outs, order.after, scratch, name, flops))
+
+    pre_got = send(preact, z_perm(0, 1))
+    grad_got = send(out_grad, z_perm(0, 1))
+    got = [send(w_out, gather_perm(i, j)) for i in range(2) for j in range(2)]
+    inputs_got = send(inputs, z_perm(0, 1))
+    in_got = send(w_in, z_perm(0, 1))
+
+    slopes, sent, kept = [None] * 2, [None] * 2, [None] * 2
+
+    def out_cut(cut):
+        s, o, k = out_total(at, cut, preact, pre_got, out_grad, grad_got, order.after)
+        order([o])
+        slopes[cut], kept[cut] = s, k
+        sent[cut] = send(o, (along_x, along_y)[cut])
+
+    def middle(k, r, next_perm, bit, dim):
+        dims = k.shape[:dim] + k.shape[dim + 1 :]
+
+        def body(at, k_ref, r_ref, out, keep):
+            b = at[bit]
+            spot = (slice(None),) * dim
+            out[...] = (k_ref[spot + (1 - b,)] + r_ref[spot + (1 - b,)].astype(F32)).astype(BF)
+            keep[...] = k_ref[spot + (b,)] + r_ref[spot + (b,)].astype(F32)
+
+        out, keep = kernel(body, [k, r], [shape(dims, BF), shape(dims, F32)], name=f"middle{dim}{bit}")
+        return keep, send(out, next_perm)
+
+    def join(one, one_got, two, two_got):
+        pair = shape((2,) + one.shape, BF)
+        return kernel(join_kernel, [one, one_got, two, two_got], [pair, pair])
+
+    order.after = [inputs_got]
+    out_cut(0)
+
+    (in_two,) = kernel(pair_kernel, [w_in, in_got], [shape((2, rows_in, half), BF)])
+    in_z = [send(in_two, z_perm(k)) for k in range(1, nz)]
+
+    rows = shape((2 * rows_out, width), BF)
+    one, two = kernel(rows_kernel, got, [rows, rows])
+    one_got, two_got = send(one, along_x), send(two, along_y)
+    out_cut(1)
+    ones, twos = join(one, one_got, two, two_got)
+    ones_got, twos_got = send(ones, along_y), send(twos, along_x)
+
+    out_sides = [middle(kept[0], sent[0], along_y, 1, 0), middle(kept[1], sent[1], along_x, 2, 0)]
+
+    spread = shape((nz, 2 * rows_in, size), BF)
+    one, two = kernel(columns_kernel, [in_two] + in_z, [spread, spread])
+    in_pieces = [one, send(one, along_x), two, send(two, along_y)]
+
+    pre_grads, in_sent, in_kept = [None] * 2, [None] * 2, [None] * 2
+
+    def in_cut(cut, pieces):
+        p, o, k = in_total(
+            at, cut, out_grad, grad_got, inputs, inputs_got, slopes[cut], pieces, nz, order.after
+        )
+        order([o])
+        pre_grads[cut], in_kept[cut] = p, k
+        in_sent[cut] = send(o, (along_x, along_y)[cut])
+
+    in_cut(0, [ones, ones_got])
+
+    def out_parts(at, k1, r1, k2, r2, o00, o01, o10, o11, own, total):
+        high, low = at[4], at[5]
+        total[0] = (k1[...] + r1[...].astype(F32)).reshape(2, rows_out, width)
+        total[1] = (k2[...] + r2[...].astype(F32)).reshape(2, rows_out, width)
+        own[...] = total[low, high]
+        o00[...] = total[low, high].astype(BF)
+        o01[...] = total[1 - low, high].astype(BF)
+        o10[...] = total[low, 1 - high].astype(BF)
+        o11[...] = total[1 - low, 1 - high].astype(BF)
+
+    row = (rows_out, width)
+    *out_got, out_own = kernel(
+        out_parts,
+        [*out_sides[0], *out_sides[1]],
+        [shape(row, BF)] * 4 + [shape(row, F32)],
+        [pltpu.VMEM((2, 2, rows_out, width), F32)],
+    )
+    out_got = [send(p, scatter_perm(*divmod(k, 2))) for k, p in enumerate(out_got)]
+
+    in_cut(1, [twos, twos_got])
+
+    def out_sum(at, own, r00, r01, r10, r11, out):
+        first = jnp.where(at[3] == at[4], own[...], r00[...].astype(F32))
+        rest = r01[...].astype(F32) + r10[...].astype(F32) + r11[...].astype(F32)
+        out[...] = (first + rest) * grad_scale
+
+    (w_out_grad,) = kernel(out_sum, [out_own] + out_got, [shape(out_own.shape, F32)])
+
+    order.after = order.after + [in_pieces[1], in_pieces[3]]
+    one, one_got = middle(in_kept[0], in_sent[0], along_y, 1, 1)
+    two, two_got = middle(in_kept[1], in_sent[1], along_x, 2, 1)
+
+    def in_parts(at, k1, r1, k2, r2, *outs):
+        z = at[0]
+        *outs, own, total = outs
+        total[:, :, :size] = k1[...] + r1[...].astype(F32)
+        total[:, :, size:] = k2[...] + r2[...].astype(F32)
+        own[...] = total[z]
+        for k in range(1, nz):
+            outs[k - 1][...] = total[z ^ k].astype(BF)
+
+    row = (2 * rows_in, half)
+    *in_got, in_own = kernel(
+        in_parts,
+        [one, one_got, two, two_got],
+        [shape(row, BF)] * (nz - 1) + [shape(row, F32)],
+        [pltpu.VMEM((nz, 2 * rows_in, half), F32)],
+    )
+    in_got = [send(p, z_perm(k)) for p, k in zip(in_got, range(1, nz))]
+
+    ones, twos = join(*in_pieces)
+    in_pieces = [ones, send(ones, along_y), twos, send(twos, along_x)]
+
+    part, part_other = input_part(at, pre_grads, in_pieces, nz, order.after)
+    order([part_other])
+    part_got = send(part_other, z_perm(0, 1))
+
+    def in_sum(at, own, r1, r2, r3, mine, other):
+        total = own[...] + r1[...].astype(F32) + r2[...].astype(F32) + r3[...].astype(F32)
+        total = total * grad_scale
+        first, second = total[:rows_in], total[rows_in:]
+        mine[...] = jnp.where(at[3] == 0, first, second)
+        other[...] = jnp.where(at[3] == 0, second, first)
+
+    row = shape((rows_in, half), F32)
+    mine, other = kernel(in_sum, [in_own] + in_got, [row, row], flops=10**11)
+    other = send(other, z_perm(0, 1))
+
+    def input_sum(at, mine, other, out):
+        out[...] = mine[...] + other[...]
+
+    (input_grad,) = kernel(input_sum, [part, part_got], [shape((tokens, width), F32)])
+
+    return (input_grad, w_out_grad, w_in_grad)
+
+
+MIB = 1 << 20
+ANY = pl.BlockSpec(memory_space=pl.ANY)
+VMEM = pl.BlockSpec(memory_space=pltpu.VMEM)
+SMEM = pl.BlockSpec(memory_space=pltpu.SMEM)
+
+
+def shape(dims, kind):
+    return jax.ShapeDtypeStruct(dims, kind)
+
+
+class Order:
+    def __init__(self):
+        self.after = []
+
+    def __call__(self, outs):
+        self.after = [outs[0]]
+        return outs
+
+
+def small(body, where, arrays, outs, after=(), scratch=(), name=None, flops=0):
+    skipped = len(after)
+
+    def run(*refs):
+        body(*refs[: 1 + len(arrays)], *refs[1 + len(arrays) + skipped :])
+
+    moved_bytes = sum(a.size * a.dtype.itemsize for a in list(arrays) + list(outs))
+    return pl.pallas_call(
+        run,
+        name=name or body.__name__,
+        out_shape=outs,
+        in_specs=[SMEM] + [VMEM] * len(arrays) + [ANY] * skipped,
+        out_specs=[VMEM] * len(outs),
+        scratch_shapes=list(scratch),
+        compiler_params=pltpu.CompilerParams(vmem_limit_bytes=16 * MIB),
+        cost_estimate=pl.CostEstimate(
+            flops=flops, bytes_accessed=moved_bytes, transcendentals=0
+        ),
+    )(where, *arrays, *after)
+
+
+def pair_kernel(at, in_ref, got_ref, out):
+    c = at[3]
+    size = out.shape[2]
+    out[c] = jnp.where(c == 0, in_ref[:, :size], in_ref[:, size:])
+    out[1 - c] = jnp.where(c == 0, got_ref[:, :size], got_ref[:, size:])
+
+
+def join_kernel(at, own1, got1, own2, got2, one, two):
+    x, y = at[2], at[1]
+    one[x] = own1[...]
+    one[1 - x] = got1[...]
+    two[y] = own2[...]
+    two[1 - y] = got2[...]
+
+
+def rows_kernel(at, g00, g01, g10, g11, one, two):
+    high, low = at[4], at[5]
+    rows = g00.shape[0]
+    for cc in range(2):
+        from_same = jnp.where(high == cc, g00[...], g10[...])
+        from_next = jnp.where(high == cc, g01[...], g11[...])
+        part = pl.ds(cc * rows, rows)
+        one[part, :] = jnp.where(low == 0, from_same, from_next)
+        two[part, :] = jnp.where(low == 0, from_next, from_same)
+
+
+def columns_kernel(at, mine, g1, g2, g3, one, two):
+    z = at[0]
+    rows, size = mine.shape[0] * mine.shape[1], one.shape[2]
+    for k, got in enumerate((mine, g1, g2, g3)):
+        value = got[...].reshape(rows, 2 * size)
+        one[z ^ k] = value[:, :size]
+        two[z ^ k] = value[:, size:]
+
+
+def out_total(at, cut, pre, pre_got, grad, grad_got, after):
+    tokens, width = grad.shape
+    size = pre_got.shape[1] // 8
+    rows = size // 2
+
+    def body(at, pre_ref, got_ref, grad_ref, grad2_ref, *refs):
+        slope, send, keep, total = refs[-4:]
+        t = pl.program_id(0)
+        x, y = at[2], at[1]
+        activ, slope1 = gelu_parts(pre_ref[...])
+        slope[pl.ds(0, tokens), :] = slope1
+        value = contract_first(activ, grad_ref[...])
+        activ, slope2 = gelu_parts(got_ref[...])
+        slope[pl.ds(tokens, tokens), :] = slope2
+        value = value + contract_first(activ, grad2_ref[...])
+        if cut == 0:
+            total[...] = value.reshape(2, rows, width)
+            send[0] = total[1 - x].astype(BF)
+            keep[0] = total[x]
+        else:
+
+            @pl.when(t == y)
+            def _():
+                keep[...] = value.reshape(2, rows, width)
+
+            @pl.when(t != y)
+            def _():
+                send[...] = value.astype(BF).reshape(2, rows, width)
+
+    whole = lambda t, at: (0, 0)
+    if cut == 0:
+        parts = pl.BlockSpec((1, rows, width), lambda t, at: (t, 0, 0))
+    else:
+        parts = pl.BlockSpec((2, rows, width), lambda t, at: (0, 0, 0))
+    return pl.pallas_call(
+        body,
+        name=f"out_total{cut}",
+        grid_spec=pltpu.PrefetchScalarGridSpec(
+            num_scalar_prefetch=1,
+            grid=(2,),
+            in_specs=[
+                pl.BlockSpec((tokens, size), lambda t, at: (0, at[3] * 4 + cut * 2 + t)),
+                pl.BlockSpec((tokens, size), lambda t, at: (0, at[3] * 4 + cut * 2 + t)),
+                pl.BlockSpec((tokens, width), whole),
+                pl.BlockSpec((tokens, width), whole),
+            ]
+            + [ANY] * len(after),
+            out_specs=[
+                pl.BlockSpec((2 * tokens, size), lambda t, at: (0, t)),
+                parts,
+                parts,
+            ],
+            scratch_shapes=[pltpu.VMEM((2, rows, width), F32)],
+        ),
+        out_shape=[
+            shape((2 * tokens, 2 * size), F32),
+            shape((2, rows, width), BF),
+            shape((2, rows, width), F32),
+        ],
+        compiler_params=pltpu.CompilerParams(vmem_limit_bytes=24 * MIB),
+        cost_estimate=pl.CostEstimate(
+            flops=8 * tokens * size * width,
+            bytes_accessed=20 * MIB,
+            transcendentals=4 * tokens * size,
+        ),
+    )(at, pre, pre_got, grad, grad_got, *after)
+
+
+def in_total(at, cut, grad, grad_got, inputs, inputs_got, slope, pieces, nz, after):
+    tokens, width = grad.shape
+    size = slope.shape[1] // 2
+    rows = size // 2
+    depth = width // (4 * nz)
+
+    def body(at, grad_ref, grad2_ref, in_ref, in2_ref, slope_ref, mine, other, _, pre_grad, send, keep):
+        t = pl.program_id(0)
+        x, y = at[2], at[1]
+        if cut == 0:
+            value = jnp.where(t == y, mine[...], other[...]).reshape(size, width)
+        else:
+            first, second = mine[t], other[t]
+            value = jnp.concatenate(
+                [jnp.where(x == 0, first, second), jnp.where(x == 0, second, first)], 0
+            )
+        totals = 0.0
+        for part, (g, i) in enumerate(((grad_ref, in_ref), (grad2_ref, in2_ref))):
+            at_rows = pl.ds(part * tokens, tokens)
+            act_grad = contract_last(g[...], value)
+            pre = (act_grad * slope_ref[at_rows, :]).astype(BF)
+            pre_grad[at_rows, :] = pre
+            totals = totals + contract_first(i[...], pre)
+        parts = totals.reshape(nz, 2, 2, depth, size)
+        if cut == 0:
+            first, second, bit = parts[:, :, 0], parts[:, :, 1], x
+        else:
+            first, second, bit = parts[:, 0], parts[:, 1], y
+        send[...] = jnp.where(bit == 0, second, first).astype(BF)
+        keep[...] = jnp.where(bit == 0, first, second)
+
+    whole = lambda t, at: (0, 0)
+    tile = lambda t, at: (0, t)
+    piece = pl.BlockSpec((2, rows, width), lambda t, at: (0, 0, 0))
+    parts = pl.BlockSpec((nz, 2, depth, size), lambda t, at: (0, 0, 0, t))
+    return pl.pallas_call(
+        body,
+        name=f"in_total{cut}",
+        grid_spec=pltpu.PrefetchScalarGridSpec(
+            num_scalar_prefetch=1,
+            grid=(2,),
+            in_specs=[pl.BlockSpec((tokens, width), whole)] * 4
+            + [pl.BlockSpec((2 * tokens, size), tile)]
+            + [piece] * 2
+            + [ANY],
+            out_specs=[pl.BlockSpec((2 * tokens, size), tile), parts, parts],
+        ),
+        out_shape=[
+            shape((2 * tokens, 2 * size), BF),
+            shape((nz, 2, depth, 2 * size), BF),
+            shape((nz, 2, depth, 2 * size), F32),
+        ],
+        compiler_params=pltpu.CompilerParams(vmem_limit_bytes=24 * MIB),
+        cost_estimate=pl.CostEstimate(
+            flops=16 * tokens * size * width, bytes_accessed=16 * MIB, transcendentals=0
+        ),
+    )(at, grad, grad_got, inputs, inputs_got, slope, *pieces, *after)
+
+
+def input_part(at, pre_grads, pieces, nz, after):
+    tokens, size = pre_grads[0].shape[0] // 2, pre_grads[0].shape[1]
+    depth = pieces[0].shape[2]
+    width = 4 * nz * depth
+
+    def body(at, g0, g1, a0, a1, b0, b1, _, mine, other, weight0, weight1):
+        t = pl.program_id(0)
+        x, y = at[2], at[1]
+
+        @pl.when(t == 0)
+        def _():
+            for k in range(2):
+                weight0[:, y, k] = a0[k]
+                weight0[:, 1 - y, k] = a1[k]
+                weight1[:, k, x] = b0[k]
+                weight1[:, k, 1 - x] = b1[k]
+
+        value = contract_last(g0[...], weight0[...].reshape(width, size))
+        value = value + contract_last(g1[...], weight1[...].reshape(width, size))
+
+        @pl.when(t == 0)
+        def _():
+            other[...] = value
+
+        @pl.when(t == 1)
+        def _():
+            mine[...] = value
+
+    piece = pl.BlockSpec((2, nz, depth, size), lambda t, at: (0, 0, 0, 0))
+    rows = pl.BlockSpec((tokens, size), lambda t, at: (1 - t, 0))
+    out = pl.BlockSpec((tokens, width), lambda t, at: (0, 0))
+    return pl.pallas_call(
+        body,
+        name="input_part",
+        grid_spec=pltpu.PrefetchScalarGridSpec(
+            num_scalar_prefetch=1,
+            grid=(2,),
+            in_specs=[rows] * 2 + [piece] * 4 + [ANY],
+            out_specs=[out, out],
+            scratch_shapes=[pltpu.VMEM((nz, 2, 2, depth, size), BF)] * 2,
+        ),
+        out_shape=[shape((tokens, width), F32)] * 2,
+        compiler_params=pltpu.CompilerParams(vmem_limit_bytes=24 * MIB),
+        cost_estimate=pl.CostEstimate(
+            flops=8 * tokens * size * width, bytes_accessed=10 * MIB, transcendentals=0
+        ),
+    )(at, *pre_grads, *pieces, *after)
+
+
+def per_device(out_grad, inputs, preact, w_out, w_in):
+    n = lax.axis_size(AXIS)
+    rows_out, rows_in = w_out.shape[0], w_in.shape[0]
+    if n != 32 or rows_out % 16 or (2 * rows_in) % 16 or out_grad.shape[1] % 128:
+        return plain(out_grad, inputs, preact, w_out, w_in)
+    nz = n // 8
+    nl = nz // 2
+    me = lax.axis_index(AXIS)
+    z, y, x, c = coords(me)
+    at = jnp.stack([z, y, x, c, z // nl, z % nl]).astype(jnp.int32)
+    grad_scale = 1.0 / math.sqrt(out_grad.shape[0] * n)
+    tokens, width = out_grad.shape
+    hidden = preact.shape[1]
+    half = hidden // 2
+    size = half // 2
+
+    along_x = moved(n, lambda z, y, x, c: (z, y, 1 - x, c))
+    along_y = moved(n, lambda z, y, x, c: (z, 1 - y, x, c))
+
+    def send(array, perm):
+        return lax.ppermute(array, AXIS, perm)
+
+    def z_perm(k, swap=0):
+        return moved(n, lambda z, y, x, c: (z ^ k, y, x, c ^ swap))
+
+    def gather_perm(i, j):
+        return moved(
+            n, lambda z, y, x, c: ((c ^ i) * nl + ((z % nl) ^ j), y, x, z // nl)
+        )
+
+    def scatter_perm(i, j):
+        return moved(
+            n, lambda z, y, x, c: (c * nl + ((z % nl) ^ j), y, x, (z // nl) ^ i)
+        )
+
+    order = Order()
+
+    def kernel(body, arrays, outs, scratch=(), name=None, flops=0):
+        return order(small(body, at, arrays, outs, order.after, scratch, name, flops))
+
+    pre_got = send(preact, z_perm(0, 1))
+    grad_got = send(out_grad, z_perm(0, 1))
+    got = [send(w_out, gather_perm(i, j)) for i in range(2) for j in range(2)]
+    inputs_got = send(inputs, z_perm(0, 1))
+    in_got = send(w_in, z_perm(0, 1))
+
+    slopes, sent, kept = [None] * 2, [None] * 2, [None] * 2
+
+    def out_cut(cut):
+        s, o, k = out_total(at, cut, preact, pre_got, out_grad, grad_got, order.after)
+        order([o])
+        slopes[cut], kept[cut] = s, k
+        sent[cut] = send(o, (along_x, along_y)[cut])
+
+    def middle(k, r, next_perm, bit, dim):
+        dims = k.shape[:dim] + k.shape[dim + 1 :]
+
+        def body(at, k_ref, r_ref, out, keep):
+            b = at[bit]
+            spot = (slice(None),) * dim
+            out[...] = (k_ref[spot + (1 - b,)] + r_ref[spot + (1 - b,)].astype(F32)).astype(BF)
+            keep[...] = k_ref[spot + (b,)] + r_ref[spot + (b,)].astype(F32)
+
+        out, keep = kernel(body, [k, r], [shape(dims, BF), shape(dims, F32)], name=f"middle{dim}{bit}")
+        return keep, send(out, next_perm)
+
+    def join(one, one_got, two, two_got):
+        pair = shape((2,) + one.shape, BF)
+        return kernel(join_kernel, [one, one_got, two, two_got], [pair, pair])
+
+    order.after = [inputs_got]
+    out_cut(0)
+
+    (in_two,) = kernel(pair_kernel, [w_in, in_got], [shape((2, rows_in, half), BF)])
+    in_z = [send(in_two, z_perm(k)) for k in range(1, nz)]
+
+    rows = shape((2 * rows_out, width), BF)
+    one, two = kernel(rows_kernel, got, [rows, rows])
+    one_got, two_got = send(one, along_x), send(two, along_y)
+    out_cut(1)
+    ones, twos = join(one, one_got, two, two_got)
+    ones_got, twos_got = send(ones, along_y), send(twos, along_x)
+
+    out_sides = [middle(kept[0], sent[0], along_y, 1, 0), middle(kept[1], sent[1], along_x, 2, 0)]
+
+    spread = shape((nz, 2 * rows_in, size), BF)
+    one, two = kernel(columns_kernel, [in_two] + in_z, [spread, spread])
+    in_pieces = [one, send(one, along_x), two, send(two, along_y)]
+
+    pre_grads, in_sent, in_kept = [None] * 2, [None] * 2, [None] * 2
+
+    def in_cut(cut, pieces):
+        p, o, k = in_total(
+            at, cut, out_grad, grad_got, inputs, inputs_got, slopes[cut], pieces, nz, order.after
+        )
+        order([o])
+        pre_grads[cut], in_kept[cut] = p, k
+        in_sent[cut] = send(o, (along_x, along_y)[cut])
+
+    in_cut(0, [ones, ones_got])
+
+    def out_parts(at, k1, r1, k2, r2, o00, o01, o10, o11, own, total):
+        high, low = at[4], at[5]
+        total[0] = (k1[...] + r1[...].astype(F32)).reshape(2, rows_out, width)
+        total[1] = (k2[...] + r2[...].astype(F32)).reshape(2, rows_out, width)
+        own[...] = total[low, high]
+        o00[...] = total[low, high].astype(BF)
+        o01[...] = total[1 - low, high].astype(BF)
+        o10[...] = total[low, 1 - high].astype(BF)
+        o11[...] = total[1 - low, 1 - high].astype(BF)
+
+    row = (rows_out, width)
+    *out_got, out_own = kernel(
+        out_parts,
+        [*out_sides[0], *out_sides[1]],
+        [shape(row, BF)] * 4 + [shape(row, F32)],
+        [pltpu.VMEM((2, 2, rows_out, width), F32)],
+    )
+    out_got = [send(p, scatter_perm(*divmod(k, 2))) for k, p in enumerate(out_got)]
+
+    in_cut(1, [twos, twos_got])
+
+    def out_sum(at, own, r00, r01, r10, r11, out):
+        first = jnp.where(at[3] == at[4], own[...], r00[...].astype(F32))
+        rest = r01[...].astype(F32) + r10[...].astype(F32) + r11[...].astype(F32)
+        out[...] = (first + rest) * grad_scale
+
+    (w_out_grad,) = kernel(out_sum, [out_own] + out_got, [shape(out_own.shape, F32)])
+
+    order.after = order.after + [in_pieces[1], in_pieces[3]]
+    one, one_got = middle(in_kept[0], in_sent[0], along_y, 1, 1)
+    two, two_got = middle(in_kept[1], in_sent[1], along_x, 2, 1)
+
+    def in_parts(at, k1, r1, k2, r2, *outs):
+        z = at[0]
+        *outs, own, total = outs
+        total[:, :, :size] = k1[...] + r1[...].astype(F32)
+        total[:, :, size:] = k2[...] + r2[...].astype(F32)
+        own[...] = total[z]
+        for k in range(1, nz):
+            outs[k - 1][...] = total[z ^ k].astype(BF)
+
+    row = (2 * rows_in, half)
+    *in_got, in_own = kernel(
+        in_parts,
+        [one, one_got, two, two_got],
+        [shape(row, BF)] * (nz - 1) + [shape(row, F32)],
+        [pltpu.VMEM((nz, 2 * rows_in, half), F32)],
+    )
+    in_got = [send(p, z_perm(k)) for p, k in zip(in_got, range(1, nz))]
+
+    ones, twos = join(*in_pieces)
+    in_pieces = [ones, send(ones, along_y), twos, send(twos, along_x)]
+
+    part, part_other = input_part(at, pre_grads, in_pieces, nz, order.after)
+    order([part_other])
+    part_got = send(part_other, z_perm(0, 1))
+
+    def in_sum(at, own, r1, r2, r3, mine, other):
+        total = own[...] + r1[...].astype(F32) + r2[...].astype(F32) + r3[...].astype(F32)
+        total = total * grad_scale
+        first, second = total[:rows_in], total[rows_in:]
+        mine[...] = jnp.where(at[3] == 0, first, second)
+        other[...] = jnp.where(at[3] == 0, second, first)
+
+    row = shape((rows_in, half), F32)
+    mine, other = kernel(in_sum, [in_own] + in_got, [row, row], flops=10**11)
+    other = send(other, z_perm(0, 1))
+
+    def input_sum(at, mine, other, out):
+        out[...] = mine[...] + other[...]
+
+    (input_grad,) = kernel(input_sum, [part, part_got], [shape((tokens, width), F32)])
+
+    def in_join(at, mine, other, out):
+        c = at[3]
+        out[:, :half] = jnp.where(c == 0, mine[...], other[...])
+        out[:, half:] = jnp.where(c == 0, other[...], mine[...])
+
+    (w_in_grad,) = kernel(in_join, [mine, other], [shape((rows_in, hidden), F32)])
+    return (input_grad, w_out_grad, w_in_grad)
+
+
 def solution(mesh):
     in_specs = (
         P(("grp", "gx"), None),

time: 187 us -> 138 us (0.74)
  waiting for transfers between devices: 86.4 us -> 40.6 us
  Pallas kernels: 0 us -> 34.6 us
  matrix products: 15.4 us -> 0 us
  local copies, waits for them, and re-layouts: 24.1 us -> 9.56 us
  other arithmetic: 6.94 us -> 0 us
    ppermute x36, waiting for transfers between devices: 86.4 us -> 40.6 us  [send(): return lax.ppermute(array, AXIS, perm)]
    pallas_call x0 -> x20, Pallas kernels: none -> 34.6 us  [the longest x15 12.7 us: small(): pl.pallas_call(run, name=name or body.__name__, out_shape=outs, in_specs=...]
    dot_general x4 -> x0, matrix products: 15.4 us -> none  [the longest x2 8.81 us: contract_last(): lax.dot_general(left, right, (((1,), (1,)), ((), ())), preferred_element_...]
    reshape x3 -> x0, local copies, waits for them, and re-layouts: 8.8 us -> none  [the longest x1 7.06 us: per_device(): pre_split = preact.reshape(tokens, 2, half)]
    dynamic_slice x3 -> x0, local copies, waits for them, and re-layouts: 8.47 us -> none  [the longest x2 8.42 us: pick(): return lax.dynamic_index_in_dim(array, at, axis, keepdims=False)]
    unnamed x6 -> x26, local copies, waits for them, and re-layouts: 3.76 us -> 9.48 us
    another operation x22 -> x0, other arithmetic: 3.43 us -> none  [the longest x14 1.79 us: paired(): return jnp.stack([first, second], axis)]
    add x9 -> x0, other arithmetic: 2 us -> none  [the longest x1 1.33 us: per_device(): input_grad = part[:tokens] + send(part[tokens:], cores)]
  transfers between devices with their start and end apart: 36 -> 36, of which waited for: 16 -> 13; matrix products, arithmetic and copies ran while one was open for 24% -> 0% of each run, Pallas kernels for 0% -> 23%
where the time goes in v2:
time: 138 us; the launch traced here: 136 us
  starting transfers between devices  50.5 us (37%)
  waiting for transfers between devices  40.6 us (29%)
  Pallas kernels  34.6 us (25%)
  local copies, waits for them, and re-layouts  9.56 us (7%)
    ppermute x36, starting transfers between devices, send(): return lax.ppermute(array, AXIS, perm)  50.5 us
    ppermute x36, waiting for transfers between devices, send(): return lax.ppermute(array, AXIS, perm)  40.6 us
    pallas_call x15, Pallas kernels, small(): pl.pallas_call(run, name=name or body.__name__, out_shape=outs, in_specs=...  12.7 us
    pallas_call x2, Pallas kernels, in_total(): pl.pallas_call(body, name=f'in_total{cut}', grid_spec=pltpu.PrefetchScala...  9.63 us
    unnamed x26, local copies, waits for them, and re-layouts  9.48 us
    pallas_call x2, Pallas kernels, out_total(): pl.pallas_call(body, name=f'out_total{cut}', grid_spec=pltpu.PrefetchScal...  8.51 us
    pallas_call x1, Pallas kernels, input_part(): pl.pallas_call(body, name='input_part', grid_spec=pltpu.PrefetchScalarGri...  3.71 us
  transfers between devices with their start and end apart: 36, of which 13 were waited for; matrix products, arithmetic and copies ran while one was open for 0% of the time, Pallas kernels for 23%

profile of v2, /device:TPU:1, one launch (start us, length us, event | category | flops | bytes accessed | tf_op | source)
XLA Modules:
  0.0 136.2 jit_solution(1127292296170201917)
XLA Ops:
  1.7 5.6 %collective-permute-start.3 = (bf16[96,768]{1,0:T(8,128)(2,1)}, bf16[96,768]{1,0:T(8,128)(2,1)S(1)}, u32[]{:S(2)}, u32[]{:S(2)}) collective-permute-start(bf16[96,768]{1,0:T(8,128)(2,1)} %param.8), channel_id=1, source_target_pairs={{0,0},{1,16},{2,2},{3,18},{4,4},{5,20},{6,6},{7,22},{8,8},{9,24},{... | collective-permute-start | bytes 442376 | tf_op jit(solution)/shard_map/ppermute | solution.py:866
  8.6 4.7 %collective-permute-start.4 = (bf16[96,768]{1,0:T(8,128)(2,1)}, bf16[96,768]{1,0:T(8,128)(2,1)}, u32[]{:S(2)}, u32[]{:S(2)}) collective-permute-start(bf16[96,768]{1,0:T(8,128)(2,1)} %param.8), channel_id=1, source_target_pairs={{0,8},{1,24},{2,10},{3,26},{4,12},{5,28},{6,14},{7,30},{8,0},{9,16... | collective-permute-start | bytes 442376 | tf_op jit(solution)/shard_map/ppermute | solution.py:866
  15.1 1.9 %copy-done = bf16[512,3072]{1,0:T(8,128)(2,1)S(1)} copy-done((bf16[512,3072]{1,0:T(8,128)(2,1)S(1)}, bf16[512,3072]{1,0:T(8,128)(2,1)}, u32[]{:S(2)}) %copy-start) | copy-done | bytes 3145752
  20.4 4.3 %out_total0.1 = (f32[1024,768]{1,0:T(8,128)S(1)}, bf16[2,192,768]{2,1,0:T(8,128)(2,1)S(1)}, f32[2,192,768]{2,1,0:T(8,128)S(1)}) custom-call(s32[6]{0:T(128)S(1)} %stack.27.at.refs_0_, bf16[512,3072]{1,0:T(8,128)(2,1)S(1)} %copy-done, bf16[512,3072]{1,0:T(8,128)(2,1)S(1)} %collective-permute-done.2.got_ref, bf16[512,768]{1,0:T(8,128)(2,1)S(1)} %copy-done.2, ...), custom_call_target="tpu_custom_call" | custom-call | flops 1207959552 | bytes 20971520 | tf_op jit(solution)/shard_map/out_total0/pallas_call | solution.py:704
  29.2 4.2 %out_total1.1 = (f32[1024,768]{1,0:T(8,128)S(1)}, bf16[2,192,768]{2,1,0:T(8,128)(2,1)S(1)}, f32[2,192,768]{2,1,0:T(8,128)S(1)}) custom-call(s32[6]{0:T(128)S(1)} %stack.27.at.refs_0_, bf16[512,3072]{1,0:T(8,128)(2,1)S(1)} %copy-done, bf16[512,3072]{1,0:T(8,128)(2,1)S(1)} %collective-permute-done.2.got_ref, bf16[512,768]{1,0:T(8,128)(2,1)S(1)} %copy-done.2, ...), custom_call_target="tpu_custom_call" | custom-call | flops 1207959552 | bytes 20971520 | tf_op jit(solution)/shard_map/out_total1/pallas_call | solution.py:704
  33.8 1.4 %collective-permute-done.8.refs_2_ = bf16[192,768]{1,0:T(8,128)(2,1)S(1)} collective-permute-done((bf16[192,768]{1,0:T(8,128)(2,1)S(1)}, bf16[192,768]{1,0:T(8,128)(2,1)S(1)}, u32[]{:S(2)}, u32[]{:S(2)}) %collective-permute-start.8) | collective-permute-done | bytes 294944 | tf_op jit(solution)/shard_map/ppermute | solution.py:866
  38.4 9.5 %collective-permute-done.15.refs_2_ = bf16[2,192,768]{2,1,0:T(8,128)(2,1)S(1)} collective-permute-done((bf16[2,192,768]{2,1,0:T(8,128)(2,1)S(1)}, bf16[2,192,768]{2,1,0:T(8,128)(2,1)S(1)}, u32[]{:S(2)}, u32[]{:S(2)}) %collective-permute-start.15) | collective-permute-done | bytes 589856 | tf_op jit(solution)/shard_map/ppermute | solution.py:866
  47.8 1.8 %collective-permute-start.12 = (bf16[2,24,1536]{2,1,0:T(8,128)(2,1)S(1)}, bf16[2,24,1536]{2,1,0:T(8,128)(2,1)S(1)}, u32[]{:S(2)}, u32[]{:S(2)}) collective-permute-start(bf16[2,24,1536]{2,1,0:T(8,128)(2,1)S(1)} %pair_kernel.1.refs_5_.refs_1_), channel_id=1, source_target_pairs={{0,16},{1,17},{2,18},{3,19},{4,20},{5,21},{6,22},{7,23},{8,24},{9,... | collective-permute-start | bytes 442376 | tf_op jit(solution)/shard_map/ppermute | solution.py:866
  52.5 7.8 %collective-permute-done.12.refs_3_ = bf16[2,24,1536]{2,1,0:T(8,128)(2,1)S(1)} collective-permute-done((bf16[2,24,1536]{2,1,0:T(8,128)(2,1)S(1)}, bf16[2,24,1536]{2,1,0:T(8,128)(2,1)S(1)}, u32[]{:S(2)}, u32[]{:S(2)}) %collective-permute-start.12) | collective-permute-done | bytes 147488 | tf_op jit(solution)/shard_map/ppermute | solution.py:866
  62.2 4.8 %in_total0.1 = (bf16[1024,768]{1,0:T(8,128)(2,1)S(1)}, bf16[4,2,48,768]{3,2,1,0:T(8,128)(2,1)S(1)}, f32[4,2,48,768]{3,2,1,0:T(8,128)S(1)}) custom-call(s32[6]{0:T(128)S(1)} %stack.27.at.refs_0_, bf16[512,768]{1,0:T(8,128)(2,1)S(1)} %copy-done.3, bf16[512,768]{1,0:T(8,128)(2,1)S(1)} %copy-done.6, bf16[512,768]{1,0:T(8,128)(2,1)S(1)} %copy-done.12, ...), custom_call_target="tpu_custom_call" | custom-call | flops 2415919104 | bytes 16777216 | tf_op jit(solution)/shard_map/in_total0/pallas_call | solution.py:773
  69.1 4.8 %in_total1.1 = (bf16[1024,768]{1,0:T(8,128)(2,1)S(1)}, bf16[4,2,48,768]{3,2,1,0:T(8,128)(2,1)S(1)}, f32[4,2,48,768]{3,2,1,0:T(8,128)S(1)}) custom-call(s32[6]{0:T(128)S(1)} %stack.27.at.refs_0_, bf16[512,768]{1,0:T(8,128)(2,1)S(1)} %copy-done.3, bf16[512,768]{1,0:T(8,128)(2,1)S(1)} %copy-done.6, bf16[512,768]{1,0:T(8,128)(2,1)S(1)} %copy-done.12, ...), custom_call_target="tpu_custom_call" | custom-call | flops 2415919104 | bytes 16777216 | tf_op jit(solution)/shard_map/in_total1/pallas_call | solution.py:773
  74.8 6.5 %collective-permute-start.22 = (bf16[96,768]{1,0:T(8,128)(2,1)S(1)}, bf16[96,768]{1,0:T(8,128)(2,1)S(1)}, u32[]{:S(2)}, u32[]{:S(2)}) collective-permute-start(bf16[96,768]{1,0:T(8,128)(2,1)S(1)} %get-tuple-element.61._), channel_id=1, source_target_pairs={{0,0},{1,16},{2,2},{3,18},{4,4},{5,20},{6,6},{7,22},{8,8},{9,24},{... | collective-permute-start | bytes 442376 | tf_op jit(solution)/shard_map/ppermute | solution.py:866
  81.7 3.9 %collective-permute-done.22.refs_2_ = bf16[96,768]{1,0:T(8,128)(2,1)S(1)} collective-permute-done((bf16[96,768]{1,0:T(8,128)(2,1)S(1)}, bf16[96,768]{1,0:T(8,128)(2,1)S(1)}, u32[]{:S(2)}, u32[]{:S(2)}) %collective-permute-start.22) | collective-permute-done | bytes 147488 | tf_op jit(solution)/shard_map/ppermute | solution.py:866
  85.9 1.9 %collective-permute-done.23.refs_3_ = bf16[96,768]{1,0:T(8,128)(2,1)S(1)} collective-permute-done((bf16[96,768]{1,0:T(8,128)(2,1)S(1)}, bf16[96,768]{1,0:T(8,128)(2,1)S(1)}, u32[]{:S(2)}, u32[]{:S(2)}) %collective-permute-start.23) | collective-permute-done | bytes 147488 | tf_op jit(solution)/shard_map/ppermute | solution.py:866
  88.0 5.4 %collective-permute-start.25 = (bf16[96,768]{1,0:T(8,128)(2,1)S(1)}, bf16[96,768]{1,0:T(8,128)(2,1)S(1)}, u32[]{:S(2)}, u32[]{:S(2)}) collective-permute-start(bf16[96,768]{1,0:T(8,128)(2,1)S(1)} %get-tuple-element.68), channel_id=1, source_target_pairs={{0,9},{1,25},{2,11},{3,27},{4,13},{5,29},{6,15},{7,31},{8,1},{9,17... | collective-permute-start | bytes 442376 | tf_op jit(solution)/shard_map/ppermute | solution.py:866
  93.4 3.1 %collective-permute-done.25.refs_5_ = bf16[96,768]{1,0:T(8,128)(2,1)S(1)} collective-permute-done((bf16[96,768]{1,0:T(8,128)(2,1)S(1)}, bf16[96,768]{1,0:T(8,128)(2,1)S(1)}, u32[]{:S(2)}, u32[]{:S(2)}) %collective-permute-start.25) | collective-permute-done | bytes 147488 | tf_op jit(solution)/shard_map/ppermute | solution.py:866
  100.8 4.4 %collective-permute-done.26.refs_2_ = bf16[4,48,768]{2,1,0:T(8,128)(2,1)S(1)} collective-permute-done((bf16[4,48,768]{2,1,0:T(8,128)(2,1)S(1)}, bf16[4,48,768]{2,1,0:T(8,128)(2,1)S(1)}, u32[]{:S(2)}, u32[]{:S(2)}) %collective-permute-start.26) | collective-permute-done | bytes 294944 | tf_op jit(solution)/shard_map/ppermute | solution.py:866
  109.3 4.1 %collective-permute-start.32 = (bf16[48,1536]{1,0:T(8,128)(2,1)S(1)}, bf16[48,1536]{1,0:T(8,128)(2,1)S(1)}, u32[]{:S(2)}, u32[]{:S(2)}) collective-permute-start(bf16[48,1536]{1,0:T(8,128)(2,1)S(1)} %get-tuple-element.75.refs_5_), channel_id=1, source_target_pairs={{0,8},{1,9},{2,10},{3,11},{4,12},{5,13},{6,14},{7,15},{8,0},{9,1},... | collective-permute-start | bytes 442376 | tf_op jit(solution)/shard_map/ppermute | solution.py:866
  113.4 2.2 %collective-permute-start.33 = (bf16[48,1536]{1,0:T(8,128)(2,1)S(1)}, bf16[48,1536]{1,0:T(8,128)(2,1)S(1)}, u32[]{:S(2)}, u32[]{:S(2)}) collective-permute-start(bf16[48,1536]{1,0:T(8,128)(2,1)S(1)} %get-tuple-element.81), channel_id=1, source_target_pairs={{0,16},{1,17},{2,18},{3,19},{4,20},{5,21},{6,22},{7,23},{8,24},{9,... | collective-permute-start | bytes 442376 | tf_op jit(solution)/shard_map/ppermute | solution.py:866
  115.6 2.9 %collective-permute-done.29.a1 = bf16[2,4,48,768]{3,2,1,0:T(8,128)(2,1)S(1)} collective-permute-done((bf16[2,4,48,768]{3,2,1,0:T(8,128)(2,1)S(1)}, bf16[2,4,48,768]{3,2,1,0:T(8,128)(2,1)S(1)}, u32[]{:S(2)}, u32[]{:S(2)}) %collective-permute-start.29) | collective-permute-done | bytes 589856 | tf_op jit(solution)/shard_map/ppermute | solution.py:866
  119.4 3.7 %input_part.1 = (f32[512,768]{1,0:T(8,128)S(1)}, f32[512,768]{1,0:T(8,128)S(1)}) custom-call(s32[6]{0:T(128)S(1)} %stack.27.at.refs_0_, bf16[1024,768]{1,0:T(8,128)(2,1)S(1)} %get-tuple-element.55.g0, bf16[1024,768]{1,0:T(8,128)(2,1)S(1)} %get-tuple-element.62.g1, bf16[2,4,48,768]{3,2,1,0:T(8,128)(2,1)S(1)} %get-tuple-element.76.a0._, ...), custom_call_target="tpu_custom_call" | custom-call | flops 2415919104 | bytes 10485760 | tf_op jit(solution)/shard_map/input_part/pallas_call | solution.py:828
  123.1 5.5 %collective-permute-start.31 = (f32[512,768]{1,0:T(8,128)S(1)}, f32[512,768]{1,0:T(8,128)S(1)}, u32[]{:S(2)}, u32[]{:S(2)}) collective-permute-start(f32[512,768]{1,0:T(8,128)S(1)} %get-tuple-element.79.refs_5_), channel_id=1, source_target_pairs={{0,1},{1,0},{2,3},{3,2},{4,5},{5,4},{6,7},{7,6},{8,9},{9,8},{10,11... | collective-permute-start | bytes 4718600 | tf_op jit(solution)/shard_map/ppermute | solution.py:866
  129.3 2.3 %collective-permute-done.31.refs_2_ = f32[512,768]{1,0:T(8,128)S(1)} collective-permute-done((f32[512,768]{1,0:T(8,128)S(1)}, f32[512,768]{1,0:T(8,128)S(1)}, u32[]{:S(2)}, u32[]{:S(2)}) %collective-permute-start.31) | collective-permute-done | bytes 1572896 | tf_op jit(solution)/shard_map/ppermute | solution.py:866
  131.6 1.8 %input_sum.1.refs_3_ = f32[512,768]{1,0:T(8,128)} custom-call(s32[6]{0:T(128)S(1)} %stack.27.at.refs_0_, f32[512,768]{1,0:T(8,128)S(1)} %get-tuple-element.78.refs_1_, f32[512,768]{1,0:T(8,128)S(1)} %collective-permute-done.31.refs_2_, f32[24,1536]{1,0:T(8,128)S(1)} %get-tuple-element.83.refs_3_.refs_1_), custom_call_target="tpu_custom_call" | custom-call | bytes 4718592 | tf_op jit(solution)/shard_map/input_sum/pallas_call | solution.py:621
  (95 shorter events, 36.7 us)
Async XLA Ops:
  0.6 13.6 %collective-permute-start.2 = (bf16[512,3072]{1,0:T(8,128)(2,1)}, bf16[512,3072]{1,0:T(8,128)(2,1)S(1)}, u32[]{:S(2)}, u32[]{:S(2)}) collective-permute-start(bf16[512,3072]{1,0:T(8,128)(2,1)} %pre_ref.3), channel_id=1, source_target_pairs={{0,1},{1,0},{2,3},{3,2},{4,5},{5,4},{6,7},{7,6},{8,9},{9,8},{10,11... | collective-permute-start | bytes 9437192 | tf_op jit(solution)/shard_map/ppermute | solution.py:866
  1.2 12.1 %collective-permute-start.1 = (bf16[512,768]{1,0:T(8,128)(2,1)}, bf16[512,768]{1,0:T(8,128)(2,1)S(1)}, u32[]{:S(2)}, u32[]{:S(2)}) collective-permute-start(bf16[512,768]{1,0:T(8,128)(2,1)} %in_ref.3), channel_id=1, source_target_pairs={{0,1},{1,0},{2,3},{3,2},{4,5},{5,4},{6,7},{7,6},{8,9},{9,8},{10,11... | collective-permute-start | bytes 2359304 | tf_op jit(solution)/shard_map/ppermute | solution.py:866
  1.3 23.4 %collective-permute-start.7 = (bf16[24,3072]{1,0:T(8,128)(2,1)}, bf16[24,3072]{1,0:T(8,128)(2,1)S(1)}, u32[]{:S(2)}, u32[]{:S(2)}) collective-permute-start(bf16[24,3072]{1,0:T(8,128)(2,1)} %refs_1_.1), channel_id=1, source_target_pairs={{0,1},{1,0},{2,3},{3,2},{4,5},{5,4},{6,7},{7,6},{8,9},{9,8},{10,11... | collective-permute-start | bytes 442376 | tf_op jit(solution)/shard_map/ppermute | solution.py:866
  1.7 23.5 %collective-permute-start.3 = (bf16[96,768]{1,0:T(8,128)(2,1)}, bf16[96,768]{1,0:T(8,128)(2,1)S(1)}, u32[]{:S(2)}, u32[]{:S(2)}) collective-permute-start(bf16[96,768]{1,0:T(8,128)(2,1)} %param.8), channel_id=1, source_target_pairs={{0,0},{1,16},{2,2},{3,18},{4,4},{5,20},{6,6},{7,22},{8,8},{9,24},{... | collective-permute-start | bytes 442376 | tf_op jit(solution)/shard_map/ppermute | solution.py:866
  8.6 16.7 %collective-permute-start.4 = (bf16[96,768]{1,0:T(8,128)(2,1)}, bf16[96,768]{1,0:T(8,128)(2,1)}, u32[]{:S(2)}, u32[]{:S(2)}) collective-permute-start(bf16[96,768]{1,0:T(8,128)(2,1)} %param.8), channel_id=1, source_target_pairs={{0,8},{1,24},{2,10},{3,26},{4,12},{5,28},{6,14},{7,30},{8,0},{9,16... | collective-permute-start | bytes 442376 | tf_op jit(solution)/shard_map/ppermute | solution.py:866
  14.2 11.1 %collective-permute-start.5 = (bf16[96,768]{1,0:T(8,128)(2,1)}, bf16[96,768]{1,0:T(8,128)(2,1)}, u32[]{:S(2)}, u32[]{:S(2)}) collective-permute-start(bf16[96,768]{1,0:T(8,128)(2,1)} %param.8), channel_id=1, source_target_pairs={{0,16},{1,0},{2,18},{3,2},{4,20},{5,4},{6,22},{7,6},{8,24},{9,8},{... | collective-permute-start | bytes 442376 | tf_op jit(solution)/shard_map/ppermute | solution.py:866
  14.2 11.1 %collective-permute-start.6 = (bf16[96,768]{1,0:T(8,128)(2,1)}, bf16[96,768]{1,0:T(8,128)(2,1)}, u32[]{:S(2)}, u32[]{:S(2)}) collective-permute-start(bf16[96,768]{1,0:T(8,128)(2,1)} %param.8), channel_id=1, source_target_pairs={{0,24},{1,8},{2,26},{3,10},{4,28},{5,12},{6,30},{7,14},{8,16},{9,0... | collective-permute-start | bytes 442376 | tf_op jit(solution)/shard_map/ppermute | solution.py:866
  29.0 18.9 %collective-permute-start.15 = (bf16[2,192,768]{2,1,0:T(8,128)(2,1)S(1)}, bf16[2,192,768]{2,1,0:T(8,128)(2,1)S(1)}, u32[]{:S(2)}, u32[]{:S(2)}) collective-permute-start(bf16[2,192,768]{2,1,0:T(8,128)(2,1)S(1)} %get-tuple-element.45.refs_3_), channel_id=1, source_target_pairs={{0,2},{1,3},{2,0},{3,1},{4,6},{5,7},{6,4},{7,5},{8,10},{9,11},{10,... | collective-permute-start | bytes 1769480 | tf_op jit(solution)/shard_map/ppermute | solution.py:866
  33.5 16.2 %collective-permute-start.14 = (bf16[2,192,768]{2,1,0:T(8,128)(2,1)S(1)}, bf16[2,192,768]{2,1,0:T(8,128)(2,1)S(1)}, u32[]{:S(2)}, u32[]{:S(2)}) collective-permute-start(bf16[2,192,768]{2,1,0:T(8,128)(2,1)S(1)} %get-tuple-element.48.refs_5_), channel_id=1, source_target_pairs={{0,4},{1,5},{2,6},{3,7},{4,0},{5,1},{6,2},{7,3},{8,12},{9,13},{10,... | collective-permute-start | bytes 1769480 | tf_op jit(solution)/shard_map/ppermute | solution.py:866
  36.7 25.4 %collective-permute-start.10 = (bf16[2,192,768]{2,1,0:T(8,128)(2,1)S(1)}, bf16[2,192,768]{2,1,0:T(8,128)(2,1)S(1)}, u32[]{:S(2)}, u32[]{:S(2)}) collective-permute-start(bf16[2,192,768]{2,1,0:T(8,128)(2,1)S(1)} %get-tuple-element.49.refs_3_.mine), channel_id=1, source_target_pairs={{0,4},{1,5},{2,6},{3,7},{4,0},{5,1},{6,2},{7,3},{8,12},{9,13},{10,... | collective-permute-start | bytes 1769480 | tf_op jit(solution)/shard_map/ppermute | solution.py:866
  38.0 31.0 %collective-permute-start.16 = (bf16[2,192,768]{2,1,0:T(8,128)(2,1)S(1)}, bf16[2,192,768]{2,1,0:T(8,128)(2,1)S(1)}, u32[]{:S(2)}, u32[]{:S(2)}) collective-permute-start(bf16[2,192,768]{2,1,0:T(8,128)(2,1)S(1)} %get-tuple-element.57.mine), channel_id=1, source_target_pairs={{0,2},{1,3},{2,0},{3,1},{4,6},{5,7},{6,4},{7,5},{8,10},{9,11},{10,... | collective-permute-start | bytes 1769480 | tf_op jit(solution)/shard_map/ppermute | solution.py:866
  38.3 13.3 %collective-permute-start.11 = (bf16[2,24,1536]{2,1,0:T(8,128)(2,1)S(1)}, bf16[2,24,1536]{2,1,0:T(8,128)(2,1)S(1)}, u32[]{:S(2)}, u32[]{:S(2)}) collective-permute-start(bf16[2,24,1536]{2,1,0:T(8,128)(2,1)S(1)} %pair_kernel.1.refs_5_.refs_1_), channel_id=1, source_target_pairs={{0,8},{1,9},{2,10},{3,11},{4,12},{5,13},{6,14},{7,15},{8,0},{9,1},... | collective-permute-start | bytes 442376 | tf_op jit(solution)/shard_map/ppermute | solution.py:866
  47.8 12.5 %collective-permute-start.12 = (bf16[2,24,1536]{2,1,0:T(8,128)(2,1)S(1)}, bf16[2,24,1536]{2,1,0:T(8,128)(2,1)S(1)}, u32[]{:S(2)}, u32[]{:S(2)}) collective-permute-start(bf16[2,24,1536]{2,1,0:T(8,128)(2,1)S(1)} %pair_kernel.1.refs_5_.refs_1_), channel_id=1, source_target_pairs={{0,16},{1,17},{2,18},{3,19},{4,20},{5,21},{6,22},{7,23},{8,24},{9,... | collective-permute-start | bytes 442376 | tf_op jit(solution)/shard_map/ppermute | solution.py:866
  49.6 11.9 %collective-permute-start.13 = (bf16[2,24,1536]{2,1,0:T(8,128)(2,1)S(1)}, bf16[2,24,1536]{2,1,0:T(8,128)(2,1)S(1)}, u32[]{:S(2)}, u32[]{:S(2)}) collective-permute-start(bf16[2,24,1536]{2,1,0:T(8,128)(2,1)S(1)} %pair_kernel.1.refs_5_.refs_1_), channel_id=1, source_target_pairs={{0,24},{1,25},{2,26},{3,27},{4,28},{5,29},{6,30},{7,31},{8,16},{9,... | collective-permute-start | bytes 442376 | tf_op jit(solution)/shard_map/ppermute | solution.py:866
  51.7 16.6 %collective-permute-start.18 = (bf16[192,768]{1,0:T(8,128)(2,1)S(1)}, bf16[192,768]{1,0:T(8,128)(2,1)S(1)}, u32[]{:S(2)}, u32[]{:S(2)}) collective-permute-start(bf16[192,768]{1,0:T(8,128)(2,1)S(1)} %get-tuple-element.53.refs_5_), channel_id=1, source_target_pairs={{0,2},{1,3},{2,0},{3,1},{4,6},{5,7},{6,4},{7,5},{8,10},{9,11},{10,... | collective-permute-start | bytes 884744 | tf_op jit(solution)/shard_map/ppermute | solution.py:866
  67.0 30.9 %collective-permute-start.21 = (bf16[4,2,48,768]{3,2,1,0:T(8,128)(2,1)S(1)}, bf16[4,2,48,768]{3,2,1,0:T(8,128)(2,1)S(1)}, u32[]{:S(2)}, u32[]{:S(2)}) collective-permute-start(bf16[4,2,48,768]{3,2,1,0:T(8,128)(2,1)S(1)} %get-tuple-element.60.refs_5_), channel_id=1, source_target_pairs={{0,2},{1,3},{2,0},{3,1},{4,6},{5,7},{6,4},{7,5},{8,10},{9,11},{10,... | collective-permute-start | bytes 1769480 | tf_op jit(solution)/shard_map/ppermute | solution.py:866
  73.9 25.9 %collective-permute-start.27 = (bf16[4,2,48,768]{3,2,1,0:T(8,128)(2,1)S(1)}, bf16[4,2,48,768]{3,2,1,0:T(8,128)(2,1)S(1)}, u32[]{:S(2)}, u32[]{:S(2)}) collective-permute-start(bf16[4,2,48,768]{3,2,1,0:T(8,128)(2,1)S(1)} %get-tuple-element.69.refs_6_), channel_id=1, source_target_pairs={{0,4},{1,5},{2,6},{3,7},{4,0},{5,1},{6,2},{7,3},{8,12},{9,13},{10,... | collective-permute-start | bytes 1769480 | tf_op jit(solution)/shard_map/ppermute | solution.py:866
  74.8 10.9 %collective-permute-start.22 = (bf16[96,768]{1,0:T(8,128)(2,1)S(1)}, bf16[96,768]{1,0:T(8,128)(2,1)S(1)}, u32[]{:S(2)}, u32[]{:S(2)}) collective-permute-start(bf16[96,768]{1,0:T(8,128)(2,1)S(1)} %get-tuple-element.61._), channel_id=1, source_target_pairs={{0,0},{1,16},{2,2},{3,18},{4,4},{5,20},{6,6},{7,22},{8,8},{9,24},{... | collective-permute-start | bytes 442376 | tf_op jit(solution)/shard_map/ppermute | solution.py:866
  85.6 12.3 %collective-permute-start.19 = (bf16[4,48,768]{2,1,0:T(8,128)(2,1)S(1)}, bf16[4,48,768]{2,1,0:T(8,128)(2,1)S(1)}, u32[]{:S(2)}, u32[]{:S(2)}) collective-permute-start(bf16[4,48,768]{2,1,0:T(8,128)(2,1)S(1)} %get-tuple-element.54._.refs_1_), channel_id=1, source_target_pairs={{0,2},{1,3},{2,0},{3,1},{4,6},{5,7},{6,4},{7,5},{8,10},{9,11},{10,... | collective-permute-start | bytes 884744 | tf_op jit(solution)/shard_map/ppermute | solution.py:866
  107.8 10.7 %collective-permute-start.29 = (bf16[2,4,48,768]{3,2,1,0:T(8,128)(2,1)S(1)}, bf16[2,4,48,768]{3,2,1,0:T(8,128)(2,1)S(1)}, u32[]{:S(2)}, u32[]{:S(2)}) collective-permute-start(bf16[2,4,48,768]{3,2,1,0:T(8,128)(2,1)S(1)} %get-tuple-element.76.a0._), channel_id=1, source_target_pairs={{0,4},{1,5},{2,6},{3,7},{4,0},{5,1},{6,2},{7,3},{8,12},{9,13},{10,... | collective-permute-start | bytes 1769480 | tf_op jit(solution)/shard_map/ppermute | solution.py:866
  109.1 10.3 %collective-permute-start.30 = (bf16[2,4,48,768]{3,2,1,0:T(8,128)(2,1)S(1)}, bf16[2,4,48,768]{3,2,1,0:T(8,128)(2,1)S(1)}, u32[]{:S(2)}, u32[]{:S(2)}) collective-permute-start(bf16[2,4,48,768]{3,2,1,0:T(8,128)(2,1)S(1)} %get-tuple-element.77.b0), channel_id=1, source_target_pairs={{0,2},{1,3},{2,0},{3,1},{4,6},{5,7},{6,4},{7,5},{8,10},{9,11},{10,... | collective-permute-start | bytes 1769480 | tf_op jit(solution)/shard_map/ppermute | solution.py:866
  109.3 19.3 %collective-permute-start.32 = (bf16[48,1536]{1,0:T(8,128)(2,1)S(1)}, bf16[48,1536]{1,0:T(8,128)(2,1)S(1)}, u32[]{:S(2)}, u32[]{:S(2)}) collective-permute-start(bf16[48,1536]{1,0:T(8,128)(2,1)S(1)} %get-tuple-element.75.refs_5_), channel_id=1, source_target_pairs={{0,8},{1,9},{2,10},{3,11},{4,12},{5,13},{6,14},{7,15},{8,0},{9,1},... | collective-permute-start | bytes 442376 | tf_op jit(solution)/shard_map/ppermute | solution.py:866
  113.4 15.2 %collective-permute-start.33 = (bf16[48,1536]{1,0:T(8,128)(2,1)S(1)}, bf16[48,1536]{1,0:T(8,128)(2,1)S(1)}, u32[]{:S(2)}, u32[]{:S(2)}) collective-permute-start(bf16[48,1536]{1,0:T(8,128)(2,1)S(1)} %get-tuple-element.81), channel_id=1, source_target_pairs={{0,16},{1,17},{2,18},{3,19},{4,20},{5,21},{6,22},{7,23},{8,24},{9,... | collective-permute-start | bytes 442376 | tf_op jit(solution)/shard_map/ppermute | solution.py:866
  115.6 13.0 %collective-permute-start.34 = (bf16[48,1536]{1,0:T(8,128)(2,1)S(1)}, bf16[48,1536]{1,0:T(8,128)(2,1)S(1)}, u32[]{:S(2)}, u32[]{:S(2)}) collective-permute-start(bf16[48,1536]{1,0:T(8,128)(2,1)S(1)} %get-tuple-element.82), channel_id=1, source_target_pairs={{0,24},{1,25},{2,26},{3,27},{4,28},{5,29},{6,30},{7,31},{8,16},{9,... | collective-permute-start | bytes 442376 | tf_op jit(solution)/shard_map/ppermute | solution.py:866
  (25 other events, 147.0 us)

commit v3 on v1

--- a/solution.py
+++ b/solution.py
@@ -3,6 +3,8 @@
 import jax
 import jax.numpy as jnp
 from jax import lax
+from jax.experimental import pallas as pl
+from jax.experimental.pallas import tpu as pltpu
 from jax.sharding import PartitionSpec as P
 
 AXIS = "gx"
@@ -56,7 +58,7 @@
     return jnp.stack([first, second], axis)
 
 
-def per_device(out_grad, inputs, preact, w_out, w_in):
+def plain(out_grad, inputs, preact, w_out, w_in):
     n = lax.axis_size(AXIS)
     nz = n // 8
     nl = nz // 2
@@ -162,6 +164,429 @@
     return (input_grad, w_out_grad, w_in_grad)
 
 
+MIB = 1 << 20
+ANY = pl.BlockSpec(memory_space=pl.ANY)
+VMEM = pl.BlockSpec(memory_space=pltpu.VMEM)
+SMEM = pl.BlockSpec(memory_space=pltpu.SMEM)
+
+
+def shape(dims, kind):
+    return jax.ShapeDtypeStruct(dims, kind)
+
+
+class Order:
+    def __init__(self):
+        self.after = []
+
+    def __call__(self, outs):
+        self.after = [outs[0]]
+        return outs
+
+
+def small(body, where, arrays, outs, after=(), scratch=(), name=None, flops=0):
+    skipped = len(after)
+
+    def run(*refs):
+        body(*refs[: 1 + len(arrays)], *refs[1 + len(arrays) + skipped :])
+
+    moved_bytes = sum(a.size * a.dtype.itemsize for a in list(arrays) + list(outs))
+    return pl.pallas_call(
+        run,
+        name=name or body.__name__,
+        out_shape=outs,
+        in_specs=[SMEM] + [VMEM] * len(arrays) + [ANY] * skipped,
+        out_specs=[VMEM] * len(outs),
+        scratch_shapes=list(scratch),
+        compiler_params=pltpu.CompilerParams(vmem_limit_bytes=16 * MIB),
+        cost_estimate=pl.CostEstimate(
+            flops=flops, bytes_accessed=moved_bytes, transcendentals=0
+        ),
+    )(where, *arrays, *after)
+
+
+def pair_kernel(at, in_ref, got_ref, out):
+    c = at[3]
+    size = out.shape[2]
+    out[c] = jnp.where(c == 0, in_ref[:, :size], in_ref[:, size:])
+    out[1 - c] = jnp.where(c == 0, got_ref[:, :size], got_ref[:, size:])
+
+
+def join_kernel(at, own1, got1, own2, got2, one, two):
+    x, y = at[2], at[1]
+    one[x] = own1[...]
+    one[1 - x] = got1[...]
+    two[y] = own2[...]
+    two[1 - y] = got2[...]
+
+
+def rows_kernel(at, g00, g01, g10, g11, one, two):
+    high, low = at[4], at[5]
+    rows = g00.shape[0]
+    for cc in range(2):
+        from_same = jnp.where(high == cc, g00[...], g10[...])
+        from_next = jnp.where(high == cc, g01[...], g11[...])
+        part = pl.ds(cc * rows, rows)
+        one[part, :] = jnp.where(low == 0, from_same, from_next)
+        two[part, :] = jnp.where(low == 0, from_next, from_same)
+
+
+def columns_kernel(at, mine, g1, g2, g3, one, two):
+    z = at[0]
+    rows, size = mine.shape[0] * mine.shape[1], one.shape[2]
+    for k, got in enumerate((mine, g1, g2, g3)):
+        value = got[...].reshape(rows, 2 * size)
+        one[z ^ k] = value[:, :size]
+        two[z ^ k] = value[:, size:]
+
+
+def out_total(at, cut, pre, pre_got, grad, grad_got, after):
+    tokens, width = grad.shape
+    size = pre_got.shape[1] // 8
+    rows = size // 2
+
+    def body(at, pre_ref, got_ref, grad_ref, grad2_ref, *refs):
+        slope, send, keep, total = refs[-4:]
+        t = pl.program_id(0)
+        x, y = at[2], at[1]
+        activ, slope1 = gelu_parts(pre_ref[...])
+        slope[pl.ds(0, tokens), :] = slope1
+        value = contract_first(activ, grad_ref[...])
+        activ, slope2 = gelu_parts(got_ref[...])
+        slope[pl.ds(tokens, tokens), :] = slope2
+        value = value + contract_first(activ, grad2_ref[...])
+        if cut == 0:
+            total[...] = value.reshape(2, rows, width)
+            send[0] = total[1 - x].astype(BF)
+            keep[0] = total[x]
+        else:
+
+            @pl.when(t == y)
+            def _():
+                keep[...] = value.reshape(2, rows, width)
+
+            @pl.when(t != y)
+            def _():
+                send[...] = value.astype(BF).reshape(2, rows, width)
+
+    whole = lambda t, at: (0, 0)
+    if cut == 0:
+        parts = pl.BlockSpec((1, rows, width), lambda t, at: (t, 0, 0))
+    else:
+        parts = pl.BlockSpec((2, rows, width), lambda t, at: (0, 0, 0))
+    return pl.pallas_call(
+        body,
+        name=f"out_total{cut}",
+        grid_spec=pltpu.PrefetchScalarGridSpec(
+            num_scalar_prefetch=1,
+            grid=(2,),
+            in_specs=[
+                pl.BlockSpec((tokens, size), lambda t, at: (0, at[3] * 4 + cut * 2 + t)),
+                pl.BlockSpec((tokens, size), lambda t, at: (0, at[3] * 4 + cut * 2 + t)),
+                pl.BlockSpec((tokens, width), whole),
+                pl.BlockSpec((tokens, width), whole),
+            ]
+            + [ANY] * len(after),
+            out_specs=[
+                pl.BlockSpec((2 * tokens, size), lambda t, at: (0, t)),
+                parts,
+                parts,
+            ],
+            scratch_shapes=[pltpu.VMEM((2, rows, width), F32)],
+        ),
+        out_shape=[
+            shape((2 * tokens, 2 * size), F32),
+            shape((2, rows, width), BF),
+            shape((2, rows, width), F32),
+        ],
+        compiler_params=pltpu.CompilerParams(vmem_limit_bytes=(56 if cut == 0 else 24) * MIB),
+        cost_estimate=pl.CostEstimate(
+            flops=8 * tokens * size * width,
+            bytes_accessed=20 * MIB,
+            transcendentals=4 * tokens * size,
+        ),
+    )(at, pre, pre_got, grad, grad_got, *after)
+
+
+def in_total(at, cut, grad, grad_got, inputs, inputs_got, slope, pieces, nz, after):
+    tokens, width = grad.shape
+    size = slope.shape[1] // 2
+    rows = size // 2
+    depth = width // (4 * nz)
+
+    def body(at, grad_ref, grad2_ref, in_ref, in2_ref, slope_ref, mine, other, _, pre_grad, send, keep):
+        t = pl.program_id(0)
+        x, y = at[2], at[1]
+        if cut == 0:
+            value = jnp.where(t == y, mine[...], other[...]).reshape(size, width)
+        else:
+            first, second = mine[t], other[t]
+            value = jnp.concatenate(
+                [jnp.where(x == 0, first, second), jnp.where(x == 0, second, first)], 0
+            )
+        totals = 0.0
+        for part, (g, i) in enumerate(((grad_ref, in_ref), (grad2_ref, in2_ref))):
+            at_rows = pl.ds(part * tokens, tokens)
+            act_grad = contract_last(g[...], value)
+            pre = (act_grad * slope_ref[at_rows, :]).astype(BF)
+            pre_grad[at_rows, :] = pre
+            totals = totals + contract_first(i[...], pre)
+        parts = totals.reshape(nz, 2, 2, depth, size)
+        if cut == 0:
+            first, second, bit = parts[:, :, 0], parts[:, :, 1], x
+        else:
+            first, second, bit = parts[:, 0], parts[:, 1], y
+        send[...] = jnp.where(bit == 0, second, first).astype(BF)
+        keep[...] = jnp.where(bit == 0, first, second)
+
+    whole = lambda t, at: (0, 0)
+    tile = lambda t, at: (0, t)
+    piece = pl.BlockSpec((2, rows, width), lambda t, at: (0, 0, 0))
+    parts = pl.BlockSpec((nz, 2, depth, size), lambda t, at: (0, 0, 0, t))
+    return pl.pallas_call(
+        body,
+        name=f"in_total{cut}",
+        grid_spec=pltpu.PrefetchScalarGridSpec(
+            num_scalar_prefetch=1,
+            grid=(2,),
+            in_specs=[pl.BlockSpec((tokens, width), whole)] * 4
+            + [pl.BlockSpec((2 * tokens, size), tile)]
+            + [piece] * 2
+            + [ANY],
+            out_specs=[pl.BlockSpec((2 * tokens, size), tile), parts, parts],
+        ),
+        out_shape=[
+            shape((2 * tokens, 2 * size), BF),
+            shape((nz, 2, depth, 2 * size), BF),
+            shape((nz, 2, depth, 2 * size), F32),
+        ],
+        compiler_params=pltpu.CompilerParams(vmem_limit_bytes=24 * MIB),
+        cost_estimate=pl.CostEstimate(
+            flops=16 * tokens * size * width, bytes_accessed=16 * MIB, transcendentals=0
+        ),
+    )(at, grad, grad_got, inputs, inputs_got, slope, *pieces, *after)
+
+
+def input_part(at, part, pre_grads, pieces, nz, after, came=None):
+    tokens, size = pre_grads[0].shape[0] // 2, pre_grads[0].shape[1]
+    depth = pieces[0].shape[2]
+    width = 4 * nz * depth
+    steps = 2
+
+    def body(at, g0, g1, a0, a1, b0, b1, *refs):
+        out, weight0, weight1 = refs[-3:]
+        x, y = at[2], at[1]
+
+        @pl.when(pl.program_id(0) == 0)
+        def _():
+            for k in range(2):
+                weight0[:, y, k] = a0[k]
+                weight0[:, 1 - y, k] = a1[k]
+                weight1[:, k, x] = b0[k]
+                weight1[:, k, 1 - x] = b1[k]
+
+        value = contract_last(g0[...], weight0[...].reshape(width, size))
+        value = value + contract_last(g1[...], weight1[...].reshape(width, size))
+        out[...] = value if came is None else value + refs[0][...]
+
+    piece = pl.BlockSpec((2, nz, depth, size), lambda t, at: (0, 0, 0, 0))
+    rows = pl.BlockSpec((tokens // steps, size), lambda t, at: (part * steps + t, 0))
+    out = pl.BlockSpec((tokens // steps, width), lambda t, at: (t, 0))
+    added = [] if came is None else [came]
+    return pl.pallas_call(
+        body,
+        name=f"input_part{part}",
+        grid_spec=pltpu.PrefetchScalarGridSpec(
+            num_scalar_prefetch=1,
+            grid=(steps,),
+            in_specs=[rows] * 2 + [piece] * 4 + [out] * len(added) + [ANY] * len(after),
+            out_specs=out,
+            scratch_shapes=[pltpu.VMEM((nz, 2, 2, depth, size), BF)] * 2,
+        ),
+        out_shape=shape((tokens, width), F32),
+        compiler_params=pltpu.CompilerParams(vmem_limit_bytes=24 * MIB),
+        cost_estimate=pl.CostEstimate(
+            flops=4 * tokens * size * width, bytes_accessed=6 * MIB, transcendentals=0
+        ),
+    )(at, *pre_grads, *pieces, *added, *after)
+
+
+def per_device(out_grad, inputs, preact, w_out, w_in):
+    n = lax.axis_size(AXIS)
+    rows_out, rows_in = w_out.shape[0], w_in.shape[0]
+    if n != 32 or rows_out % 16 or (2 * rows_in) % 16 or out_grad.shape[1] % 128:
+        return plain(out_grad, inputs, preact, w_out, w_in)
+    nz = n // 8
+    nl = nz // 2
+    me = lax.axis_index(AXIS)
+    z, y, x, c = coords(me)
+    at = jnp.stack([z, y, x, c, z // nl, z % nl]).astype(jnp.int32)
+    grad_scale = 1.0 / math.sqrt(out_grad.shape[0] * n)
+    tokens, width = out_grad.shape
+    hidden = preact.shape[1]
+    half = hidden // 2
+    size = half // 2
+
+    along_x = moved(n, lambda z, y, x, c: (z, y, 1 - x, c))
+    along_y = moved(n, lambda z, y, x, c: (z, 1 - y, x, c))
+
+    def send(array, perm):
+        return lax.ppermute(array, AXIS, perm)
+
+    def z_perm(k, swap=0):
+        return moved(n, lambda z, y, x, c: (z ^ k, y, x, c ^ swap))
+
+    def gather_perm(i, j):
+        return moved(
+            n, lambda z, y, x, c: ((c ^ i) * nl + ((z % nl) ^ j), y, x, z // nl)
+        )
+
+    def scatter_perm(i, j):
+        return moved(
+            n, lambda z, y, x, c: (c * nl + ((z % nl) ^ j), y, x, (z // nl) ^ i)
+        )
+
+    order = Order()
+
+    def kernel(body, arrays, outs, scratch=(), name=None, flops=0):
+        return order(small(body, at, arrays, outs, order.after, scratch, name, flops))
+
+    pre_got = send(preact, z_perm(0, 1))
+    grad_got = send(out_grad, z_perm(0, 1))
+    got = [send(w_out, gather_perm(i, j)) for i in range(2) for j in range(2)]
+    inputs_got = send(inputs, z_perm(0, 1))
+    in_got = send(w_in, z_perm(0, 1))
+
+    slopes, sent, kept = [None] * 2, [None] * 2, [None] * 2
+
+    def out_cut(cut):
+        s, o, k = out_total(at, cut, preact, pre_got, out_grad, grad_got, order.after)
+        order([o])
+        slopes[cut], kept[cut] = s, k
+        sent[cut] = send(o, (along_x, along_y)[cut])
+
+    def middle(k, r, next_perm, bit, dim):
+        dims = k.shape[:dim] + k.shape[dim + 1 :]
+
+        def body(at, k_ref, r_ref, out, keep):
+            b = at[bit]
+            spot = (slice(None),) * dim
+            out[...] = (k_ref[spot + (1 - b,)] + r_ref[spot + (1 - b,)].astype(F32)).astype(BF)
+            keep[...] = k_ref[spot + (b,)] + r_ref[spot + (b,)].astype(F32)
+
+        out, keep = kernel(body, [k, r], [shape(dims, BF), shape(dims, F32)], name=f"middle{dim}{bit}")
+        return keep, send(out, next_perm)
+
+    def join(one, one_got, two, two_got):
+        pair = shape((2,) + one.shape, BF)
+        return kernel(join_kernel, [one, one_got, two, two_got], [pair, pair])
+
+    order.after = [inputs_got]
+    out_cut(0)
+
+    (in_two,) = kernel(pair_kernel, [w_in, in_got], [shape((2, rows_in, half), BF)])
+    in_z = [send(in_two, z_perm(k)) for k in range(1, nz)]
+
+    rows = shape((2 * rows_out, width), BF)
+    one, two = kernel(rows_kernel, got, [rows, rows])
+    one_got, two_got = send(one, along_x), send(two, along_y)
+    out_cut(1)
+    ones, twos = join(one, one_got, two, two_got)
+    ones_got, twos_got = send(ones, along_y), send(twos, along_x)
+
+    out_sides = [middle(kept[0], sent[0], along_y, 1, 0), middle(kept[1], sent[1], along_x, 2, 0)]
+
+    spread = shape((nz, 2 * rows_in, size), BF)
+    one, two = kernel(columns_kernel, [in_two] + in_z, [spread, spread])
+    in_pieces = [one, send(one, along_x), two, send(two, along_y)]
+
+    pre_grads, in_sent, in_kept = [None] * 2, [None] * 2, [None] * 2
+
+    def in_cut(cut, pieces):
+        p, o, k = in_total(
+            at, cut, out_grad, grad_got, inputs, inputs_got, slopes[cut], pieces, nz, order.after
+        )
+        order([o])
+        pre_grads[cut], in_kept[cut] = p, k
+        in_sent[cut] = send(o, (along_x, along_y)[cut])
+
+    in_cut(0, [ones, ones_got])
+
+    def out_parts(at, k1, r1, k2, r2, o00, o01, o10, o11, own, total):
+        high, low = at[4], at[5]
+        total[0] = (k1[...] + r1[...].astype(F32)).reshape(2, rows_out, width)
+        total[1] = (k2[...] + r2[...].astype(F32)).reshape(2, rows_out, width)
+        own[...] = total[low, high]
+        o00[...] = total[low, high].astype(BF)
+        o01[...] = total[1 - low, high].astype(BF)
+        o10[...] = total[low, 1 - high].astype(BF)
+        o11[...] = total[1 - low, 1 - high].astype(BF)
+
+    row = (rows_out, width)
+    *out_got, out_own = kernel(
+        out_parts,
+        [*out_sides[0], *out_sides[1]],
+        [shape(row, BF)] * 4 + [shape(row, F32)],
+        [pltpu.VMEM((2, 2, rows_out, width), F32)],
+    )
+    out_got = [send(p, scatter_perm(*divmod(k, 2))) for k, p in enumerate(out_got)]
+
+    in_cut(1, [twos, twos_got])
+
+    one, one_got = middle(in_kept[0], in_sent[0], along_y, 1, 1)
+    two, two_got = middle(in_kept[1], in_sent[1], along_x, 2, 1)
+
+    def out_sum(at, own, r00, r01, r10, r11, out):
+        first = jnp.where(at[3] == at[4], own[...], r00[...].astype(F32))
+        rest = r01[...].astype(F32) + r10[...].astype(F32) + r11[...].astype(F32)
+        out[...] = (first + rest) * grad_scale
+
+    (w_out_grad,) = kernel(out_sum, [out_own] + out_got, [shape(out_own.shape, F32)])
+
+    def in_parts(at, k1, r1, k2, r2, *outs):
+        z = at[0]
+        *outs, own, total = outs
+        total[:, :, :size] = k1[...] + r1[...].astype(F32)
+        total[:, :, size:] = k2[...] + r2[...].astype(F32)
+        own[...] = total[z]
+        for k in range(1, nz):
+            outs[k - 1][...] = total[z ^ k].astype(BF)
+
+    row = (2 * rows_in, half)
+    *in_got, in_own = kernel(
+        in_parts,
+        [one, one_got, two, two_got],
+        [shape(row, BF)] * (nz - 1) + [shape(row, F32)],
+        [pltpu.VMEM((nz, 2 * rows_in, half), F32)],
+    )
+    in_got = [send(p, z_perm(k)) for p, k in zip(in_got, range(1, nz))]
+
+    ones, twos = join(*in_pieces)
+    in_pieces = [ones, send(ones, along_y), twos, send(twos, along_x)]
+
+    (part,) = order([input_part(at, 1, pre_grads, in_pieces, nz, order.after)])
+    part_got = send(part, z_perm(0, 1))
+
+    def in_sum(at, own, r1, r2, r3, mine, other):
+        total = own[...] + r1[...].astype(F32) + r2[...].astype(F32) + r3[...].astype(F32)
+        total = total * grad_scale
+        first, second = total[:rows_in], total[rows_in:]
+        mine[...] = jnp.where(at[3] == 0, first, second)
+        other[...] = jnp.where(at[3] == 0, second, first)
+
+    row = shape((rows_in, half), F32)
+    mine, other = kernel(in_sum, [in_own] + in_got, [row, row], flops=10**11)
+    other = send(other, z_perm(0, 1))
+
+    def in_join(at, mine, other, out):
+        c = at[3]
+        out[:, :half] = jnp.where(c == 0, mine[...], other[...])
+        out[:, half:] = jnp.where(c == 0, other[...], mine[...])
+
+    (w_in_grad,) = kernel(in_join, [mine, other], [shape((rows_in, hidden), F32)])
+    input_grad = input_part(at, 0, pre_grads, in_pieces, nz, order.after, part_got)
+    return (input_grad, w_out_grad, w_in_grad)
+
+
 def solution(mesh):
     in_specs = (
         P(("grp", "gx"), None),

time: 187 us -> 131 us (0.70)
  waiting for transfers between devices: 86.4 us -> 34.3 us
  Pallas kernels: 0 us -> 37.2 us
  local copies, waits for them, and re-layouts: 24.1 us -> 5.71 us
  matrix products: 15.4 us -> 0 us
  other arithmetic: 6.94 us -> 0 us
    ppermute x36, waiting for transfers between devices: 86.4 us -> 34.3 us  [send(): return lax.ppermute(array, AXIS, perm)]
    pallas_call x0 -> x20, Pallas kernels: none -> 37.2 us  [the longest x2 11.2 us: out_total(): pl.pallas_call(body, name=f'out_total{cut}', grid_spec=pltpu.PrefetchScal...]
    dot_general x4 -> x0, matrix products: 15.4 us -> none  [the longest x2 8.81 us: contract_last(): lax.dot_general(left, right, (((1,), (1,)), ((), ())), preferred_element_...]
    reshape x3 -> x0, local copies, waits for them, and re-layouts: 8.8 us -> none  [the longest x1 7.06 us: per_device(): pre_split = preact.reshape(tokens, 2, half)]
    dynamic_slice x3 -> x0, local copies, waits for them, and re-layouts: 8.47 us -> none  [the longest x2 8.42 us: pick(): return lax.dynamic_index_in_dim(array, at, axis, keepdims=False)]
    another operation x22 -> x0, other arithmetic: 3.43 us -> none  [the longest x14 1.79 us: paired(): return jnp.stack([first, second], axis)]
    add x9 -> x0, other arithmetic: 2 us -> none  [the longest x1 1.33 us: per_device(): input_grad = part[:tokens] + send(part[tokens:], cores)]
    unnamed x6 -> x32, local copies, waits for them, and re-layouts: 3.76 us -> 5.03 us
  transfers between devices with their start and end apart: 36 -> 36, of which waited for: 16 -> 10; matrix products, arithmetic and copies ran while one was open for 24% -> 1% of each run, Pallas kernels for 0% -> 25%
where the time goes in v3:
time: 131 us; the launch traced here: 130 us
  starting transfers between devices  51.7 us (39%)
  Pallas kernels  37.2 us (28%)
  waiting for transfers between devices  34.3 us (26%)
  local copies, waits for them, and re-layouts  5.71 us (4%)
    ppermute x36, starting transfers between devices, send(): return lax.ppermute(array, AXIS, perm)  51.7 us
    ppermute x36, waiting for transfers between devices, send(): return lax.ppermute(array, AXIS, perm)  34.3 us
    pallas_call x2, Pallas kernels, out_total(): pl.pallas_call(body, name=f'out_total{cut}', grid_spec=pltpu.PrefetchScal...  11.2 us
    pallas_call x14, Pallas kernels, small(): pl.pallas_call(run, name=name or body.__name__, out_shape=outs, in_specs=...  10.8 us
    pallas_call x2, Pallas kernels, in_total(): pl.pallas_call(body, name=f'in_total{cut}', grid_spec=pltpu.PrefetchScala...  9.59 us
    pallas_call x2, Pallas kernels, input_part(): pl.pallas_call(body, name=f'input_part{part}', grid_spec=pltpu.PrefetchSc...  5.59 us
    unnamed x32, local copies, waits for them, and re-layouts  5.03 us
  transfers between devices with their start and end apart: 36, of which 10 were waited for; matrix products, arithmetic and copies ran while one was open for 1% of the time, Pallas kernels for 25%

profile of v3, /device:TPU:1, one launch (start us, length us, event | category | flops | bytes accessed | tf_op | source)
XLA Modules:
  0.0 129.9 jit_solution(6493392179259501716)
XLA Ops:
  1.7 5.6 %collective-permute-start.3 = (bf16[96,768]{1,0:T(8,128)(2,1)}, bf16[96,768]{1,0:T(8,128)(2,1)S(1)}, u32[]{:S(2)}, u32[]{:S(2)}) collective-permute-start(bf16[96,768]{1,0:T(8,128)(2,1)} %param.8), channel_id=1, source_target_pairs={{0,0},{1,16},{2,2},{3,18},{4,4},{5,20},{6,6},{7,22},{8,8},{9,24},{... | collective-permute-start | bytes 442376 | tf_op jit(solution)/shard_map/ppermute | solution.py:433
  7.7 4.7 %collective-permute-start.4 = (bf16[96,768]{1,0:T(8,128)(2,1)}, bf16[96,768]{1,0:T(8,128)(2,1)}, u32[]{:S(2)}, u32[]{:S(2)}) collective-permute-start(bf16[96,768]{1,0:T(8,128)(2,1)} %param.8), channel_id=1, source_target_pairs={{0,8},{1,24},{2,10},{3,26},{4,12},{5,28},{6,14},{7,30},{8,0},{9,16... | collective-permute-start | bytes 442376 | tf_op jit(solution)/shard_map/ppermute | solution.py:433
  12.4 1.7 %collective-permute-start.6 = (bf16[96,768]{1,0:T(8,128)(2,1)}, bf16[96,768]{1,0:T(8,128)(2,1)}, u32[]{:S(2)}, u32[]{:S(2)}) collective-permute-start(bf16[96,768]{1,0:T(8,128)(2,1)} %param.8), channel_id=1, source_target_pairs={{0,24},{1,8},{2,26},{3,10},{4,28},{5,12},{6,30},{7,14},{8,16},{9,0... | collective-permute-start | bytes 442376 | tf_op jit(solution)/shard_map/ppermute | solution.py:433
  14.9 6.9 %out_total0.1 = (f32[1024,768]{1,0:T(8,128)}, bf16[2,192,768]{2,1,0:T(8,128)(2,1)}, f32[2,192,768]{2,1,0:T(8,128)}) custom-call(s32[6]{0:T(128)} %stack.27.at.refs_0_, bf16[512,3072]{1,0:T(8,128)(2,1)} %pre_ref.3, bf16[512,3072]{1,0:T(8,128)(2,1)} %copy-done.1, bf16[512,768]{1,0:T(8,128)(2,1)} %grad_ref.7, bf16[512,768]{1,0:T(8,128)(2,1)} %copy-done.4, ...), custom_call_target="tpu_custom_call" | custom-call | flops 1207959552 | bytes 20971520 | tf_op jit(solution)/shard_map/out_total0/pallas_call | solution.py:276
  27.5 1.9 %copy-done.2 = bf16[512,3072]{1,0:T(8,128)(2,1)S(1)} copy-done((bf16[512,3072]{1,0:T(8,128)(2,1)S(1)}, bf16[512,3072]{1,0:T(8,128)(2,1)}, u32[]{:S(2)}) %copy-start.2) | copy-done | bytes 3145752
  29.4 4.2 %out_total1.1 = (f32[1024,768]{1,0:T(8,128)S(1)}, bf16[2,192,768]{2,1,0:T(8,128)(2,1)S(1)}, f32[2,192,768]{2,1,0:T(8,128)S(1)}) custom-call(s32[6]{0:T(128)S(1)} %copy-done.12, bf16[512,3072]{1,0:T(8,128)(2,1)S(1)} %copy-done, bf16[512,3072]{1,0:T(8,128)(2,1)S(1)} %copy-done.2, bf16[512,768]{1,0:T(8,128)(2,1)S(1)} %copy-done.3, ...), custom_call_target="tpu_custom_call" | custom-call | flops 1207959552 | bytes 20971520 | tf_op jit(solution)/shard_map/out_total1/pallas_call | solution.py:276
  37.3 8.9 %collective-permute-done.15.refs_2_ = bf16[2,192,768]{2,1,0:T(8,128)(2,1)S(1)} collective-permute-done((bf16[2,192,768]{2,1,0:T(8,128)(2,1)}, bf16[2,192,768]{2,1,0:T(8,128)(2,1)S(1)}, u32[]{:S(2)}, u32[]{:S(2)}) %collective-permute-start.15) | collective-permute-done | bytes 589856 | tf_op jit(solution)/shard_map/ppermute | solution.py:433
  46.1 1.9 %collective-permute-start.12 = (bf16[2,24,1536]{2,1,0:T(8,128)(2,1)S(1)}, bf16[2,24,1536]{2,1,0:T(8,128)(2,1)S(1)}, u32[]{:S(2)}, u32[]{:S(2)}) collective-permute-start(bf16[2,24,1536]{2,1,0:T(8,128)(2,1)S(1)} %pair_kernel.1.refs_5_.refs_1_), channel_id=1, source_target_pairs={{0,16},{1,17},{2,18},{3,19},{4,20},{5,21},{6,22},{7,23},{8,24},{9,... | collective-permute-start | bytes 442376 | tf_op jit(solution)/shard_map/ppermute | solution.py:433
  51.3 4.1 %collective-permute-done.12.refs_3_ = bf16[2,24,1536]{2,1,0:T(8,128)(2,1)S(1)} collective-permute-done((bf16[2,24,1536]{2,1,0:T(8,128)(2,1)S(1)}, bf16[2,24,1536]{2,1,0:T(8,128)(2,1)S(1)}, u32[]{:S(2)}, u32[]{:S(2)}) %collective-permute-start.12) | collective-permute-done | bytes 147488 | tf_op jit(solution)/shard_map/ppermute | solution.py:433
  55.4 2.8 %collective-permute-start.17 = (bf16[192,768]{1,0:T(8,128)(2,1)S(1)}, bf16[192,768]{1,0:T(8,128)(2,1)S(1)}, u32[]{:S(2)}, u32[]{:S(2)}) collective-permute-start(bf16[192,768]{1,0:T(8,128)(2,1)S(1)} %get-tuple-element.50.refs_3_), channel_id=1, source_target_pairs={{0,4},{1,5},{2,6},{3,7},{4,0},{5,1},{6,2},{7,3},{8,12},{9,13},{10,... | collective-permute-start | bytes 884744 | tf_op jit(solution)/shard_map/ppermute | solution.py:433
  58.8 1.6 %collective-permute-done.10.other = bf16[2,192,768]{2,1,0:T(8,128)(2,1)S(1)} collective-permute-done((bf16[2,192,768]{2,1,0:T(8,128)(2,1)S(1)}, bf16[2,192,768]{2,1,0:T(8,128)(2,1)S(1)}, u32[]{:S(2)}, u32[]{:S(2)}) %collective-permute-start.10) | collective-permute-done | bytes 589856 | tf_op jit(solution)/shard_map/ppermute | solution.py:433
  60.4 4.8 %in_total0.1 = (bf16[1024,768]{1,0:T(8,128)(2,1)S(1)}, bf16[4,2,48,768]{3,2,1,0:T(8,128)(2,1)S(1)}, f32[4,2,48,768]{3,2,1,0:T(8,128)S(1)}) custom-call(s32[6]{0:T(128)S(1)} %copy-done.12, bf16[512,768]{1,0:T(8,128)(2,1)S(1)} %copy-done.3, bf16[512,768]{1,0:T(8,128)(2,1)S(1)} %copy-done.5, bf16[512,768]{1,0:T(8,128)(2,1)S(1)} %copy-done.15, ...), custom_call_target="tpu_custom_call" | custom-call | flops 2415919104 | bytes 16777216 | tf_op jit(solution)/shard_map/in_total0/pallas_call | solution.py:345
  67.5 4.8 %in_total1.1 = (bf16[1024,768]{1,0:T(8,128)(2,1)S(1)}, bf16[4,2,48,768]{3,2,1,0:T(8,128)(2,1)S(1)}, f32[4,2,48,768]{3,2,1,0:T(8,128)S(1)}) custom-call(s32[6]{0:T(128)S(1)} %copy-done.12, bf16[512,768]{1,0:T(8,128)(2,1)S(1)} %copy-done.3, bf16[512,768]{1,0:T(8,128)(2,1)S(1)} %copy-done.5, bf16[512,768]{1,0:T(8,128)(2,1)S(1)} %copy-done.15, ...), custom_call_target="tpu_custom_call" | custom-call | flops 2415919104 | bytes 16777216 | tf_op jit(solution)/shard_map/in_total1/pallas_call | solution.py:345
  72.4 6.5 %collective-permute-start.25 = (bf16[96,768]{1,0:T(8,128)(2,1)S(1)}, bf16[96,768]{1,0:T(8,128)(2,1)S(1)}, u32[]{:S(2)}, u32[]{:S(2)}) collective-permute-start(bf16[96,768]{1,0:T(8,128)(2,1)S(1)} %get-tuple-element.59._), channel_id=1, source_target_pairs={{0,0},{1,16},{2,2},{3,18},{4,4},{5,20},{6,6},{7,22},{8,8},{9,24},{... | collective-permute-start | bytes 442376 | tf_op jit(solution)/shard_map/ppermute | solution.py:433
  82.1 2.1 %collective-permute-done.23.refs_2_ = bf16[4,2,48,768]{3,2,1,0:T(8,128)(2,1)S(1)} collective-permute-done((bf16[4,2,48,768]{3,2,1,0:T(8,128)(2,1)S(1)}, bf16[4,2,48,768]{3,2,1,0:T(8,128)(2,1)S(1)}, u32[]{:S(2)}, u32[]{:S(2)}) %collective-permute-start.23) | collective-permute-done | bytes 589856 | tf_op jit(solution)/shard_map/ppermute | solution.py:433
  84.8 2.2 %collective-permute-start.24 = (bf16[4,48,768]{2,1,0:T(8,128)(2,1)S(1)}, bf16[4,48,768]{2,1,0:T(8,128)(2,1)S(1)}, u32[]{:S(2)}, u32[]{:S(2)}) collective-permute-start(bf16[4,48,768]{2,1,0:T(8,128)(2,1)S(1)} %get-tuple-element.68.refs_6_), channel_id=1, source_target_pairs={{0,2},{1,3},{2,0},{3,1},{4,6},{5,7},{6,4},{7,5},{8,10},{9,11},{10,... | collective-permute-start | bytes 884744 | tf_op jit(solution)/shard_map/ppermute | solution.py:433
  87.3 5.4 %collective-permute-start.28 = (bf16[96,768]{1,0:T(8,128)(2,1)S(1)}, bf16[96,768]{1,0:T(8,128)(2,1)S(1)}, u32[]{:S(2)}, u32[]{:S(2)}) collective-permute-start(bf16[96,768]{1,0:T(8,128)(2,1)S(1)} %get-tuple-element.72), channel_id=1, source_target_pairs={{0,9},{1,25},{2,11},{3,27},{4,13},{5,29},{6,15},{7,31},{8,1},{9,17... | collective-permute-start | bytes 442376 | tf_op jit(solution)/shard_map/ppermute | solution.py:433
  92.6 6.3 %collective-permute-done.28.refs_5_ = bf16[96,768]{1,0:T(8,128)(2,1)S(1)} collective-permute-done((bf16[96,768]{1,0:T(8,128)(2,1)S(1)}, bf16[96,768]{1,0:T(8,128)(2,1)S(1)}, u32[]{:S(2)}, u32[]{:S(2)}) %collective-permute-start.28) | collective-permute-done | bytes 147488 | tf_op jit(solution)/shard_map/ppermute | solution.py:433
  104.8 2.0 %collective-permute-start.34 = (bf16[48,1536]{1,0:T(8,128)(2,1)S(1)}, bf16[48,1536]{1,0:T(8,128)(2,1)S(1)}, u32[]{:S(2)}, u32[]{:S(2)}) collective-permute-start(bf16[48,1536]{1,0:T(8,128)(2,1)S(1)} %get-tuple-element.78), channel_id=1, source_target_pairs={{0,24},{1,25},{2,26},{3,27},{4,28},{5,29},{6,30},{7,31},{8,16},{9,... | collective-permute-start | bytes 442376 | tf_op jit(solution)/shard_map/ppermute | solution.py:433
  106.8 7.7 %collective-permute-done.29.a1 = bf16[2,4,48,768]{3,2,1,0:T(8,128)(2,1)S(1)} collective-permute-done((bf16[2,4,48,768]{3,2,1,0:T(8,128)(2,1)S(1)}, bf16[2,4,48,768]{3,2,1,0:T(8,128)(2,1)S(1)}, u32[]{:S(2)}, u32[]{:S(2)}) %collective-permute-start.29) | collective-permute-done | bytes 589856 | tf_op jit(solution)/shard_map/ppermute | solution.py:433
  114.5 2.3 %input_part1.1.refs_5_ = f32[512,768]{1,0:T(8,128)S(1)} custom-call(s32[6]{0:T(128)S(1)} %copy-done.12, bf16[1024,768]{1,0:T(8,128)(2,1)S(1)} %get-tuple-element.53.g0, bf16[1024,768]{1,0:T(8,128)(2,1)S(1)} %get-tuple-element.60.g1, bf16[2,4,48,768]{3,2,1,0:T(8,128)(2,1)S(1)} %get-tuple-element.74.a0.refs_0_, ...), custom_call_target="tpu_custom_call" | custom-call | flops 1207959552 | bytes 6291456 | tf_op jit(solution)/shard_map/input_part1/pallas_call | solution.py:395
  116.8 4.3 %collective-permute-start.31 = (f32[512,768]{1,0:T(8,128)S(1)}, f32[512,768]{1,0:T(8,128)S(1)}, u32[]{:S(2)}, u32[]{:S(2)}) collective-permute-start(f32[512,768]{1,0:T(8,128)S(1)} %input_part1.1.refs_5_), channel_id=1, source_target_pairs={{0,1},{1,0},{2,3},{3,2},{4,5},{5,4},{6,7},{7,6},{8,9},{9,8},{10,11... | collective-permute-start | bytes 4718600 | tf_op jit(solution)/shard_map/ppermute | solution.py:433
  121.9 2.5 %collective-permute-done.35.refs_2_ = f32[24,1536]{1,0:T(8,128)S(1)} collective-permute-done((f32[24,1536]{1,0:T(8,128)S(1)}, f32[24,1536]{1,0:T(8,128)S(1)}, u32[]{:S(2)}, u32[]{:S(2)}) %collective-permute-start.35) | collective-permute-done | bytes 147488 | tf_op jit(solution)/shard_map/ppermute | solution.py:433
  126.6 3.2 %input_part0.1 = f32[512,768]{1,0:T(8,128)} custom-call(s32[6]{0:T(128)S(1)} %copy-done.12, bf16[1024,768]{1,0:T(8,128)(2,1)S(1)} %get-tuple-element.53.g0, bf16[1024,768]{1,0:T(8,128)(2,1)S(1)} %get-tuple-element.60.g1, bf16[2,4,48,768]{3,2,1,0:T(8,128)(2,1)S(1)} %get-tuple-element.74.a0.refs_0_, bf16[2,4,48,768]{3,2,1,0:T(8,128)(2,1)S(1)} %collective-permute-done.29.a1, ...), custom_call_target="tpu_custom_call" | custom-call | flops 1207959552 | bytes 6291456 | tf_op jit(solution)/shard_map/input_part0/pallas_call | solution.py:395
  (101 shorter events, 30.5 us)
Async XLA Ops:
  0.6 11.8 %collective-permute-start.2 = (bf16[512,3072]{1,0:T(8,128)(2,1)}, bf16[512,3072]{1,0:T(8,128)(2,1)S(1)}, u32[]{:S(2)}, u32[]{:S(2)}) collective-permute-start(bf16[512,3072]{1,0:T(8,128)(2,1)} %pre_ref.3), channel_id=1, source_target_pairs={{0,1},{1,0},{2,3},{3,2},{4,5},{5,4},{6,7},{7,6},{8,9},{9,8},{10,11... | collective-permute-start | bytes 9437192 | tf_op jit(solution)/shard_map/ppermute | solution.py:433
  1.3 20.5 %collective-permute-start.7 = (bf16[24,3072]{1,0:T(8,128)(2,1)}, bf16[24,3072]{1,0:T(8,128)(2,1)S(1)}, u32[]{:S(2)}, u32[]{:S(2)}) collective-permute-start(bf16[24,3072]{1,0:T(8,128)(2,1)} %refs_1_.1), channel_id=1, source_target_pairs={{0,1},{1,0},{2,3},{3,2},{4,5},{5,4},{6,7},{7,6},{8,9},{9,8},{10,11... | collective-permute-start | bytes 442376 | tf_op jit(solution)/shard_map/ppermute | solution.py:433
  1.7 21.8 %collective-permute-start.3 = (bf16[96,768]{1,0:T(8,128)(2,1)}, bf16[96,768]{1,0:T(8,128)(2,1)S(1)}, u32[]{:S(2)}, u32[]{:S(2)}) collective-permute-start(bf16[96,768]{1,0:T(8,128)(2,1)} %param.8), channel_id=1, source_target_pairs={{0,0},{1,16},{2,2},{3,18},{4,4},{5,20},{6,6},{7,22},{8,8},{9,24},{... | collective-permute-start | bytes 442376 | tf_op jit(solution)/shard_map/ppermute | solution.py:433
  7.7 15.9 %collective-permute-start.4 = (bf16[96,768]{1,0:T(8,128)(2,1)}, bf16[96,768]{1,0:T(8,128)(2,1)}, u32[]{:S(2)}, u32[]{:S(2)}) collective-permute-start(bf16[96,768]{1,0:T(8,128)(2,1)} %param.8), channel_id=1, source_target_pairs={{0,8},{1,24},{2,10},{3,26},{4,12},{5,28},{6,14},{7,30},{8,0},{9,16... | collective-permute-start | bytes 442376 | tf_op jit(solution)/shard_map/ppermute | solution.py:433
  27.3 18.9 %collective-permute-start.15 = (bf16[2,192,768]{2,1,0:T(8,128)(2,1)}, bf16[2,192,768]{2,1,0:T(8,128)(2,1)S(1)}, u32[]{:S(2)}, u32[]{:S(2)}) collective-permute-start(bf16[2,192,768]{2,1,0:T(8,128)(2,1)} %get-tuple-element.43.refs_3_), channel_id=1, source_target_pairs={{0,2},{1,3},{2,0},{3,1},{4,6},{5,7},{6,4},{7,5},{8,10},{9,11},{10,... | collective-permute-start | bytes 1769480 | tf_op jit(solution)/shard_map/ppermute | solution.py:433
  33.7 14.3 %collective-permute-start.14 = (bf16[2,192,768]{2,1,0:T(8,128)(2,1)S(1)}, bf16[2,192,768]{2,1,0:T(8,128)(2,1)S(1)}, u32[]{:S(2)}, u32[]{:S(2)}) collective-permute-start(bf16[2,192,768]{2,1,0:T(8,128)(2,1)S(1)} %get-tuple-element.46.refs_5_), channel_id=1, source_target_pairs={{0,4},{1,5},{2,6},{3,7},{4,0},{5,1},{6,2},{7,3},{8,12},{9,13},{10,... | collective-permute-start | bytes 1769480 | tf_op jit(solution)/shard_map/ppermute | solution.py:433
  35.0 25.4 %collective-permute-start.10 = (bf16[2,192,768]{2,1,0:T(8,128)(2,1)S(1)}, bf16[2,192,768]{2,1,0:T(8,128)(2,1)S(1)}, u32[]{:S(2)}, u32[]{:S(2)}) collective-permute-start(bf16[2,192,768]{2,1,0:T(8,128)(2,1)S(1)} %get-tuple-element.47.refs_3_.mine), channel_id=1, source_target_pairs={{0,4},{1,5},{2,6},{3,7},{4,0},{5,1},{6,2},{7,3},{8,12},{9,13},{10,... | collective-permute-start | bytes 1769480 | tf_op jit(solution)/shard_map/ppermute | solution.py:433
  36.3 31.2 %collective-permute-start.16 = (bf16[2,192,768]{2,1,0:T(8,128)(2,1)S(1)}, bf16[2,192,768]{2,1,0:T(8,128)(2,1)S(1)}, u32[]{:S(2)}, u32[]{:S(2)}) collective-permute-start(bf16[2,192,768]{2,1,0:T(8,128)(2,1)S(1)} %get-tuple-element.55.mine), channel_id=1, source_target_pairs={{0,2},{1,3},{2,0},{3,1},{4,6},{5,7},{6,4},{7,5},{8,10},{9,11},{10,... | collective-permute-start | bytes 1769480 | tf_op jit(solution)/shard_map/ppermute | solution.py:433
  37.1 12.9 %collective-permute-start.11 = (bf16[2,24,1536]{2,1,0:T(8,128)(2,1)S(1)}, bf16[2,24,1536]{2,1,0:T(8,128)(2,1)S(1)}, u32[]{:S(2)}, u32[]{:S(2)}) collective-permute-start(bf16[2,24,1536]{2,1,0:T(8,128)(2,1)S(1)} %pair_kernel.1.refs_5_.refs_1_), channel_id=1, source_target_pairs={{0,8},{1,9},{2,10},{3,11},{4,12},{5,13},{6,14},{7,15},{8,0},{9,1},... | collective-permute-start | bytes 442376 | tf_op jit(solution)/shard_map/ppermute | solution.py:433
  50.0 16.5 %collective-permute-start.18 = (bf16[192,768]{1,0:T(8,128)(2,1)S(1)}, bf16[192,768]{1,0:T(8,128)(2,1)S(1)}, u32[]{:S(2)}, u32[]{:S(2)}) collective-permute-start(bf16[192,768]{1,0:T(8,128)(2,1)S(1)} %get-tuple-element.51.refs_5_), channel_id=1, source_target_pairs={{0,2},{1,3},{2,0},{3,1},{4,6},{5,7},{6,4},{7,5},{8,10},{9,11},{10,... | collective-permute-start | bytes 884744 | tf_op jit(solution)/shard_map/ppermute | solution.py:433
  55.4 11.3 %collective-permute-start.17 = (bf16[192,768]{1,0:T(8,128)(2,1)S(1)}, bf16[192,768]{1,0:T(8,128)(2,1)S(1)}, u32[]{:S(2)}, u32[]{:S(2)}) collective-permute-start(bf16[192,768]{1,0:T(8,128)(2,1)S(1)} %get-tuple-element.50.refs_3_), channel_id=1, source_target_pairs={{0,4},{1,5},{2,6},{3,7},{4,0},{5,1},{6,2},{7,3},{8,12},{9,13},{10,... | collective-permute-start | bytes 884744 | tf_op jit(solution)/shard_map/ppermute | solution.py:433
  65.2 14.9 %collective-permute-start.21 = (bf16[4,2,48,768]{3,2,1,0:T(8,128)(2,1)S(1)}, bf16[4,2,48,768]{3,2,1,0:T(8,128)(2,1)S(1)}, u32[]{:S(2)}, u32[]{:S(2)}) collective-permute-start(bf16[4,2,48,768]{3,2,1,0:T(8,128)(2,1)S(1)} %get-tuple-element.58.refs_5_), channel_id=1, source_target_pairs={{0,2},{1,3},{2,0},{3,1},{4,6},{5,7},{6,4},{7,5},{8,10},{9,11},{10,... | collective-permute-start | bytes 1769480 | tf_op jit(solution)/shard_map/ppermute | solution.py:433
  72.3 11.8 %collective-permute-start.23 = (bf16[4,2,48,768]{3,2,1,0:T(8,128)(2,1)S(1)}, bf16[4,2,48,768]{3,2,1,0:T(8,128)(2,1)S(1)}, u32[]{:S(2)}, u32[]{:S(2)}) collective-permute-start(bf16[4,2,48,768]{3,2,1,0:T(8,128)(2,1)S(1)} %get-tuple-element.63.refs_3_), channel_id=1, source_target_pairs={{0,4},{1,5},{2,6},{3,7},{4,0},{5,1},{6,2},{7,3},{8,12},{9,13},{10,... | collective-permute-start | bytes 1769480 | tf_op jit(solution)/shard_map/ppermute | solution.py:433
  72.4 14.6 %collective-permute-start.25 = (bf16[96,768]{1,0:T(8,128)(2,1)S(1)}, bf16[96,768]{1,0:T(8,128)(2,1)S(1)}, u32[]{:S(2)}, u32[]{:S(2)}) collective-permute-start(bf16[96,768]{1,0:T(8,128)(2,1)S(1)} %get-tuple-element.59._), channel_id=1, source_target_pairs={{0,0},{1,16},{2,2},{3,18},{4,4},{5,20},{6,6},{7,22},{8,8},{9,24},{... | collective-permute-start | bytes 442376 | tf_op jit(solution)/shard_map/ppermute | solution.py:433
  80.8 19.6 %collective-permute-start.22 = (bf16[4,48,768]{2,1,0:T(8,128)(2,1)S(1)}, bf16[4,48,768]{2,1,0:T(8,128)(2,1)S(1)}, u32[]{:S(2)}, u32[]{:S(2)}) collective-permute-start(bf16[4,48,768]{2,1,0:T(8,128)(2,1)S(1)} %get-tuple-element.65.refs_3_), channel_id=1, source_target_pairs={{0,4},{1,5},{2,6},{3,7},{4,0},{5,1},{6,2},{7,3},{8,12},{9,13},{10,... | collective-permute-start | bytes 884744 | tf_op jit(solution)/shard_map/ppermute | solution.py:433
  84.8 15.5 %collective-permute-start.24 = (bf16[4,48,768]{2,1,0:T(8,128)(2,1)S(1)}, bf16[4,48,768]{2,1,0:T(8,128)(2,1)S(1)}, u32[]{:S(2)}, u32[]{:S(2)}) collective-permute-start(bf16[4,48,768]{2,1,0:T(8,128)(2,1)S(1)} %get-tuple-element.68.refs_6_), channel_id=1, source_target_pairs={{0,2},{1,3},{2,0},{3,1},{4,6},{5,7},{6,4},{7,5},{8,10},{9,11},{10,... | collective-permute-start | bytes 884744 | tf_op jit(solution)/shard_map/ppermute | solution.py:433
  87.0 15.0 %collective-permute-start.19 = (bf16[4,48,768]{2,1,0:T(8,128)(2,1)S(1)}, bf16[4,48,768]{2,1,0:T(8,128)(2,1)S(1)}, u32[]{:S(2)}, u32[]{:S(2)}) collective-permute-start(bf16[4,48,768]{2,1,0:T(8,128)(2,1)S(1)} %get-tuple-element.52._.refs_1_), channel_id=1, source_target_pairs={{0,2},{1,3},{2,0},{3,1},{4,6},{5,7},{6,4},{7,5},{8,10},{9,11},{10,... | collective-permute-start | bytes 884744 | tf_op jit(solution)/shard_map/ppermute | solution.py:433
  87.1 14.9 %collective-permute-start.20 = (bf16[4,48,768]{2,1,0:T(8,128)(2,1)S(1)}, bf16[4,48,768]{2,1,0:T(8,128)(2,1)S(1)}, u32[]{:S(2)}, u32[]{:S(2)}) collective-permute-start(bf16[4,48,768]{2,1,0:T(8,128)(2,1)S(1)} %get-tuple-element.61.refs_3_), channel_id=1, source_target_pairs={{0,4},{1,5},{2,6},{3,7},{4,0},{5,1},{6,2},{7,3},{8,12},{9,13},{10,... | collective-permute-start | bytes 884744 | tf_op jit(solution)/shard_map/ppermute | solution.py:433
  87.3 11.7 %collective-permute-start.28 = (bf16[96,768]{1,0:T(8,128)(2,1)S(1)}, bf16[96,768]{1,0:T(8,128)(2,1)S(1)}, u32[]{:S(2)}, u32[]{:S(2)}) collective-permute-start(bf16[96,768]{1,0:T(8,128)(2,1)S(1)} %get-tuple-element.72), channel_id=1, source_target_pairs={{0,9},{1,25},{2,11},{3,27},{4,13},{5,29},{6,15},{7,31},{8,1},{9,17... | collective-permute-start | bytes 442376 | tf_op jit(solution)/shard_map/ppermute | solution.py:433
  102.7 11.8 %collective-permute-start.29 = (bf16[2,4,48,768]{3,2,1,0:T(8,128)(2,1)S(1)}, bf16[2,4,48,768]{3,2,1,0:T(8,128)(2,1)S(1)}, u32[]{:S(2)}, u32[]{:S(2)}) collective-permute-start(bf16[2,4,48,768]{3,2,1,0:T(8,128)(2,1)S(1)} %get-tuple-element.74.a0.refs_0_), channel_id=1, source_target_pairs={{0,4},{1,5},{2,6},{3,7},{4,0},{5,1},{6,2},{7,3},{8,12},{9,13},{10,... | collective-permute-start | bytes 1769480 | tf_op jit(solution)/shard_map/ppermute | solution.py:433
  103.0 11.5 %collective-permute-start.30 = (bf16[2,4,48,768]{3,2,1,0:T(8,128)(2,1)S(1)}, bf16[2,4,48,768]{3,2,1,0:T(8,128)(2,1)S(1)}, u32[]{:S(2)}, u32[]{:S(2)}) collective-permute-start(bf16[2,4,48,768]{3,2,1,0:T(8,128)(2,1)S(1)} %get-tuple-element.75.b0), channel_id=1, source_target_pairs={{0,2},{1,3},{2,0},{3,1},{4,6},{5,7},{6,4},{7,5},{8,10},{9,11},{10,... | collective-permute-start | bytes 1769480 | tf_op jit(solution)/shard_map/ppermute | solution.py:433
  103.2 17.9 %collective-permute-start.32 = (bf16[48,1536]{1,0:T(8,128)(2,1)S(1)}, bf16[48,1536]{1,0:T(8,128)(2,1)S(1)}, u32[]{:S(2)}, u32[]{:S(2)}) collective-permute-start(bf16[48,1536]{1,0:T(8,128)(2,1)S(1)} %get-tuple-element.73.refs_5_), channel_id=1, source_target_pairs={{0,8},{1,9},{2,10},{3,11},{4,12},{5,13},{6,14},{7,15},{8,0},{9,1},... | collective-permute-start | bytes 442376 | tf_op jit(solution)/shard_map/ppermute | solution.py:433
  104.7 16.5 %collective-permute-start.33 = (bf16[48,1536]{1,0:T(8,128)(2,1)S(1)}, bf16[48,1536]{1,0:T(8,128)(2,1)S(1)}, u32[]{:S(2)}, u32[]{:S(2)}) collective-permute-start(bf16[48,1536]{1,0:T(8,128)(2,1)S(1)} %get-tuple-element.77), channel_id=1, source_target_pairs={{0,16},{1,17},{2,18},{3,19},{4,20},{5,21},{6,22},{7,23},{8,24},{9,... | collective-permute-start | bytes 442376 | tf_op jit(solution)/shard_map/ppermute | solution.py:433
  104.8 16.3 %collective-permute-start.34 = (bf16[48,1536]{1,0:T(8,128)(2,1)S(1)}, bf16[48,1536]{1,0:T(8,128)(2,1)S(1)}, u32[]{:S(2)}, u32[]{:S(2)}) collective-permute-start(bf16[48,1536]{1,0:T(8,128)(2,1)S(1)} %get-tuple-element.78), channel_id=1, source_target_pairs={{0,24},{1,25},{2,26},{3,27},{4,28},{5,29},{6,30},{7,31},{8,16},{9,... | collective-permute-start | bytes 442376 | tf_op jit(solution)/shard_map/ppermute | solution.py:433
  (28 other events, 205.3 us)

commit v4 on v3

--- a/solution.py
+++ b/solution.py
@@ -511,36 +511,43 @@
 
     in_cut(0, [ones, ones_got])
 
-    def out_parts(at, k1, r1, k2, r2, o00, o01, o10, o11, own, total):
-        high, low = at[4], at[5]
+    def out_parts(at, k1, r1, k2, r2, o0, o1, own, total):
+        high = at[4]
         total[0] = (k1[...] + r1[...].astype(F32)).reshape(2, rows_out, width)
         total[1] = (k2[...] + r2[...].astype(F32)).reshape(2, rows_out, width)
-        own[...] = total[low, high]
-        o00[...] = total[low, high].astype(BF)
-        o01[...] = total[1 - low, high].astype(BF)
-        o10[...] = total[low, 1 - high].astype(BF)
-        o11[...] = total[1 - low, 1 - high].astype(BF)
-
-    row = (rows_out, width)
+        own[...] = total[:, high]
+        o0[...] = total[:, high].astype(BF)
+        o1[...] = total[:, 1 - high].astype(BF)
+
+    both = (2, rows_out, width)
     *out_got, out_own = kernel(
         out_parts,
         [*out_sides[0], *out_sides[1]],
-        [shape(row, BF)] * 4 + [shape(row, F32)],
+        [shape(both, BF)] * 2 + [shape(both, F32)],
         [pltpu.VMEM((2, 2, rows_out, width), F32)],
     )
-    out_got = [send(p, scatter_perm(*divmod(k, 2))) for k, p in enumerate(out_got)]
+    out_got = [send(p, scatter_perm(i, 0)) for i, p in enumerate(out_got)]
 
     in_cut(1, [twos, twos_got])
 
     one, one_got = middle(in_kept[0], in_sent[0], along_y, 1, 1)
     two, two_got = middle(in_kept[1], in_sent[1], along_x, 2, 1)
 
-    def out_sum(at, own, r00, r01, r10, r11, out):
-        first = jnp.where(at[3] == at[4], own[...], r00[...].astype(F32))
-        rest = r01[...].astype(F32) + r10[...].astype(F32) + r11[...].astype(F32)
-        out[...] = (first + rest) * grad_scale
-
-    (w_out_grad,) = kernel(out_sum, [out_own] + out_got, [shape(out_own.shape, F32)])
+    def out_middle(at, own, r0, r1, out, keep, total):
+        high, low = at[4], at[5]
+        total[...] = jnp.where(at[3] == high, own[...], r0[...].astype(F32)) + r1[...].astype(F32)
+        out[...] = total[1 - low].astype(BF)
+        keep[...] = total[low]
+
+    row = (rows_out, width)
+    out_got, out_own = kernel(
+        out_middle,
+        [out_own] + out_got,
+        [shape(row, BF), shape(row, F32)],
+        [pltpu.VMEM(both, F32)],
+    )
+    out_got = send(out_got, z_perm(1))
+
 
     def in_parts(at, k1, r1, k2, r2, *outs):
         z = at[0]
@@ -560,11 +567,17 @@
     )
     in_got = [send(p, z_perm(k)) for p, k in zip(in_got, range(1, nz))]
 
+    def out_sum(at, own, got, out):
+        out[...] = (own[...] + got[...].astype(F32)) * grad_scale
+
+    (w_out_grad,) = kernel(out_sum, [out_own, out_got], [shape(out_own.shape, F32)])
+
     ones, twos = join(*in_pieces)
     in_pieces = [ones, send(ones, along_y), twos, send(twos, along_x)]
 
     (part,) = order([input_part(at, 1, pre_grads, in_pieces, nz, order.after)])
     part_got = send(part, z_perm(0, 1))
+    (part_own,) = order([input_part(at, 0, pre_grads, in_pieces, nz, order.after)])
 
     def in_sum(at, own, r1, r2, r3, mine, other):
         total = own[...] + r1[...].astype(F32) + r2[...].astype(F32) + r3[...].astype(F32)
@@ -583,7 +596,10 @@
         out[:, half:] = jnp.where(c == 0, other[...], mine[...])
 
     (w_in_grad,) = kernel(in_join, [mine, other], [shape((rows_in, hidden), F32)])
-    input_grad = input_part(at, 0, pre_grads, in_pieces, nz, order.after, part_got)
+    def input_sum(at, mine, other, out):
+        out[...] = mine[...] + other[...]
+
+    (input_grad,) = kernel(input_sum, [part_own, part_got], [shape((tokens, width), F32)])
     return (input_grad, w_out_grad, w_in_grad)
 
 

time: 131 us -> 128 us (0.977)
  waiting for transfers between devices: 34.3 us -> 30.9 us
  Pallas kernels: 37.2 us -> 38.8 us
    ppermute x36 -> x35, waiting for transfers between devices: 34.3 us -> 30.9 us  [send(): return lax.ppermute(array, AXIS, perm)]
    pallas_call x14 -> x16, Pallas kernels: 10.8 us -> 13.3 us  [small(): pl.pallas_call(run, name=name or body.__name__, out_shape=outs, in_specs=...]
    ppermute x36 -> x35, starting transfers between devices: 51.7 us -> 51.3 us  [send(): return lax.ppermute(array, AXIS, perm)]
  transfers between devices with their start and end apart: 36 -> 35, of which waited for: 10 -> 12; matrix products, arithmetic and copies ran while one was open for 1% -> 1% of each run, Pallas kernels for 25% -> 28%
where the time goes in v4:
time: 128 us
  starting transfers between devices  51.3 us (40%)
  Pallas kernels  38.8 us (30%)
  waiting for transfers between devices  30.9 us (24%)
  local copies, waits for them, and re-layouts  5.71 us (4%)
    ppermute x35, starting transfers between devices, send(): return lax.ppermute(array, AXIS, perm)  51.3 us
    ppermute x35, waiting for transfers between devices, send(): return lax.ppermute(array, AXIS, perm)  30.9 us
    pallas_call x16, Pallas kernels, small(): pl.pallas_call(run, name=name or body.__name__, out_shape=outs, in_specs=...  13.3 us
    pallas_call x2, Pallas kernels, out_total(): pl.pallas_call(body, name=f'out_total{cut}', grid_spec=pltpu.PrefetchScal...  11.2 us
    pallas_call x2, Pallas kernels, in_total(): pl.pallas_call(body, name=f'in_total{cut}', grid_spec=pltpu.PrefetchScala...  9.58 us
    unnamed x32, local copies, waits for them, and re-layouts  5.03 us
    pallas_call x2, Pallas kernels, input_part(): pl.pallas_call(body, name=f'input_part{part}', grid_spec=pltpu.PrefetchSc...  4.69 us
  transfers between devices with their start and end apart: 35, of which 12 were waited for; matrix products, arithmetic and copies ran while one was open for 1% of the time, Pallas kernels for 28%

profile of v4, /device:TPU:1, one launch (start us, length us, event | category | flops | bytes accessed | tf_op | source)
XLA Modules:
  0.0 127.7 jit_solution(1018790619527583507)
XLA Ops:
  1.7 5.6 %collective-permute-start.3 = (bf16[96,768]{1,0:T(8,128)(2,1)}, bf16[96,768]{1,0:T(8,128)(2,1)S(1)}, u32[]{:S(2)}, u32[]{:S(2)}) collective-permute-start(bf16[96,768]{1,0:T(8,128)(2,1)} %param.8), channel_id=1, source_target_pairs={{0,0},{1,16},{2,2},{3,18},{4,4},{5,20},{6,6},{7,22},{8,8},{9,24},{... | collective-permute-start | bytes 442376 | tf_op jit(solution)/shard_map/ppermute | solution.py:433
  7.7 4.7 %collective-permute-start.4 = (bf16[96,768]{1,0:T(8,128)(2,1)}, bf16[96,768]{1,0:T(8,128)(2,1)}, u32[]{:S(2)}, u32[]{:S(2)}) collective-permute-start(bf16[96,768]{1,0:T(8,128)(2,1)} %param.8), channel_id=1, source_target_pairs={{0,8},{1,24},{2,10},{3,26},{4,12},{5,28},{6,14},{7,30},{8,0},{9,16... | collective-permute-start | bytes 442376 | tf_op jit(solution)/shard_map/ppermute | solution.py:433
  12.4 1.7 %collective-permute-start.6 = (bf16[96,768]{1,0:T(8,128)(2,1)}, bf16[96,768]{1,0:T(8,128)(2,1)}, u32[]{:S(2)}, u32[]{:S(2)}) collective-permute-start(bf16[96,768]{1,0:T(8,128)(2,1)} %param.8), channel_id=1, source_target_pairs={{0,24},{1,8},{2,26},{3,10},{4,28},{5,12},{6,30},{7,14},{8,16},{9,0... | collective-permute-start | bytes 442376 | tf_op jit(solution)/shard_map/ppermute | solution.py:433
  14.9 6.9 %out_total0.1 = (f32[1024,768]{1,0:T(8,128)}, bf16[2,192,768]{2,1,0:T(8,128)(2,1)}, f32[2,192,768]{2,1,0:T(8,128)}) custom-call(s32[6]{0:T(128)} %stack.27.at.refs_0_, bf16[512,3072]{1,0:T(8,128)(2,1)} %pre_ref.3, bf16[512,3072]{1,0:T(8,128)(2,1)} %copy-done.1, bf16[512,768]{1,0:T(8,128)(2,1)} %grad_ref.7, bf16[512,768]{1,0:T(8,128)(2,1)} %copy-done.4, ...), custom_call_target="tpu_custom_call" | custom-call | flops 1207959552 | bytes 20971520 | tf_op jit(solution)/shard_map/out_total0/pallas_call | solution.py:276
  27.5 1.9 %copy-done.2 = bf16[512,3072]{1,0:T(8,128)(2,1)S(1)} copy-done((bf16[512,3072]{1,0:T(8,128)(2,1)S(1)}, bf16[512,3072]{1,0:T(8,128)(2,1)}, u32[]{:S(2)}) %copy-start.2) | copy-done | bytes 3145752
  29.4 4.2 %out_total1.1 = (f32[1024,768]{1,0:T(8,128)S(1)}, bf16[2,192,768]{2,1,0:T(8,128)(2,1)S(1)}, f32[2,192,768]{2,1,0:T(8,128)S(1)}) custom-call(s32[6]{0:T(128)S(1)} %copy-done.12, bf16[512,3072]{1,0:T(8,128)(2,1)S(1)} %copy-done, bf16[512,3072]{1,0:T(8,128)(2,1)S(1)} %copy-done.2, bf16[512,768]{1,0:T(8,128)(2,1)S(1)} %copy-done.3, ...), custom_call_target="tpu_custom_call" | custom-call | flops 1207959552 | bytes 20971520 | tf_op jit(solution)/shard_map/out_total1/pallas_call | solution.py:276
  37.3 8.9 %collective-permute-done.15.refs_2_ = bf16[2,192,768]{2,1,0:T(8,128)(2,1)S(1)} collective-permute-done((bf16[2,192,768]{2,1,0:T(8,128)(2,1)}, bf16[2,192,768]{2,1,0:T(8,128)(2,1)S(1)}, u32[]{:S(2)}, u32[]{:S(2)}) %collective-permute-start.15) | collective-permute-done | bytes 589856 | tf_op jit(solution)/shard_map/ppermute | solution.py:433
  46.1 1.9 %collective-permute-start.12 = (bf16[2,24,1536]{2,1,0:T(8,128)(2,1)S(1)}, bf16[2,24,1536]{2,1,0:T(8,128)(2,1)S(1)}, u32[]{:S(2)}, u32[]{:S(2)}) collective-permute-start(bf16[2,24,1536]{2,1,0:T(8,128)(2,1)S(1)} %pair_kernel.1.refs_5_.refs_1_), channel_id=1, source_target_pairs={{0,16},{1,17},{2,18},{3,19},{4,20},{5,21},{6,22},{7,23},{8,24},{9,... | collective-permute-start | bytes 442376 | tf_op jit(solution)/shard_map/ppermute | solution.py:433
  51.3 4.1 %collective-permute-done.12.refs_3_ = bf16[2,24,1536]{2,1,0:T(8,128)(2,1)S(1)} collective-permute-done((bf16[2,24,1536]{2,1,0:T(8,128)(2,1)S(1)}, bf16[2,24,1536]{2,1,0:T(8,128)(2,1)S(1)}, u32[]{:S(2)}, u32[]{:S(2)}) %collective-permute-start.12) | collective-permute-done | bytes 147488 | tf_op jit(solution)/shard_map/ppermute | solution.py:433
  55.4 2.8 %collective-permute-start.17 = (bf16[192,768]{1,0:T(8,128)(2,1)S(1)}, bf16[192,768]{1,0:T(8,128)(2,1)S(1)}, u32[]{:S(2)}, u32[]{:S(2)}) collective-permute-start(bf16[192,768]{1,0:T(8,128)(2,1)S(1)} %get-tuple-element.50.refs_3_), channel_id=1, source_target_pairs={{0,4},{1,5},{2,6},{3,7},{4,0},{5,1},{6,2},{7,3},{8,12},{9,13},{10,... | collective-permute-start | bytes 884744 | tf_op jit(solution)/shard_map/ppermute | solution.py:433
  60.4 4.8 %in_total0.1 = (bf16[1024,768]{1,0:T(8,128)(2,1)S(1)}, bf16[4,2,48,768]{3,2,1,0:T(8,128)(2,1)S(1)}, f32[4,2,48,768]{3,2,1,0:T(8,128)S(1)}) custom-call(s32[6]{0:T(128)S(1)} %copy-done.12, bf16[512,768]{1,0:T(8,128)(2,1)S(1)} %copy-done.3, bf16[512,768]{1,0:T(8,128)(2,1)S(1)} %copy-done.5, bf16[512,768]{1,0:T(8,128)(2,1)S(1)} %copy-done.15, ...), custom_call_target="tpu_custom_call" | custom-call | flops 2415919104 | bytes 16777216 | tf_op jit(solution)/shard_map/in_total0/pallas_call | solution.py:345
  67.5 4.8 %in_total1.1 = (bf16[1024,768]{1,0:T(8,128)(2,1)S(1)}, bf16[4,2,48,768]{3,2,1,0:T(8,128)(2,1)S(1)}, f32[4,2,48,768]{3,2,1,0:T(8,128)S(1)}) custom-call(s32[6]{0:T(128)S(1)} %copy-done.12, bf16[512,768]{1,0:T(8,128)(2,1)S(1)} %copy-done.3, bf16[512,768]{1,0:T(8,128)(2,1)S(1)} %copy-done.5, bf16[512,768]{1,0:T(8,128)(2,1)S(1)} %copy-done.15, ...), custom_call_target="tpu_custom_call" | custom-call | flops 2415919104 | bytes 16777216 | tf_op jit(solution)/shard_map/in_total1/pallas_call | solution.py:345
  72.4 6.5 %collective-permute-start.21 = (bf16[2,96,768]{2,1,0:T(8,128)(2,1)S(1)}, bf16[2,96,768]{2,1,0:T(8,128)(2,1)S(1)}, u32[]{:S(2)}, u32[]{:S(2)}) collective-permute-start(bf16[2,96,768]{2,1,0:T(8,128)(2,1)S(1)} %get-tuple-element.59._), channel_id=1, source_target_pairs={{0,0},{1,16},{2,2},{3,18},{4,4},{5,20},{6,6},{7,22},{8,8},{9,24},{... | collective-permute-start | bytes 884744 | tf_op jit(solution)/shard_map/ppermute | solution.py:433
  81.1 3.1 %collective-permute-done.23.refs_2_ = bf16[4,2,48,768]{3,2,1,0:T(8,128)(2,1)S(1)} collective-permute-done((bf16[4,2,48,768]{3,2,1,0:T(8,128)(2,1)S(1)}, bf16[4,2,48,768]{3,2,1,0:T(8,128)(2,1)S(1)}, u32[]{:S(2)}, u32[]{:S(2)}) %collective-permute-start.23) | collective-permute-done | bytes 589856 | tf_op jit(solution)/shard_map/ppermute | solution.py:433
  84.8 2.2 %collective-permute-start.27 = (bf16[4,48,768]{2,1,0:T(8,128)(2,1)S(1)}, bf16[4,48,768]{2,1,0:T(8,128)(2,1)S(1)}, u32[]{:S(2)}, u32[]{:S(2)}) collective-permute-start(bf16[4,48,768]{2,1,0:T(8,128)(2,1)S(1)} %get-tuple-element.68.refs_4_), channel_id=1, source_target_pairs={{0,2},{1,3},{2,0},{3,1},{4,6},{5,7},{6,4},{7,5},{8,10},{9,11},{10,... | collective-permute-start | bytes 884744 | tf_op jit(solution)/shard_map/ppermute | solution.py:433
  87.1 2.5 %collective-permute-done.21.refs_2_ = bf16[2,96,768]{2,1,0:T(8,128)(2,1)S(1)} collective-permute-done((bf16[2,96,768]{2,1,0:T(8,128)(2,1)S(1)}, bf16[2,96,768]{2,1,0:T(8,128)(2,1)S(1)}, u32[]{:S(2)}, u32[]{:S(2)}) %collective-permute-start.21) | collective-permute-done | bytes 294944 | tf_op jit(solution)/shard_map/ppermute | solution.py:433
  91.5 2.4 %collective-permute-start.25 = (bf16[96,768]{1,0:T(8,128)(2,1)S(1)}, bf16[96,768]{1,0:T(8,128)(2,1)S(1)}, u32[]{:S(2)}, u32[]{:S(2)}) collective-permute-start(bf16[96,768]{1,0:T(8,128)(2,1)S(1)} %get-tuple-element.70.refs_5_), channel_id=1, source_target_pairs={{0,8},{1,9},{2,10},{3,11},{4,12},{5,13},{6,14},{7,15},{8,0},{9,1},... | collective-permute-start | bytes 442376 | tf_op jit(solution)/shard_map/ppermute | solution.py:433
  94.7 2.1 %collective-permute-done.25.refs_2_ = bf16[96,768]{1,0:T(8,128)(2,1)S(1)} collective-permute-done((bf16[96,768]{1,0:T(8,128)(2,1)S(1)}, bf16[96,768]{1,0:T(8,128)(2,1)S(1)}, u32[]{:S(2)}, u32[]{:S(2)}) %collective-permute-start.25) | collective-permute-done | bytes 147488 | tf_op jit(solution)/shard_map/ppermute | solution.py:433
  102.7 2.8 %collective-permute-start.32 = (bf16[48,1536]{1,0:T(8,128)(2,1)S(1)}, bf16[48,1536]{1,0:T(8,128)(2,1)S(1)}, u32[]{:S(2)}, u32[]{:S(2)}) collective-permute-start(bf16[48,1536]{1,0:T(8,128)(2,1)S(1)} %get-tuple-element.77), channel_id=1, source_target_pairs={{0,16},{1,17},{2,18},{3,19},{4,20},{5,21},{6,22},{7,23},{8,24},{9,... | collective-permute-start | bytes 442376 | tf_op jit(solution)/shard_map/ppermute | solution.py:433
  105.5 5.2 %collective-permute-done.28.a1 = bf16[2,4,48,768]{3,2,1,0:T(8,128)(2,1)S(1)} collective-permute-done((bf16[2,4,48,768]{3,2,1,0:T(8,128)(2,1)S(1)}, bf16[2,4,48,768]{3,2,1,0:T(8,128)(2,1)S(1)}, u32[]{:S(2)}, u32[]{:S(2)}) %collective-permute-start.28) | collective-permute-done | bytes 589856 | tf_op jit(solution)/shard_map/ppermute | solution.py:433
  111.8 2.3 %input_part1.1.refs_0_ = f32[512,768]{1,0:T(8,128)S(1)} custom-call(s32[6]{0:T(128)S(1)} %copy-done.12, bf16[1024,768]{1,0:T(8,128)(2,1)S(1)} %get-tuple-element.53.g0, bf16[1024,768]{1,0:T(8,128)(2,1)S(1)} %get-tuple-element.60.g1, bf16[2,4,48,768]{3,2,1,0:T(8,128)(2,1)S(1)} %get-tuple-element.74.a0.refs_0_, ...), custom_call_target="tpu_custom_call" | custom-call | flops 1207959552 | bytes 6291456 | tf_op jit(solution)/shard_map/input_part1/pallas_call | solution.py:395
  114.1 5.0 %collective-permute-start.30 = (f32[512,768]{1,0:T(8,128)S(1)}, f32[512,768]{1,0:T(8,128)S(1)}, u32[]{:S(2)}, u32[]{:S(2)}) collective-permute-start(f32[512,768]{1,0:T(8,128)S(1)} %input_part1.1.refs_0_), channel_id=1, source_target_pairs={{0,1},{1,0},{2,3},{3,2},{4,5},{5,4},{6,7},{7,6},{8,9},{9,8},{10,11... | collective-permute-start | bytes 4718600 | tf_op jit(solution)/shard_map/ppermute | solution.py:433
  119.1 2.3 %input_part0.1.refs_5_.refs_1_ = f32[512,768]{1,0:T(8,128)S(1)} custom-call(s32[6]{0:T(128)S(1)} %copy-done.12, bf16[1024,768]{1,0:T(8,128)(2,1)S(1)} %get-tuple-element.53.g0, bf16[1024,768]{1,0:T(8,128)(2,1)S(1)} %get-tuple-element.60.g1, bf16[2,4,48,768]{3,2,1,0:T(8,128)(2,1)S(1)} %get-tuple-element.74.a0.refs_0_, ...), custom_call_target="tpu_custom_call" | custom-call | flops 1207959552 | bytes 6291456 | tf_op jit(solution)/shard_map/input_part0/pallas_call | solution.py:395
  125.8 1.8 %input_sum.1 = f32[512,768]{1,0:T(8,128)} custom-call(s32[6]{0:T(128)S(1)} %copy-done.12, f32[512,768]{1,0:T(8,128)S(1)} %input_part0.1.refs_5_.refs_1_, f32[512,768]{1,0:T(8,128)S(1)} %collective-permute-done.30.refs_2_, f32[24,3072]{1,0:T(8,128)S(1)} %copy-done.8), custom_call_target="tpu_custom_call" | custom-call | bytes 4718592 | tf_op jit(solution)/shard_map/input_sum/pallas_call | solution.py:193
  (101 shorter events, 36.1 us)
Async XLA Ops:
  0.6 11.8 %collective-permute-start.2 = (bf16[512,3072]{1,0:T(8,128)(2,1)}, bf16[512,3072]{1,0:T(8,128)(2,1)S(1)}, u32[]{:S(2)}, u32[]{:S(2)}) collective-permute-start(bf16[512,3072]{1,0:T(8,128)(2,1)} %pre_ref.3), channel_id=1, source_target_pairs={{0,1},{1,0},{2,3},{3,2},{4,5},{5,4},{6,7},{7,6},{8,9},{9,8},{10,11... | collective-permute-start | bytes 9437192 | tf_op jit(solution)/shard_map/ppermute | solution.py:433
  1.2 11.2 %collective-permute-start.1 = (bf16[512,768]{1,0:T(8,128)(2,1)}, bf16[512,768]{1,0:T(8,128)(2,1)S(1)}, u32[]{:S(2)}, u32[]{:S(2)}) collective-permute-start(bf16[512,768]{1,0:T(8,128)(2,1)} %in_ref.3), channel_id=1, source_target_pairs={{0,1},{1,0},{2,3},{3,2},{4,5},{5,4},{6,7},{7,6},{8,9},{9,8},{10,11... | collective-permute-start | bytes 2359304 | tf_op jit(solution)/shard_map/ppermute | solution.py:433
  1.3 20.5 %collective-permute-start.7 = (bf16[24,3072]{1,0:T(8,128)(2,1)}, bf16[24,3072]{1,0:T(8,128)(2,1)S(1)}, u32[]{:S(2)}, u32[]{:S(2)}) collective-permute-start(bf16[24,3072]{1,0:T(8,128)(2,1)} %refs_1_.1), channel_id=1, source_target_pairs={{0,1},{1,0},{2,3},{3,2},{4,5},{5,4},{6,7},{7,6},{8,9},{9,8},{10,11... | collective-permute-start | bytes 442376 | tf_op jit(solution)/shard_map/ppermute | solution.py:433
  1.7 21.8 %collective-permute-start.3 = (bf16[96,768]{1,0:T(8,128)(2,1)}, bf16[96,768]{1,0:T(8,128)(2,1)S(1)}, u32[]{:S(2)}, u32[]{:S(2)}) collective-permute-start(bf16[96,768]{1,0:T(8,128)(2,1)} %param.8), channel_id=1, source_target_pairs={{0,0},{1,16},{2,2},{3,18},{4,4},{5,20},{6,6},{7,22},{8,8},{9,24},{... | collective-permute-start | bytes 442376 | tf_op jit(solution)/shard_map/ppermute | solution.py:433
  7.7 15.9 %collective-permute-start.4 = (bf16[96,768]{1,0:T(8,128)(2,1)}, bf16[96,768]{1,0:T(8,128)(2,1)}, u32[]{:S(2)}, u32[]{:S(2)}) collective-permute-start(bf16[96,768]{1,0:T(8,128)(2,1)} %param.8), channel_id=1, source_target_pairs={{0,8},{1,24},{2,10},{3,26},{4,12},{5,28},{6,14},{7,30},{8,0},{9,16... | collective-permute-start | bytes 442376 | tf_op jit(solution)/shard_map/ppermute | solution.py:433
  12.4 11.2 %collective-permute-start.5 = (bf16[96,768]{1,0:T(8,128)(2,1)}, bf16[96,768]{1,0:T(8,128)(2,1)}, u32[]{:S(2)}, u32[]{:S(2)}) collective-permute-start(bf16[96,768]{1,0:T(8,128)(2,1)} %param.8), channel_id=1, source_target_pairs={{0,16},{1,0},{2,18},{3,2},{4,20},{5,4},{6,22},{7,6},{8,24},{9,8},{... | collective-permute-start | bytes 442376 | tf_op jit(solution)/shard_map/ppermute | solution.py:433
  12.4 11.2 %collective-permute-start.6 = (bf16[96,768]{1,0:T(8,128)(2,1)}, bf16[96,768]{1,0:T(8,128)(2,1)}, u32[]{:S(2)}, u32[]{:S(2)}) collective-permute-start(bf16[96,768]{1,0:T(8,128)(2,1)} %param.8), channel_id=1, source_target_pairs={{0,24},{1,8},{2,26},{3,10},{4,28},{5,12},{6,30},{7,14},{8,16},{9,0... | collective-permute-start | bytes 442376 | tf_op jit(solution)/shard_map/ppermute | solution.py:433
  27.3 18.9 %collective-permute-start.15 = (bf16[2,192,768]{2,1,0:T(8,128)(2,1)}, bf16[2,192,768]{2,1,0:T(8,128)(2,1)S(1)}, u32[]{:S(2)}, u32[]{:S(2)}) collective-permute-start(bf16[2,192,768]{2,1,0:T(8,128)(2,1)} %get-tuple-element.43.refs_3_), channel_id=1, source_target_pairs={{0,2},{1,3},{2,0},{3,1},{4,6},{5,7},{6,4},{7,5},{8,10},{9,11},{10,... | collective-permute-start | bytes 1769480 | tf_op jit(solution)/shard_map/ppermute | solution.py:433
  33.7 14.3 %collective-permute-start.14 = (bf16[2,192,768]{2,1,0:T(8,128)(2,1)S(1)}, bf16[2,192,768]{2,1,0:T(8,128)(2,1)S(1)}, u32[]{:S(2)}, u32[]{:S(2)}) collective-permute-start(bf16[2,192,768]{2,1,0:T(8,128)(2,1)S(1)} %get-tuple-element.46.refs_5_), channel_id=1, source_target_pairs={{0,4},{1,5},{2,6},{3,7},{4,0},{5,1},{6,2},{7,3},{8,12},{9,13},{10,... | collective-permute-start | bytes 1769480 | tf_op jit(solution)/shard_map/ppermute | solution.py:433
  35.0 25.4 %collective-permute-start.10 = (bf16[2,192,768]{2,1,0:T(8,128)(2,1)S(1)}, bf16[2,192,768]{2,1,0:T(8,128)(2,1)S(1)}, u32[]{:S(2)}, u32[]{:S(2)}) collective-permute-start(bf16[2,192,768]{2,1,0:T(8,128)(2,1)S(1)} %get-tuple-element.47.refs_3_.mine), channel_id=1, source_target_pairs={{0,4},{1,5},{2,6},{3,7},{4,0},{5,1},{6,2},{7,3},{8,12},{9,13},{10,... | collective-permute-start | bytes 1769480 | tf_op jit(solution)/shard_map/ppermute | solution.py:433
  36.3 31.2 %collective-permute-start.16 = (bf16[2,192,768]{2,1,0:T(8,128)(2,1)S(1)}, bf16[2,192,768]{2,1,0:T(8,128)(2,1)S(1)}, u32[]{:S(2)}, u32[]{:S(2)}) collective-permute-start(bf16[2,192,768]{2,1,0:T(8,128)(2,1)S(1)} %get-tuple-element.55.mine), channel_id=1, source_target_pairs={{0,2},{1,3},{2,0},{3,1},{4,6},{5,7},{6,4},{7,5},{8,10},{9,11},{10,... | collective-permute-start | bytes 1769480 | tf_op jit(solution)/shard_map/ppermute | solution.py:433
  37.1 12.9 %collective-permute-start.11 = (bf16[2,24,1536]{2,1,0:T(8,128)(2,1)S(1)}, bf16[2,24,1536]{2,1,0:T(8,128)(2,1)S(1)}, u32[]{:S(2)}, u32[]{:S(2)}) collective-permute-start(bf16[2,24,1536]{2,1,0:T(8,128)(2,1)S(1)} %pair_kernel.1.refs_5_.refs_1_), channel_id=1, source_target_pairs={{0,8},{1,9},{2,10},{3,11},{4,12},{5,13},{6,14},{7,15},{8,0},{9,1},... | collective-permute-start | bytes 442376 | tf_op jit(solution)/shard_map/ppermute | solution.py:433
  50.0 16.5 %collective-permute-start.18 = (bf16[192,768]{1,0:T(8,128)(2,1)S(1)}, bf16[192,768]{1,0:T(8,128)(2,1)S(1)}, u32[]{:S(2)}, u32[]{:S(2)}) collective-permute-start(bf16[192,768]{1,0:T(8,128)(2,1)S(1)} %get-tuple-element.51.refs_5_), channel_id=1, source_target_pairs={{0,2},{1,3},{2,0},{3,1},{4,6},{5,7},{6,4},{7,5},{8,10},{9,11},{10,... | collective-permute-start | bytes 884744 | tf_op jit(solution)/shard_map/ppermute | solution.py:433
  55.4 11.3 %collective-permute-start.17 = (bf16[192,768]{1,0:T(8,128)(2,1)S(1)}, bf16[192,768]{1,0:T(8,128)(2,1)S(1)}, u32[]{:S(2)}, u32[]{:S(2)}) collective-permute-start(bf16[192,768]{1,0:T(8,128)(2,1)S(1)} %get-tuple-element.50.refs_3_), channel_id=1, source_target_pairs={{0,4},{1,5},{2,6},{3,7},{4,0},{5,1},{6,2},{7,3},{8,12},{9,13},{10,... | collective-permute-start | bytes 884744 | tf_op jit(solution)/shard_map/ppermute | solution.py:433
  65.2 13.9 %collective-permute-start.24 = (bf16[4,2,48,768]{3,2,1,0:T(8,128)(2,1)S(1)}, bf16[4,2,48,768]{3,2,1,0:T(8,128)(2,1)S(1)}, u32[]{:S(2)}, u32[]{:S(2)}) collective-permute-start(bf16[4,2,48,768]{3,2,1,0:T(8,128)(2,1)S(1)} %get-tuple-element.58.refs_5_), channel_id=1, source_target_pairs={{0,2},{1,3},{2,0},{3,1},{4,6},{5,7},{6,4},{7,5},{8,10},{9,11},{10,... | collective-permute-start | bytes 1769480 | tf_op jit(solution)/shard_map/ppermute | solution.py:433
  72.3 11.8 %collective-permute-start.23 = (bf16[4,2,48,768]{3,2,1,0:T(8,128)(2,1)S(1)}, bf16[4,2,48,768]{3,2,1,0:T(8,128)(2,1)S(1)}, u32[]{:S(2)}, u32[]{:S(2)}) collective-permute-start(bf16[4,2,48,768]{3,2,1,0:T(8,128)(2,1)S(1)} %get-tuple-element.65.refs_3_), channel_id=1, source_target_pairs={{0,4},{1,5},{2,6},{3,7},{4,0},{5,1},{6,2},{7,3},{8,12},{9,13},{10,... | collective-permute-start | bytes 1769480 | tf_op jit(solution)/shard_map/ppermute | solution.py:433
  72.4 17.2 %collective-permute-start.21 = (bf16[2,96,768]{2,1,0:T(8,128)(2,1)S(1)}, bf16[2,96,768]{2,1,0:T(8,128)(2,1)S(1)}, u32[]{:S(2)}, u32[]{:S(2)}) collective-permute-start(bf16[2,96,768]{2,1,0:T(8,128)(2,1)S(1)} %get-tuple-element.59._), channel_id=1, source_target_pairs={{0,0},{1,16},{2,2},{3,18},{4,4},{5,20},{6,6},{7,22},{8,8},{9,24},{... | collective-permute-start | bytes 884744 | tf_op jit(solution)/shard_map/ppermute | solution.py:433
  78.9 11.9 %collective-permute-start.22 = (bf16[2,96,768]{2,1,0:T(8,128)(2,1)S(1)}, bf16[2,96,768]{2,1,0:T(8,128)(2,1)S(1)}, u32[]{:S(2)}, u32[]{:S(2)}) collective-permute-start(bf16[2,96,768]{2,1,0:T(8,128)(2,1)S(1)} %get-tuple-element.63), channel_id=1, source_target_pairs={{0,1},{1,17},{2,3},{3,19},{4,5},{5,21},{6,7},{7,23},{8,9},{9,25},{... | collective-permute-start | bytes 884744 | tf_op jit(solution)/shard_map/ppermute | solution.py:433
  79.8 14.2 %collective-permute-start.26 = (bf16[4,48,768]{2,1,0:T(8,128)(2,1)S(1)}, bf16[4,48,768]{2,1,0:T(8,128)(2,1)S(1)}, u32[]{:S(2)}, u32[]{:S(2)}) collective-permute-start(bf16[4,48,768]{2,1,0:T(8,128)(2,1)S(1)} %get-tuple-element.67.refs_3_), channel_id=1, source_target_pairs={{0,4},{1,5},{2,6},{3,7},{4,0},{5,1},{6,2},{7,3},{8,12},{9,13},{10,... | collective-permute-start | bytes 884744 | tf_op jit(solution)/shard_map/ppermute | solution.py:433
  87.0 11.0 %collective-permute-start.19 = (bf16[4,48,768]{2,1,0:T(8,128)(2,1)S(1)}, bf16[4,48,768]{2,1,0:T(8,128)(2,1)S(1)}, u32[]{:S(2)}, u32[]{:S(2)}) collective-permute-start(bf16[4,48,768]{2,1,0:T(8,128)(2,1)S(1)} %get-tuple-element.52._.refs_1_), channel_id=1, source_target_pairs={{0,2},{1,3},{2,0},{3,1},{4,6},{5,7},{6,4},{7,5},{8,10},{9,11},{10,... | collective-permute-start | bytes 884744 | tf_op jit(solution)/shard_map/ppermute | solution.py:433
  99.7 11.1 %collective-permute-start.28 = (bf16[2,4,48,768]{3,2,1,0:T(8,128)(2,1)S(1)}, bf16[2,4,48,768]{3,2,1,0:T(8,128)(2,1)S(1)}, u32[]{:S(2)}, u32[]{:S(2)}) collective-permute-start(bf16[2,4,48,768]{3,2,1,0:T(8,128)(2,1)S(1)} %get-tuple-element.74.a0.refs_0_), channel_id=1, source_target_pairs={{0,4},{1,5},{2,6},{3,7},{4,0},{5,1},{6,2},{7,3},{8,12},{9,13},{10,... | collective-permute-start | bytes 1769480 | tf_op jit(solution)/shard_map/ppermute | solution.py:433
  101.2 20.2 %collective-permute-start.31 = (bf16[48,1536]{1,0:T(8,128)(2,1)S(1)}, bf16[48,1536]{1,0:T(8,128)(2,1)S(1)}, u32[]{:S(2)}, u32[]{:S(2)}) collective-permute-start(bf16[48,1536]{1,0:T(8,128)(2,1)S(1)} %get-tuple-element.73.refs_3_), channel_id=1, source_target_pairs={{0,8},{1,9},{2,10},{3,11},{4,12},{5,13},{6,14},{7,15},{8,0},{9,1},... | collective-permute-start | bytes 442376 | tf_op jit(solution)/shard_map/ppermute | solution.py:433
  102.7 18.8 %collective-permute-start.32 = (bf16[48,1536]{1,0:T(8,128)(2,1)S(1)}, bf16[48,1536]{1,0:T(8,128)(2,1)S(1)}, u32[]{:S(2)}, u32[]{:S(2)}) collective-permute-start(bf16[48,1536]{1,0:T(8,128)(2,1)S(1)} %get-tuple-element.77), channel_id=1, source_target_pairs={{0,16},{1,17},{2,18},{3,19},{4,20},{5,21},{6,22},{7,23},{8,24},{9,... | collective-permute-start | bytes 442376 | tf_op jit(solution)/shard_map/ppermute | solution.py:433
  105.5 16.0 %collective-permute-start.33 = (bf16[48,1536]{1,0:T(8,128)(2,1)S(1)}, bf16[48,1536]{1,0:T(8,128)(2,1)S(1)}, u32[]{:S(2)}, u32[]{:S(2)}) collective-permute-start(bf16[48,1536]{1,0:T(8,128)(2,1)S(1)} %get-tuple-element.78), channel_id=1, source_target_pairs={{0,24},{1,25},{2,26},{3,27},{4,28},{5,29},{6,30},{7,31},{8,16},{9,... | collective-permute-start | bytes 442376 | tf_op jit(solution)/shard_map/ppermute | solution.py:433
  (27 other events, 190.8 us)

commit v5 on v4

--- a/solution.py
+++ b/solution.py
@@ -599,6 +599,7 @@
     def input_sum(at, mine, other, out):
         out[...] = mine[...] + other[...]
 
+    order.after = [mine]
     (input_grad,) = kernel(input_sum, [part_own, part_got], [shape((tokens, width), F32)])
     return (input_grad, w_out_grad, w_in_grad)
 

time: 128 us -> 127 us (level)
  waiting for transfers between devices: 30.9 us -> 32.5 us
  starting transfers between devices: 51.3 us -> 49.8 us
    ppermute x35, waiting for transfers between devices: 30.9 us -> 32.5 us  [send(): return lax.ppermute(array, AXIS, perm)]
    ppermute x35, starting transfers between devices: 51.3 us -> 49.8 us  [send(): return lax.ppermute(array, AXIS, perm)]
    unnamed x32 -> x30, local copies, waits for them, and re-layouts: 5.03 us -> 4.07 us
  transfers between devices with their start and end apart: 35 -> 35, of which waited for: 12 -> 13; matrix products, arithmetic and copies ran while one was open for 1% -> 0% of each run, Pallas kernels for 28% -> 28%
where the time goes in v5:
time: 127 us
  starting transfers between devices  49.8 us (39%)
  Pallas kernels  38.8 us (31%)
  waiting for transfers between devices  32.5 us (26%)
  local copies, waits for them, and re-layouts  4.67 us (4%)
    ppermute x35, starting transfers between devices, send(): return lax.ppermute(array, AXIS, perm)  49.8 us
    ppermute x35, waiting for transfers between devices, send(): return lax.ppermute(array, AXIS, perm)  32.5 us
    pallas_call x16, Pallas kernels, small(): pl.pallas_call(run, name=name or body.__name__, out_shape=outs, in_specs=...  13.3 us
    pallas_call x2, Pallas kernels, out_total(): pl.pallas_call(body, name=f'out_total{cut}', grid_spec=pltpu.PrefetchScal...  11.2 us
    pallas_call x2, Pallas kernels, in_total(): pl.pallas_call(body, name=f'in_total{cut}', grid_spec=pltpu.PrefetchScala...  9.58 us
    pallas_call x2, Pallas kernels, input_part(): pl.pallas_call(body, name=f'input_part{part}', grid_spec=pltpu.PrefetchSc...  4.69 us
    unnamed x30, local copies, waits for them, and re-layouts  4.07 us
  transfers between devices with their start and end apart: 35, of which 13 were waited for; matrix products, arithmetic and copies ran while one was open for 0% of the time, Pallas kernels for 28%

profile of v5, /device:TPU:1, one launch (start us, length us, event | category | flops | bytes accessed | tf_op | source)
XLA Modules:
  0.0 126.7 jit_solution(18270476848587528735)
XLA Ops:
  1.7 5.6 %collective-permute-start.3 = (bf16[96,768]{1,0:T(8,128)(2,1)}, bf16[96,768]{1,0:T(8,128)(2,1)S(1)}, u32[]{:S(2)}, u32[]{:S(2)}) collective-permute-start(bf16[96,768]{1,0:T(8,128)(2,1)} %param.8), channel_id=1, source_target_pairs={{0,0},{1,16},{2,2},{3,18},{4,4},{5,20},{6,6},{7,22},{8,8},{9,24},{... | collective-permute-start | bytes 442376 | tf_op jit(solution)/shard_map/ppermute | solution.py:433
  7.7 4.7 %collective-permute-start.4 = (bf16[96,768]{1,0:T(8,128)(2,1)}, bf16[96,768]{1,0:T(8,128)(2,1)}, u32[]{:S(2)}, u32[]{:S(2)}) collective-permute-start(bf16[96,768]{1,0:T(8,128)(2,1)} %param.8), channel_id=1, source_target_pairs={{0,8},{1,24},{2,10},{3,26},{4,12},{5,28},{6,14},{7,30},{8,0},{9,16... | collective-permute-start | bytes 442376 | tf_op jit(solution)/shard_map/ppermute | solution.py:433
  12.4 1.7 %collective-permute-start.6 = (bf16[96,768]{1,0:T(8,128)(2,1)}, bf16[96,768]{1,0:T(8,128)(2,1)}, u32[]{:S(2)}, u32[]{:S(2)}) collective-permute-start(bf16[96,768]{1,0:T(8,128)(2,1)} %param.8), channel_id=1, source_target_pairs={{0,24},{1,8},{2,26},{3,10},{4,28},{5,12},{6,30},{7,14},{8,16},{9,0... | collective-permute-start | bytes 442376 | tf_op jit(solution)/shard_map/ppermute | solution.py:433
  14.8 6.9 %out_total0.1 = (f32[1024,768]{1,0:T(8,128)}, bf16[2,192,768]{2,1,0:T(8,128)(2,1)}, f32[2,192,768]{2,1,0:T(8,128)}) custom-call(s32[6]{0:T(128)} %stack.27.at.refs_0_, bf16[512,3072]{1,0:T(8,128)(2,1)} %pre_ref.3, bf16[512,3072]{1,0:T(8,128)(2,1)} %copy-done.1, bf16[512,768]{1,0:T(8,128)(2,1)} %grad_ref.7, bf16[512,768]{1,0:T(8,128)(2,1)} %copy-done.4, ...), custom_call_target="tpu_custom_call" | custom-call | flops 1207959552 | bytes 20971520 | tf_op jit(solution)/shard_map/out_total0/pallas_call | solution.py:276
  27.5 1.9 %copy-done.2 = bf16[512,3072]{1,0:T(8,128)(2,1)S(1)} copy-done((bf16[512,3072]{1,0:T(8,128)(2,1)S(1)}, bf16[512,3072]{1,0:T(8,128)(2,1)}, u32[]{:S(2)}) %copy-start.2) | copy-done | bytes 3145752
  29.3 4.2 %out_total1.1 = (f32[1024,768]{1,0:T(8,128)S(1)}, bf16[2,192,768]{2,1,0:T(8,128)(2,1)S(1)}, f32[2,192,768]{2,1,0:T(8,128)S(1)}) custom-call(s32[6]{0:T(128)S(1)} %copy-done.11, bf16[512,3072]{1,0:T(8,128)(2,1)S(1)} %copy-done, bf16[512,3072]{1,0:T(8,128)(2,1)S(1)} %copy-done.2, bf16[512,768]{1,0:T(8,128)(2,1)S(1)} %copy-done.3, ...), custom_call_target="tpu_custom_call" | custom-call | flops 1207959552 | bytes 20971520 | tf_op jit(solution)/shard_map/out_total1/pallas_call | solution.py:276
  37.2 8.9 %collective-permute-done.15.refs_2_ = bf16[2,192,768]{2,1,0:T(8,128)(2,1)S(1)} collective-permute-done((bf16[2,192,768]{2,1,0:T(8,128)(2,1)}, bf16[2,192,768]{2,1,0:T(8,128)(2,1)S(1)}, u32[]{:S(2)}, u32[]{:S(2)}) %collective-permute-start.15) | collective-permute-done | bytes 589856 | tf_op jit(solution)/shard_map/ppermute | solution.py:433
  46.1 1.9 %collective-permute-start.12 = (bf16[2,24,1536]{2,1,0:T(8,128)(2,1)S(1)}, bf16[2,24,1536]{2,1,0:T(8,128)(2,1)S(1)}, u32[]{:S(2)}, u32[]{:S(2)}) collective-permute-start(bf16[2,24,1536]{2,1,0:T(8,128)(2,1)S(1)} %pair_kernel.1.refs_5_.refs_1_), channel_id=1, source_target_pairs={{0,16},{1,17},{2,18},{3,19},{4,20},{5,21},{6,22},{7,23},{8,24},{9,... | collective-permute-start | bytes 442376 | tf_op jit(solution)/shard_map/ppermute | solution.py:433
  53.3 1.8 %collective-permute-done.13.refs_4_ = bf16[2,24,1536]{2,1,0:T(8,128)(2,1)S(1)} collective-permute-done((bf16[2,24,1536]{2,1,0:T(8,128)(2,1)S(1)}, bf16[2,24,1536]{2,1,0:T(8,128)(2,1)S(1)}, u32[]{:S(2)}, u32[]{:S(2)}) %collective-permute-start.13) | collective-permute-done | bytes 147488 | tf_op jit(solution)/shard_map/ppermute | solution.py:433
  55.7 4.6 %collective-permute-done.10.other = bf16[2,192,768]{2,1,0:T(8,128)(2,1)S(1)} collective-permute-done((bf16[2,192,768]{2,1,0:T(8,128)(2,1)S(1)}, bf16[2,192,768]{2,1,0:T(8,128)(2,1)S(1)}, u32[]{:S(2)}, u32[]{:S(2)}) %collective-permute-start.10) | collective-permute-done | bytes 589856 | tf_op jit(solution)/shard_map/ppermute | solution.py:433
  60.4 4.8 %in_total0.1 = (bf16[1024,768]{1,0:T(8,128)(2,1)S(1)}, bf16[4,2,48,768]{3,2,1,0:T(8,128)(2,1)S(1)}, f32[4,2,48,768]{3,2,1,0:T(8,128)S(1)}) custom-call(s32[6]{0:T(128)S(1)} %copy-done.11, bf16[512,768]{1,0:T(8,128)(2,1)S(1)} %copy-done.3, bf16[512,768]{1,0:T(8,128)(2,1)S(1)} %copy-done.5, bf16[512,768]{1,0:T(8,128)(2,1)S(1)} %copy-done.14, ...), custom_call_target="tpu_custom_call" | custom-call | flops 2415919104 | bytes 16777216 | tf_op jit(solution)/shard_map/in_total0/pallas_call | solution.py:345
  67.4 4.8 %in_total1.1 = (bf16[1024,768]{1,0:T(8,128)(2,1)S(1)}, bf16[4,2,48,768]{3,2,1,0:T(8,128)(2,1)S(1)}, f32[4,2,48,768]{3,2,1,0:T(8,128)S(1)}) custom-call(s32[6]{0:T(128)S(1)} %copy-done.11, bf16[512,768]{1,0:T(8,128)(2,1)S(1)} %copy-done.3, bf16[512,768]{1,0:T(8,128)(2,1)S(1)} %copy-done.5, bf16[512,768]{1,0:T(8,128)(2,1)S(1)} %copy-done.14, ...), custom_call_target="tpu_custom_call" | custom-call | flops 2415919104 | bytes 16777216 | tf_op jit(solution)/shard_map/in_total1/pallas_call | solution.py:345
  72.3 6.5 %collective-permute-start.21 = (bf16[2,96,768]{2,1,0:T(8,128)(2,1)S(1)}, bf16[2,96,768]{2,1,0:T(8,128)(2,1)S(1)}, u32[]{:S(2)}, u32[]{:S(2)}) collective-permute-start(bf16[2,96,768]{2,1,0:T(8,128)(2,1)S(1)} %get-tuple-element.59._), channel_id=1, source_target_pairs={{0,0},{1,16},{2,2},{3,18},{4,4},{5,20},{6,6},{7,22},{8,8},{9,24},{... | collective-permute-start | bytes 884744 | tf_op jit(solution)/shard_map/ppermute | solution.py:433
  81.1 3.0 %collective-permute-done.23.refs_2_ = bf16[4,2,48,768]{3,2,1,0:T(8,128)(2,1)S(1)} collective-permute-done((bf16[4,2,48,768]{3,2,1,0:T(8,128)(2,1)S(1)}, bf16[4,2,48,768]{3,2,1,0:T(8,128)(2,1)S(1)}, u32[]{:S(2)}, u32[]{:S(2)}) %collective-permute-start.23) | collective-permute-done | bytes 589856 | tf_op jit(solution)/shard_map/ppermute | solution.py:433
  84.7 2.2 %collective-permute-start.27 = (bf16[4,48,768]{2,1,0:T(8,128)(2,1)S(1)}, bf16[4,48,768]{2,1,0:T(8,128)(2,1)S(1)}, u32[]{:S(2)}, u32[]{:S(2)}) collective-permute-start(bf16[4,48,768]{2,1,0:T(8,128)(2,1)S(1)} %get-tuple-element.68.refs_4_), channel_id=1, source_target_pairs={{0,2},{1,3},{2,0},{3,1},{4,6},{5,7},{6,4},{7,5},{8,10},{9,11},{10,... | collective-permute-start | bytes 884744 | tf_op jit(solution)/shard_map/ppermute | solution.py:433
  87.0 2.5 %collective-permute-done.21.refs_2_ = bf16[2,96,768]{2,1,0:T(8,128)(2,1)S(1)} collective-permute-done((bf16[2,96,768]{2,1,0:T(8,128)(2,1)S(1)}, bf16[2,96,768]{2,1,0:T(8,128)(2,1)S(1)}, u32[]{:S(2)}, u32[]{:S(2)}) %collective-permute-start.21) | collective-permute-done | bytes 294944 | tf_op jit(solution)/shard_map/ppermute | solution.py:433
  91.5 2.4 %collective-permute-start.25 = (bf16[96,768]{1,0:T(8,128)(2,1)S(1)}, bf16[96,768]{1,0:T(8,128)(2,1)S(1)}, u32[]{:S(2)}, u32[]{:S(2)}) collective-permute-start(bf16[96,768]{1,0:T(8,128)(2,1)S(1)} %get-tuple-element.70.refs_5_), channel_id=1, source_target_pairs={{0,8},{1,9},{2,10},{3,11},{4,12},{5,13},{6,14},{7,15},{8,0},{9,1},... | collective-permute-start | bytes 442376 | tf_op jit(solution)/shard_map/ppermute | solution.py:433
  94.7 2.1 %collective-permute-done.25.refs_2_ = bf16[96,768]{1,0:T(8,128)(2,1)S(1)} collective-permute-done((bf16[96,768]{1,0:T(8,128)(2,1)S(1)}, bf16[96,768]{1,0:T(8,128)(2,1)S(1)}, u32[]{:S(2)}, u32[]{:S(2)}) %collective-permute-start.25) | collective-permute-done | bytes 147488 | tf_op jit(solution)/shard_map/ppermute | solution.py:433
  102.7 2.9 %collective-permute-start.32 = (bf16[48,1536]{1,0:T(8,128)(2,1)S(1)}, bf16[48,1536]{1,0:T(8,128)(2,1)S(1)}, u32[]{:S(2)}, u32[]{:S(2)}) collective-permute-start(bf16[48,1536]{1,0:T(8,128)(2,1)S(1)} %get-tuple-element.77), channel_id=1, source_target_pairs={{0,16},{1,17},{2,18},{3,19},{4,20},{5,21},{6,22},{7,23},{8,24},{9,... | collective-permute-start | bytes 442376 | tf_op jit(solution)/shard_map/ppermute | solution.py:433
  105.6 5.2 %collective-permute-done.28.a1 = bf16[2,4,48,768]{3,2,1,0:T(8,128)(2,1)S(1)} collective-permute-done((bf16[2,4,48,768]{3,2,1,0:T(8,128)(2,1)S(1)}, bf16[2,4,48,768]{3,2,1,0:T(8,128)(2,1)S(1)}, u32[]{:S(2)}, u32[]{:S(2)}) %collective-permute-start.28) | collective-permute-done | bytes 589856 | tf_op jit(solution)/shard_map/ppermute | solution.py:433
  111.9 2.3 %input_part1.1.refs_0_ = f32[512,768]{1,0:T(8,128)S(1)} custom-call(s32[6]{0:T(128)S(1)} %copy-done.11, bf16[1024,768]{1,0:T(8,128)(2,1)S(1)} %get-tuple-element.53.g0, bf16[1024,768]{1,0:T(8,128)(2,1)S(1)} %get-tuple-element.60.g1, bf16[2,4,48,768]{3,2,1,0:T(8,128)(2,1)S(1)} %get-tuple-element.74.a0.refs_0_, ...), custom_call_target="tpu_custom_call" | custom-call | flops 1207959552 | bytes 6291456 | tf_op jit(solution)/shard_map/input_part1/pallas_call | solution.py:395
  114.2 4.9 %collective-permute-start.30 = (f32[512,768]{1,0:T(8,128)S(1)}, f32[512,768]{1,0:T(8,128)S(1)}, u32[]{:S(2)}, u32[]{:S(2)}) collective-permute-start(f32[512,768]{1,0:T(8,128)S(1)} %input_part1.1.refs_0_), channel_id=1, source_target_pairs={{0,1},{1,0},{2,3},{3,2},{4,5},{5,4},{6,7},{7,6},{8,9},{9,8},{10,11... | collective-permute-start | bytes 4718600 | tf_op jit(solution)/shard_map/ppermute | solution.py:433
  119.1 2.3 %input_part0.1.refs_5_.refs_1_ = f32[512,768]{1,0:T(8,128)S(1)} custom-call(s32[6]{0:T(128)S(1)} %copy-done.11, bf16[1024,768]{1,0:T(8,128)(2,1)S(1)} %get-tuple-element.53.g0, bf16[1024,768]{1,0:T(8,128)(2,1)S(1)} %get-tuple-element.60.g1, bf16[2,4,48,768]{3,2,1,0:T(8,128)(2,1)S(1)} %get-tuple-element.74.a0.refs_0_, ...), custom_call_target="tpu_custom_call" | custom-call | flops 1207959552 | bytes 6291456 | tf_op jit(solution)/shard_map/input_part0/pallas_call | solution.py:395
  124.9 1.8 %input_sum.1 = f32[512,768]{1,0:T(8,128)} custom-call(s32[6]{0:T(128)S(1)} %copy-done.11, f32[512,768]{1,0:T(8,128)S(1)} %input_part0.1.refs_5_.refs_1_, f32[512,768]{1,0:T(8,128)S(1)} %collective-permute-done.30.refs_2_, f32[24,1536]{1,0:T(8,128)S(1)} %get-tuple-element.79.refs_3_.refs_1_), custom_call_target="tpu_custom_call" | custom-call | bytes 4718592 | tf_op jit(solution)/shard_map/input_sum/pallas_call | solution.py:193
  (99 shorter events, 35.5 us)
Async XLA Ops:
  0.6 11.8 %collective-permute-start.2 = (bf16[512,3072]{1,0:T(8,128)(2,1)}, bf16[512,3072]{1,0:T(8,128)(2,1)S(1)}, u32[]{:S(2)}, u32[]{:S(2)}) collective-permute-start(bf16[512,3072]{1,0:T(8,128)(2,1)} %pre_ref.3), channel_id=1, source_target_pairs={{0,1},{1,0},{2,3},{3,2},{4,5},{5,4},{6,7},{7,6},{8,9},{9,8},{10,11... | collective-permute-start | bytes 9437192 | tf_op jit(solution)/shard_map/ppermute | solution.py:433
  1.2 11.2 %collective-permute-start.1 = (bf16[512,768]{1,0:T(8,128)(2,1)}, bf16[512,768]{1,0:T(8,128)(2,1)S(1)}, u32[]{:S(2)}, u32[]{:S(2)}) collective-permute-start(bf16[512,768]{1,0:T(8,128)(2,1)} %in_ref.3), channel_id=1, source_target_pairs={{0,1},{1,0},{2,3},{3,2},{4,5},{5,4},{6,7},{7,6},{8,9},{9,8},{10,11... | collective-permute-start | bytes 2359304 | tf_op jit(solution)/shard_map/ppermute | solution.py:433
  1.3 20.4 %collective-permute-start.7 = (bf16[24,3072]{1,0:T(8,128)(2,1)}, bf16[24,3072]{1,0:T(8,128)(2,1)S(1)}, u32[]{:S(2)}, u32[]{:S(2)}) collective-permute-start(bf16[24,3072]{1,0:T(8,128)(2,1)} %refs_1_.1), channel_id=1, source_target_pairs={{0,1},{1,0},{2,3},{3,2},{4,5},{5,4},{6,7},{7,6},{8,9},{9,8},{10,11... | collective-permute-start | bytes 442376 | tf_op jit(solution)/shard_map/ppermute | solution.py:433
  1.7 21.8 %collective-permute-start.3 = (bf16[96,768]{1,0:T(8,128)(2,1)}, bf16[96,768]{1,0:T(8,128)(2,1)S(1)}, u32[]{:S(2)}, u32[]{:S(2)}) collective-permute-start(bf16[96,768]{1,0:T(8,128)(2,1)} %param.8), channel_id=1, source_target_pairs={{0,0},{1,16},{2,2},{3,18},{4,4},{5,20},{6,6},{7,22},{8,8},{9,24},{... | collective-permute-start | bytes 442376 | tf_op jit(solution)/shard_map/ppermute | solution.py:433
  7.7 15.8 %collective-permute-start.4 = (bf16[96,768]{1,0:T(8,128)(2,1)}, bf16[96,768]{1,0:T(8,128)(2,1)}, u32[]{:S(2)}, u32[]{:S(2)}) collective-permute-start(bf16[96,768]{1,0:T(8,128)(2,1)} %param.8), channel_id=1, source_target_pairs={{0,8},{1,24},{2,10},{3,26},{4,12},{5,28},{6,14},{7,30},{8,0},{9,16... | collective-permute-start | bytes 442376 | tf_op jit(solution)/shard_map/ppermute | solution.py:433
  12.4 11.1 %collective-permute-start.5 = (bf16[96,768]{1,0:T(8,128)(2,1)}, bf16[96,768]{1,0:T(8,128)(2,1)}, u32[]{:S(2)}, u32[]{:S(2)}) collective-permute-start(bf16[96,768]{1,0:T(8,128)(2,1)} %param.8), channel_id=1, source_target_pairs={{0,16},{1,0},{2,18},{3,2},{4,20},{5,4},{6,22},{7,6},{8,24},{9,8},{... | collective-permute-start | bytes 442376 | tf_op jit(solution)/shard_map/ppermute | solution.py:433
  12.4 11.1 %collective-permute-start.6 = (bf16[96,768]{1,0:T(8,128)(2,1)}, bf16[96,768]{1,0:T(8,128)(2,1)}, u32[]{:S(2)}, u32[]{:S(2)}) collective-permute-start(bf16[96,768]{1,0:T(8,128)(2,1)} %param.8), channel_id=1, source_target_pairs={{0,24},{1,8},{2,26},{3,10},{4,28},{5,12},{6,30},{7,14},{8,16},{9,0... | collective-permute-start | bytes 442376 | tf_op jit(solution)/shard_map/ppermute | solution.py:433
  27.2 18.9 %collective-permute-start.15 = (bf16[2,192,768]{2,1,0:T(8,128)(2,1)}, bf16[2,192,768]{2,1,0:T(8,128)(2,1)S(1)}, u32[]{:S(2)}, u32[]{:S(2)}) collective-permute-start(bf16[2,192,768]{2,1,0:T(8,128)(2,1)} %get-tuple-element.43.refs_3_), channel_id=1, source_target_pairs={{0,2},{1,3},{2,0},{3,1},{4,6},{5,7},{6,4},{7,5},{8,10},{9,11},{10,... | collective-permute-start | bytes 1769480 | tf_op jit(solution)/shard_map/ppermute | solution.py:433
  33.6 14.4 %collective-permute-start.14 = (bf16[2,192,768]{2,1,0:T(8,128)(2,1)S(1)}, bf16[2,192,768]{2,1,0:T(8,128)(2,1)S(1)}, u32[]{:S(2)}, u32[]{:S(2)}) collective-permute-start(bf16[2,192,768]{2,1,0:T(8,128)(2,1)S(1)} %get-tuple-element.46.refs_5_), channel_id=1, source_target_pairs={{0,4},{1,5},{2,6},{3,7},{4,0},{5,1},{6,2},{7,3},{8,12},{9,13},{10,... | collective-permute-start | bytes 1769480 | tf_op jit(solution)/shard_map/ppermute | solution.py:433
  34.9 25.4 %collective-permute-start.10 = (bf16[2,192,768]{2,1,0:T(8,128)(2,1)S(1)}, bf16[2,192,768]{2,1,0:T(8,128)(2,1)S(1)}, u32[]{:S(2)}, u32[]{:S(2)}) collective-permute-start(bf16[2,192,768]{2,1,0:T(8,128)(2,1)S(1)} %get-tuple-element.47.refs_3_.mine), channel_id=1, source_target_pairs={{0,4},{1,5},{2,6},{3,7},{4,0},{5,1},{6,2},{7,3},{8,12},{9,13},{10,... | collective-permute-start | bytes 1769480 | tf_op jit(solution)/shard_map/ppermute | solution.py:433
  36.2 31.2 %collective-permute-start.16 = (bf16[2,192,768]{2,1,0:T(8,128)(2,1)S(1)}, bf16[2,192,768]{2,1,0:T(8,128)(2,1)S(1)}, u32[]{:S(2)}, u32[]{:S(2)}) collective-permute-start(bf16[2,192,768]{2,1,0:T(8,128)(2,1)S(1)} %get-tuple-element.55.mine), channel_id=1, source_target_pairs={{0,2},{1,3},{2,0},{3,1},{4,6},{5,7},{6,4},{7,5},{8,10},{9,11},{10,... | collective-permute-start | bytes 1769480 | tf_op jit(solution)/shard_map/ppermute | solution.py:433
  37.0 12.9 %collective-permute-start.11 = (bf16[2,24,1536]{2,1,0:T(8,128)(2,1)S(1)}, bf16[2,24,1536]{2,1,0:T(8,128)(2,1)S(1)}, u32[]{:S(2)}, u32[]{:S(2)}) collective-permute-start(bf16[2,24,1536]{2,1,0:T(8,128)(2,1)S(1)} %pair_kernel.1.refs_5_.refs_1_), channel_id=1, source_target_pairs={{0,8},{1,9},{2,10},{3,11},{4,12},{5,13},{6,14},{7,15},{8,0},{9,1},... | collective-permute-start | bytes 442376 | tf_op jit(solution)/shard_map/ppermute | solution.py:433
  49.9 16.5 %collective-permute-start.18 = (bf16[192,768]{1,0:T(8,128)(2,1)S(1)}, bf16[192,768]{1,0:T(8,128)(2,1)S(1)}, u32[]{:S(2)}, u32[]{:S(2)}) collective-permute-start(bf16[192,768]{1,0:T(8,128)(2,1)S(1)} %get-tuple-element.51.refs_5_), channel_id=1, source_target_pairs={{0,2},{1,3},{2,0},{3,1},{4,6},{5,7},{6,4},{7,5},{8,10},{9,11},{10,... | collective-permute-start | bytes 884744 | tf_op jit(solution)/shard_map/ppermute | solution.py:433
  52.0 14.6 %collective-permute-start.17 = (bf16[192,768]{1,0:T(8,128)(2,1)S(1)}, bf16[192,768]{1,0:T(8,128)(2,1)S(1)}, u32[]{:S(2)}, u32[]{:S(2)}) collective-permute-start(bf16[192,768]{1,0:T(8,128)(2,1)S(1)} %get-tuple-element.50.refs_3_), channel_id=1, source_target_pairs={{0,4},{1,5},{2,6},{3,7},{4,0},{5,1},{6,2},{7,3},{8,12},{9,13},{10,... | collective-permute-start | bytes 884744 | tf_op jit(solution)/shard_map/ppermute | solution.py:433
  65.1 14.0 %collective-permute-start.24 = (bf16[4,2,48,768]{3,2,1,0:T(8,128)(2,1)S(1)}, bf16[4,2,48,768]{3,2,1,0:T(8,128)(2,1)S(1)}, u32[]{:S(2)}, u32[]{:S(2)}) collective-permute-start(bf16[4,2,48,768]{3,2,1,0:T(8,128)(2,1)S(1)} %get-tuple-element.58.refs_5_), channel_id=1, source_target_pairs={{0,2},{1,3},{2,0},{3,1},{4,6},{5,7},{6,4},{7,5},{8,10},{9,11},{10,... | collective-permute-start | bytes 1769480 | tf_op jit(solution)/shard_map/ppermute | solution.py:433
  72.2 11.8 %collective-permute-start.23 = (bf16[4,2,48,768]{3,2,1,0:T(8,128)(2,1)S(1)}, bf16[4,2,48,768]{3,2,1,0:T(8,128)(2,1)S(1)}, u32[]{:S(2)}, u32[]{:S(2)}) collective-permute-start(bf16[4,2,48,768]{3,2,1,0:T(8,128)(2,1)S(1)} %get-tuple-element.65.refs_3_), channel_id=1, source_target_pairs={{0,4},{1,5},{2,6},{3,7},{4,0},{5,1},{6,2},{7,3},{8,12},{9,13},{10,... | collective-permute-start | bytes 1769480 | tf_op jit(solution)/shard_map/ppermute | solution.py:433
  72.3 17.3 %collective-permute-start.21 = (bf16[2,96,768]{2,1,0:T(8,128)(2,1)S(1)}, bf16[2,96,768]{2,1,0:T(8,128)(2,1)S(1)}, u32[]{:S(2)}, u32[]{:S(2)}) collective-permute-start(bf16[2,96,768]{2,1,0:T(8,128)(2,1)S(1)} %get-tuple-element.59._), channel_id=1, source_target_pairs={{0,0},{1,16},{2,2},{3,18},{4,4},{5,20},{6,6},{7,22},{8,8},{9,24},{... | collective-permute-start | bytes 884744 | tf_op jit(solution)/shard_map/ppermute | solution.py:433
  78.9 12.0 %collective-permute-start.22 = (bf16[2,96,768]{2,1,0:T(8,128)(2,1)S(1)}, bf16[2,96,768]{2,1,0:T(8,128)(2,1)S(1)}, u32[]{:S(2)}, u32[]{:S(2)}) collective-permute-start(bf16[2,96,768]{2,1,0:T(8,128)(2,1)S(1)} %get-tuple-element.63), channel_id=1, source_target_pairs={{0,1},{1,17},{2,3},{3,19},{4,5},{5,21},{6,7},{7,23},{8,9},{9,25},{... | collective-permute-start | bytes 884744 | tf_op jit(solution)/shard_map/ppermute | solution.py:433
  79.8 14.2 %collective-permute-start.26 = (bf16[4,48,768]{2,1,0:T(8,128)(2,1)S(1)}, bf16[4,48,768]{2,1,0:T(8,128)(2,1)S(1)}, u32[]{:S(2)}, u32[]{:S(2)}) collective-permute-start(bf16[4,48,768]{2,1,0:T(8,128)(2,1)S(1)} %get-tuple-element.67.refs_3_), channel_id=1, source_target_pairs={{0,4},{1,5},{2,6},{3,7},{4,0},{5,1},{6,2},{7,3},{8,12},{9,13},{10,... | collective-permute-start | bytes 884744 | tf_op jit(solution)/shard_map/ppermute | solution.py:433
  87.0 11.1 %collective-permute-start.19 = (bf16[4,48,768]{2,1,0:T(8,128)(2,1)S(1)}, bf16[4,48,768]{2,1,0:T(8,128)(2,1)S(1)}, u32[]{:S(2)}, u32[]{:S(2)}) collective-permute-start(bf16[4,48,768]{2,1,0:T(8,128)(2,1)S(1)} %get-tuple-element.52._.refs_1_), channel_id=1, source_target_pairs={{0,2},{1,3},{2,0},{3,1},{4,6},{5,7},{6,4},{7,5},{8,10},{9,11},{10,... | collective-permute-start | bytes 884744 | tf_op jit(solution)/shard_map/ppermute | solution.py:433
  99.7 11.1 %collective-permute-start.28 = (bf16[2,4,48,768]{3,2,1,0:T(8,128)(2,1)S(1)}, bf16[2,4,48,768]{3,2,1,0:T(8,128)(2,1)S(1)}, u32[]{:S(2)}, u32[]{:S(2)}) collective-permute-start(bf16[2,4,48,768]{3,2,1,0:T(8,128)(2,1)S(1)} %get-tuple-element.74.a0.refs_0_), channel_id=1, source_target_pairs={{0,4},{1,5},{2,6},{3,7},{4,0},{5,1},{6,2},{7,3},{8,12},{9,13},{10,... | collective-permute-start | bytes 1769480 | tf_op jit(solution)/shard_map/ppermute | solution.py:433
  101.2 20.2 %collective-permute-start.31 = (bf16[48,1536]{1,0:T(8,128)(2,1)S(1)}, bf16[48,1536]{1,0:T(8,128)(2,1)S(1)}, u32[]{:S(2)}, u32[]{:S(2)}) collective-permute-start(bf16[48,1536]{1,0:T(8,128)(2,1)S(1)} %get-tuple-element.73.refs_3_), channel_id=1, source_target_pairs={{0,8},{1,9},{2,10},{3,11},{4,12},{5,13},{6,14},{7,15},{8,0},{9,1},... | collective-permute-start | bytes 442376 | tf_op jit(solution)/shard_map/ppermute | solution.py:433
  102.7 18.8 %collective-permute-start.32 = (bf16[48,1536]{1,0:T(8,128)(2,1)S(1)}, bf16[48,1536]{1,0:T(8,128)(2,1)S(1)}, u32[]{:S(2)}, u32[]{:S(2)}) collective-permute-start(bf16[48,1536]{1,0:T(8,128)(2,1)S(1)} %get-tuple-element.77), channel_id=1, source_target_pairs={{0,16},{1,17},{2,18},{3,19},{4,20},{5,21},{6,22},{7,23},{8,24},{9,... | collective-permute-start | bytes 442376 | tf_op jit(solution)/shard_map/ppermute | solution.py:433
  105.6 15.9 %collective-permute-start.33 = (bf16[48,1536]{1,0:T(8,128)(2,1)S(1)}, bf16[48,1536]{1,0:T(8,128)(2,1)S(1)}, u32[]{:S(2)}, u32[]{:S(2)}) collective-permute-start(bf16[48,1536]{1,0:T(8,128)(2,1)S(1)} %get-tuple-element.78), channel_id=1, source_target_pairs={{0,24},{1,25},{2,26},{3,27},{4,28},{5,29},{6,30},{7,31},{8,16},{9,... | collective-permute-start | bytes 442376 | tf_op jit(solution)/shard_map/ppermute | solution.py:433
  (26 other events, 183.4 us)
